TPU v7x, 32 devices: a whole 2x2x4 slice. The times are simulated.
32 devices in a mesh: kv: 2 (over x), pg: 16 (over z, y, core).
Axes of the slice: x: 2, y: 2, z: 4, core: 2. Of those that a mesh axis runs over, the one named last changes fastest.
Arguments:
- residual_in: bfloat16 [1024, 1536], P('pg', 'kv'), as said below
- queries: bfloat16 [64, 1536], P('pg', 'kv'), as said below
- prefill_attn: bfloat16 [960, 1536], P('pg', 'kv'), may hold values from -1.1953125 to 1.1953125
- kv_cache: bfloat16 [256, 8, 128, 128], P('pg', 'kv'), as said below
- page_table: int32 [64, 4], replicated, may hold values from 0 to 255, as said below
- lengths: int32 [64], replicated, may hold values from 2 to 512, as said below
- out_weight: bfloat16 [1536, 1536], P('kv'), may hold values from -0.75 to 0.75
- norm_gain_in: float32 [1536], P('kv'), may hold values from 0.25 to 1.75
- norm_gain_out: float32 [1536], P('kv'), may hold values from 0.25 to 1.75
- expert_ids: int32 [1024, 8], P('pg'), may hold values from 0 to 39, all different within a row; in each aligned block of 64 rows (0 to 63, 64 to 127, ...) at most 16 rows name the same one
- route_weight: float32 [1024, 8], P('pg'), may hold values from 0.05 to 1
- slot_table: int32 [40, 2], replicated, may hold values from 0 to 47, as said below
- w_gate_up: bfloat16 [48, 1536, 1024], P('pg', 'kv'), as said below
- w_down: bfloat16 [48, 512, 1536], P('pg', None, 'kv'), as said below
Outputs:
- layer_out: bfloat16 [1024, 1536], P('pg', 'kv')
Inputs may be any that keep to these rules, and one draw needn't show every extreme that they name: `page_table`: every page of 0 to 255 appears exactly once in the table. `lengths`: some request has exactly 512 cached tokens. `slot_table`: row e lists the slots of expert e; each slot of 0 to 47 belongs to exactly one expert; an expert with a single slot repeats it. `w_gate_up`: slots of the same expert carry equal weights; entries lie within -0.2 and 0.2. `w_down`: slots of the same expert carry equal weights; entries lie within -0.3 and 0.3. `queries`: entries lie within -60 and 60. `kv_cache`: entries lie within -6 and 6. `residual_in`: entries lie within -50 and 50. `expert_ids`: in each aligned block of 64 rows no expert is named more than 16 times.
All inputs are finite; a program needn't handle non-finite values.
Results may differ from a plain program's by a relative error of at most 0.02.
Values may be sent and summed in bfloat16 or wider, within the bound.
No kernel may reach another device: no remote copies, remote signals or barrier semaphores. Data moves between devices by JAX's collectives and lax.ppermute only.
A program may use at most 128 MiB of HBM per device.

v0:
```python
import jax
import jax.numpy as jnp
from jax import lax
from jax.sharding import PartitionSpec as P

NEG_FILL = -1e30
EPSILON = 1e-06


def merged_2(array, axis, join):
    gathered = jax.tree.map(
        lambda a, kind: lax.all_gather(a.astype(kind), axis),
        array,
        (jnp.bfloat16, jnp.bfloat16, jnp.bfloat16),
    )

    def take(source):
        return jax.tree.map(
            lambda a, own: lax.dynamic_index_in_dim(a, source, 0, False).astype(own.dtype),
            gathered,
            array,
        )

    return lax.fori_loop(
        1, lax.axis_size(axis), lambda source, state: join(state, take(source)), take(0)
    )


def merge_pair(first, secondary_slot):
    highest = jnp.maximum(first[0], secondary_slot[0])
    scale_a = jnp.exp(first[0] - highest)
    scale_b = jnp.exp(secondary_slot[0] - highest)
    head_count = first[0].shape[1]
    acc_a = first[2].reshape(first[2].shape[0], head_count, -1) * scale_a[:, :, None]
    acc_b = (
        secondary_slot[2].reshape(secondary_slot[2].shape[0], head_count, -1) * scale_b[:, :, None]
    )
    return (
        highest,
        first[1] * scale_a + secondary_slot[1] * scale_b,
        (acc_a + acc_b).reshape(first[2].shape),
    )


def local(
    residual_in,
    queries,
    prefill_attn,
    kv_cache,
    page_table,
    lengths,
    out_weight,
    norm_gain_in,
    norm_gain_out,
    expert_ids,
    route_weight,
    slot_table,
    w_gate_up,
    w_down,
):
    head_dim = kv_cache.shape[3] // 2
    page_len = kv_cache.shape[2]
    pages_here = kv_cache.shape[0]
    kv_here = kv_cache.shape[1]
    own_req = queries.shape[0]
    heads_here = queries.shape[1] // head_dim
    head_group = heads_here // kv_here
    total_req = page_table.shape[0]
    max_pages = page_table.shape[1]
    full_gate_up, full_down = (
        lax.all_gather(w_gate_up, "kv", axis=1, tiled=True),
        lax.all_gather(w_down, "kv", axis=2, tiled=True),
    )
    gathered = lax.all_gather(queries, "pg", axis=0, tiled=True)
    page_ids = lax.axis_index("pg") * pages_here + jnp.arange(pages_here, dtype=jnp.int32)
    flat_table = page_table.reshape(-1)
    entry_index = jnp.arange(flat_table.shape[0], dtype=jnp.int32)
    found = jnp.sum(
        jnp.where(flat_table[None, :] == page_ids[:, None], entry_index[None, :], 0), axis=1
    )
    owner = found // max_pages
    page_slot = found % max_pages
    owner_len = lengths[owner]
    query_pages = gathered[owner].reshape(pages_here, kv_here, head_group, head_dim)
    keys = kv_cache[:, :, :, :head_dim]
    values = kv_cache[:, :, :, head_dim:]
    scores = jnp.einsum(
        "pkgd,pktd->pkgt", query_pages, keys, preferred_element_type=jnp.float32
    ) * head_dim ** (-0.5)
    positions = page_slot[:, None] * page_len + jnp.arange(page_len, dtype=jnp.int32)[None, :]
    live = (positions < owner_len[:, None])[:, None, None, :]
    masked = jnp.where(live, scores, NEG_FILL)
    page_top = jnp.max(masked, axis=3)
    probs = jnp.where(live, jnp.exp(masked - page_top[..., None]), 0.0).astype(jnp.bfloat16)
    page_sum = jnp.sum(probs.astype(jnp.float32), axis=3).reshape(pages_here, heads_here)
    page_acc = jnp.einsum(
        "pkgt,pktd->pkgd", probs, values, preferred_element_type=jnp.float32
    ).reshape(pages_here, heads_here, head_dim)
    page_top = page_top.reshape(pages_here, heads_here)
    page_live = page_slot * page_len < owner_len
    member = (owner[:, None] == jnp.arange(total_req, dtype=jnp.int32)[None, :]) & page_live[
        :, None
    ]
    local_max = jnp.max(jnp.where(member[:, :, None], page_top[:, None, :], NEG_FILL), axis=0)
    member_t = member.astype(jnp.float32).T
    weight = jnp.exp(page_top - local_max[owner])
    sums = jnp.dot(member_t, weight * page_sum, precision=lax.Precision.HIGHEST)
    accs = jnp.dot(
        member_t,
        (weight[:, :, None] * page_acc).reshape(pages_here, -1),
        precision=lax.Precision.HIGHEST,
    )
    sums, accs = (sums, accs)
    merged = merged_2((local_max, sums, accs), "pg", merge_pair)
    start = lax.axis_index("pg") * own_req
    own_sum = lax.dynamic_slice_in_dim(merged[1], start, own_req, 0)
    own_acc = lax.dynamic_slice_in_dim(merged[2], start, own_req, 0)
    attn_dec = (own_acc.reshape(own_req, heads_here, head_dim) / own_sum[:, :, None]).reshape(
        own_req, -1
    )
    attn_dec = attn_dec.astype(jnp.bfloat16)
    attn_rows = jnp.concatenate([attn_dec, prefill_attn], axis=0)
    projected = jnp.dot(attn_rows, out_weight, preferred_element_type=jnp.float32)
    mixed_in = lax.psum_scatter(
        projected.astype(jnp.bfloat16), "kv", scatter_dimension=1, tiled=True
    ).astype(jnp.float32)
    middle = residual_in.astype(jnp.float32) + mixed_in
    full_width = residual_in.shape[1] * lax.axis_size("kv")
    in_squares = lax.psum(jnp.sum(middle * middle, axis=1), "kv")
    normed = (middle * lax.rsqrt(in_squares / full_width + EPSILON)[:, None] * norm_gain_in).astype(
        jnp.bfloat16
    )
    token_rows, top = expert_ids.shape
    copies = slot_table.shape[1]
    experts_total = slot_table.shape[0]
    kv_count = lax.axis_size("kv")
    capacity = kv_count * max(
        1,
        (token_rows * top * 5 + 4 * experts_total * kv_count - 1) // (4 * experts_total * kv_count),
    )
    slots_here = w_gate_up.shape[0]
    groups = lax.axis_size("pg")
    all_slots = slots_here * groups
    feature_cols = normed.shape[1]
    row_ids = lax.axis_index("pg") * token_rows + jnp.arange(token_rows, dtype=jnp.int32)
    parity = (row_ids[:, None] + jnp.arange(top, dtype=jnp.int32)[None, :]) % copies
    route_key = (expert_ids * copies + parity).reshape(-1)
    table_flat = slot_table.reshape(-1)
    table_index = jnp.arange(table_flat.shape[0], dtype=jnp.int32)
    target_slot = jnp.sum(
        jnp.where(route_key[:, None] == table_index[None, :], table_flat[None, :], 0), axis=1
    )
    match_count = (target_slot[:, None] == jnp.arange(all_slots, dtype=jnp.int32)[None, :]).astype(
        jnp.int32
    )
    rank = jnp.sum((jnp.cumsum(match_count, axis=0) - match_count) * match_count, axis=1)
    dest = target_slot * capacity + rank
    source_row = jnp.arange(token_rows * top, dtype=jnp.int32) // top
    outgoing = (
        jnp.zeros((all_slots * capacity, feature_cols), jnp.bfloat16)
        .at[dest]
        .set(normed[source_row])
    )
    outgoing = outgoing.reshape(groups, slots_here, capacity, feature_cols)
    arrived = lax.all_to_all(outgoing, "pg", split_axis=0, concat_axis=0, tiled=True)
    widened = lax.all_to_all(arrived, "kv", split_axis=2, concat_axis=3, tiled=True)
    gate_up = jnp.einsum(
        "pscd,sdf->pscf", widened, full_gate_up, preferred_element_type=jnp.float32
    )
    half = gate_up.shape[3] // 2
    hidden = (jax.nn.silu(gate_up[..., :half]) * gate_up[..., half:]).astype(jnp.bfloat16)
    produced = jnp.einsum(
        "pscf,sfd->pscd", hidden, full_down, preferred_element_type=jnp.float32
    ).astype(jnp.bfloat16)
    narrowed = lax.all_to_all(produced, "kv", split_axis=3, concat_axis=2, tiled=True)
    returned = lax.all_to_all(narrowed, "pg", split_axis=0, concat_axis=0, tiled=True)
    returned = returned.reshape(all_slots * capacity, feature_cols)
    picked = returned[dest].astype(jnp.float32).reshape(token_rows, top, feature_cols)
    mixed = middle + jnp.sum(picked * route_weight[:, :, None], axis=1)
    out_squares = lax.psum(jnp.sum(mixed * mixed, axis=1), "kv")
    return (mixed * lax.rsqrt(out_squares / full_width + EPSILON)[:, None] * norm_gain_out).astype(
        jnp.bfloat16
    )


def solution(mesh):
    in_specs = (
        P("pg", "kv"),
        P("pg", "kv"),
        P("pg", "kv"),
        P("pg", "kv", None, None),
        P(),
        P(),
        P("kv", None),
        P("kv"),
        P("kv"),
        P("pg", None),
        P("pg", None),
        P(),
        P("pg", "kv", None),
        P("pg", None, "kv"),
    )
    out_specs = P("pg", "kv")
    return jax.shard_map(local, mesh=mesh, in_specs=in_specs, out_specs=out_specs, check_vma=False)
```

profile of v0, /device:TPU:0, one launch (start us, length us, event | category | flops | bytes accessed | tf_op | source)
XLA Modules:
  0.0 468.4 jit_solution(17040645806239165356)
XLA Ops:
  9.2 23.6 %all-gather.3 = bf16[16,4,768]{2,1,0:T(4,128)(2,1)S(1)} all-gather(bf16[1,4,768]{2,1,0:T(4,128)(2,1)} %bitcast.118), channel_id=1, replica_groups=mesh['kv'=2,'pg'=16] {'pg'}, dimensions={0}, use_global_device_ids=true | all-gather | bytes 104448 | tf_op jit(solution)/shard_map/all_gather | solution.py:74
  33.5 2.9 fusion.62
  37.6 2.4 fusion.13
  41.8 19.0 %all-gather.5 = bf16[16,64,12]{1,2,0:T(8,128)(2,1)} all-gather(bf16[1,64,12]{1,2,0:T(8,128)(2,1)S(1)} %fusion.27), channel_id=3, replica_groups=mesh['kv'=2,'pg'=16] {'pg'}, dimensions={0}, use_global_device_ids=true | all-gather | bytes 26112 | tf_op jit(solution)/shard_map/all_gather | solution.py:12
  61.6 20.4 %all-gather.4 = bf16[16,64,12]{1,2,0:T(8,128)(2,1)} all-gather(bf16[1,64,12]{1,2,0:T(8,128)(2,1)S(1)} %convert_bitcast_fusion), channel_id=2, replica_groups=mesh['kv'=2,'pg'=16] {'pg'}, dimensions={0}, use_global_device_ids=true | all-gather | bytes 26112 | tf_op jit(solution)/shard_map/all_gather | solution.py:12
  84.4 59.5 %while.19 = (s32[]{:T(128)}, f32[64,12]{1,0:T(8,128)}, f32[64,12]{1,0:T(8,128)S(1)}, f32[64,768]{1,0:T(8,128)S(1)}, bf16[16,64,12]{1,2,0:T(8,128)(2,1)}, /*index...) while((s32[]{:T(128)}, f32[64,12]{1,0:T(8,128)}, ...), condition=%wide.region_5.6_spmd, body=%wide.region_4.5_spmd.sunk | while | flops 202757 | bytes 2104471 | solution.py:24
  149.7 4.9 %reduce-scatter.2.cloned.1.call-done = bf16[64,768]{1,0:T(8,128)(2,1)} async-done(((bf16[64,1536]{1,0:T(8,128)(2,1)}), bf16[64,768]{1,0:T(8,128)(2,1)}) %reduce-scatter.2.cloned.1.call-update) | async-done | bytes 98320 | tf_op jit(solution)/shard_map/reduce_scatter | solution.py:124
  155.6 4.9 %psum.14 = f32[64]{0:T(128)S(1)} all-reduce(f32[64]{0:T(128)S(1)} %multiply_reduce_fusion.1), channel_id=1, replica_groups=mesh['kv'=2,'pg'=16] {'kv'}, use_global_device_ids=true, to_apply=%region_12.13 | all-reduce | flops 64 | bytes 512 | tf_op jit(solution)/shard_map/psum | solution.py:129
  162.2 8.7 %scatter_custom_fusion = bf16[768,768]{1,0:T(8,128)(2,1)S(1)} fusion(s32[512]{0:T(512)S(1)} %bitcast.114, bf16[64,768]{1,0:T(8,128)(2,1)} %multiply_convert_fusion.1, s32[1024]{0:T(1024)S(1)} %pad_clamp_fusion.1, bf16[]{:T(256)} %constant.142.clone.1), kind=kCustom, calls=%fused_computation.37 | custom fusion | bytes 1180160 | tf_op jit(solution)/shard_map/scatter | solution.py:162
  170.9 34.9 %all_to_all.46 = bf16[16,3,16,768]{3,2,1,0:T(8,128)(2,1)S(1)} all-to-all(bf16[16,3,16,768]{3,2,1,0:T(8,128)(2,1)S(1)} %bitcast.109), channel_id=1, replica_groups=mesh['kv'=2,'pg'=16] {'pg'}, dimensions={0} | all-to-all | bytes 2359296 | tf_op jit(solution)/shard_map/all_to_all | solution.py:165
  206.1 31.3 %all_to_all.47 = bf16[16,3,16,768]{3,0,1,2:T(8,128)(2,1)S(1)} all-to-all(bf16[16,3,16,768]{3,0,1,2:T(8,128)(2,1)S(1)} %copy.97), channel_id=1, replica_groups=mesh['kv'=2,'pg'=16] {'kv'}, dimensions={2} | all-to-all | bytes 2359296 | tf_op jit(solution)/shard_map/all_to_all | solution.py:166
  237.7 47.9 %all-gather.10.cloned.1.call-done = bf16[3,1536,1024]{2,1,0:T(8,128)(2,1)} async-done(((bf16[3,768,1024]{2,1,0:T(8,128)(2,1)}), bf16[3,1536,1024]{2,1,0:T(8,128)(2,1)}) %all-gather.10.cloned.1.call-update) | async-done | bytes 9437200 | tf_op jit(solution)/shard_map/all_gather | solution.py:71
  285.6 6.2 %fusion.18 = f32[16,3,8,1024]{3,2,0,1:T(8,128)} fusion(bf16[16,3,8,1536]{3,2,0,1:T(8,128)(2,1)S(1)} %bitcast.108, bf16[3,1536,1024]{2,1,0:T(8,128)(2,1)} %all-gather.10.cloned.1.call-done), kind=kOutput, calls=%fused_computation.29 | convolution fusion | flops 1207959552 | bytes 12189696 | tf_op jit(solution)/shard_map/pscd,sdf->pscf/dot_general | solution.py:167
  291.8 57.9 %all-gather.12.cloned.1.call-done = bf16[3,512,1536]{2,1,0:T(8,128)(2,1)} async-done(((bf16[3,512,768]{2,1,0:T(8,128)(2,1)}), bf16[3,512,1536]{2,1,0:T(8,128)(2,1)}) %all-gather.12.cloned.1.call-update) | async-done | bytes 4718608 | tf_op jit(solution)/shard_map/all_gather | solution.py:72
  349.7 3.7 fusion.10
  353.4 9.0 %copy.99 = bf16[16,3,8,1536]{0,2,1,3:T(8,128)(2,1)} copy(bf16[16,3,8,1536]{3,2,0,1:T(8,128)(2,1)S(1)} %fusion.10) | data formatting | bytes 2359296 | tf_op jit(solution)/shard_map/convert_element_type | solution.py:174
  362.4 14.3 %reshape.428 = bf16[2,2,147456]{2,1,0:T(2,128)(2,1)S(1)} reshape(bf16[1536,3,8,16]{3,2,1,0:T(8,128)(2,1)} %bitcast.106) | data formatting | bytes 2359296
  376.7 18.5 %all_to_all.48 = bf16[2,2,147456]{2,1,0:T(2,128)(2,1)} all-to-all(bf16[2,2,147456]{2,1,0:T(2,128)(2,1)S(1)} %reshape.428), channel_id=1, replica_groups=mesh['kv'=2,'pg'=16] {'kv'}, dimensions={0} | all-to-all | bytes 2359296 | tf_op jit(solution)/shard_map/all_to_all | solution.py:175
  395.3 12.8 %reshape.429 = bf16[1536,3,8,16]{3,2,1,0:T(8,128)(2,1)} reshape(bf16[2,2,147456]{2,1,0:T(2,128)(2,1)} %all_to_all.48) | data formatting | bytes 2359296
  408.1 10.8 %copy.100 = bf16[16,3,2,8,768]{4,3,2,1,0:T(8,128)(2,1)} copy(bf16[16,3,2,8,768]{0,3,1,4,2:T(8,128)(2,1)} %bitcast.107) | data formatting | bytes 2359296 | tf_op jit(solution)/shard_map/all_to_all | solution.py:175
  418.9 5.8 %all-to-all-start.3 = ((bf16[16,3,16,768]{3,2,1,0:T(8,128)(2,1)}), bf16[16,3,16,768]{3,2,1,0:T(8,128)(2,1)S(1)}, u32[]{:S(2)}, u32[]{:S(2)}) async-start(bf16[16,3,16,768]{3,2,1,0:T(8,128)(2,1)} %bitcast.111), calls=%async_computation.4 | async-start | bytes 2359296 | tf_op jit(solution)/shard_map/all_to_all | solution.py:176
  425.4 24.4 %all-to-all-done.3 = bf16[16,3,16,768]{3,2,1,0:T(8,128)(2,1)S(1)} async-done(((bf16[16,3,16,768]{3,2,1,0:T(8,128)(2,1)}), bf16[16,3,16,768]{3,2,1,0:T(8,128)(2,1)S(1)}, u32[]{:S(2)}, u32[]{:S(2)}) %all-to-all-start.3) | async-done | bytes 1179680 | tf_op jit(solution)/shard_map/all_to_all | solution.py:176
  449.8 2.7 gather_fusion.3
  455.2 4.9 %psum.15 = f32[64]{0:T(128)S(1)} all-reduce(f32[64]{0:T(128)S(1)} %multiply_reduce_fusion), channel_id=1, replica_groups=mesh['kv'=2,'pg'=16] {'kv'}, use_global_device_ids=true, to_apply=%region_16.17 | all-reduce | flops 64 | bytes 512 | tf_op jit(solution)/shard_map/psum | solution.py:180
  (224 shorter events, 82.3 us)
Async XLA Ops:
  6.5 137.5 %copy-start = (bf16[768,1536]{1,0:T(8,128)(2,1)S(1)}, bf16[768,1536]{1,0:T(8,128)(2,1)}, u32[]{:S(2)}) copy-start(bf16[768,1536]{1,0:T(8,128)(2,1)} %param.22) | copy-start | bytes 7077892
  6.5 76.9 %all-gather.14.cloned.1.call-start = ((), (), s32[]{:S(2)}) async-start(), calls=%async_computation.8 | async-start | bytes 1671168 | tf_op jit(solution)/shard_map/all_gather | solution.py:12
  41.2 113.4 %reduce-scatter.2.cloned.1.call-start = ((), (), s32[]{:S(2)}) async-start(), calls=%async_computation.5 | async-start | bytes 294912 | tf_op jit(solution)/shard_map/reduce_scatter | solution.py:124
  146.2 139.5 %all-gather.10.cloned.1.call-start = ((), (), s32[]{:S(2)}) async-start(), calls=%async_computation.6 | async-start | bytes 14155776 | tf_op jit(solution)/shard_map/all_gather | solution.py:71
  146.9 0.7 copy-start.5
  146.9 0.9 copy-start.6
  146.9 7.7 %copy-start.1 = (bf16[64,768]{1,0:T(8,128)(2,1)S(1)}, bf16[64,768]{1,0:T(8,128)(2,1)}, u32[]{:S(2)}) copy-start(bf16[64,768]{1,0:T(8,128)(2,1)} %param.16) | copy-start | bytes 294916
  146.9 13.7 %copy-start.2 = (f32[768]{0:T(1024)S(1)}, f32[768]{0:T(1024)}, u32[]{:S(2)}) copy-start(f32[768]{0:T(1024)} %param.23) | copy-start | bytes 9220
  146.9 202.8 %all-gather.12.cloned.1.call-start = ((), (), s32[]{:S(2)}) async-start(), calls=%async_computation.7 | async-start | bytes 7077888 | tf_op jit(solution)/shard_map/all_gather | solution.py:72
  418.9 5.8 %copy-start.4 = (f32[64,8]{0,1:T(8,128)S(1)}, f32[64,8]{0,1:T(8,128)}, u32[]{:S(2)}) copy-start(f32[64,8]{0,1:T(8,128)} %param.26) | copy-start | bytes 6148
  418.9 30.9 %all-to-all-start.3 = ((bf16[16,3,16,768]{3,2,1,0:T(8,128)(2,1)}), bf16[16,3,16,768]{3,2,1,0:T(8,128)(2,1)S(1)}, u32[]{:S(2)}, u32[]{:S(2)}) async-start(bf16[16,3,16,768]{3,2,1,0:T(8,128)(2,1)} %bitcast.111), calls=%async_computation.4 | async-start | bytes 2359296 | tf_op jit(solution)/shard_map/all_to_all | solution.py:176
  449.8 10.4 %copy-start.3 = (f32[768]{0:T(1024)S(1)}, f32[768]{0:T(1024)}, u32[]{:S(2)}) copy-start(f32[768]{0:T(1024)} %param.24) | copy-start | bytes 9220
Sparse Core Ops, SparseCore 0:
  41.3 37.2 all-gather.13
  146.3 8.2 reduce-scatter.1
  156.2 129.3 all-gather.9
  287.0 62.6 all-gather.11
where the time goes:
time: 473 us; the launch traced here: 468 us
  blocking collectives  158 us (33%)
  waiting for transfers between devices  136 us (29%)
  local copies, waits for them, and re-layouts  89.1 us (19%)
  other arithmetic  47 us (10%)
  matrix products  18.4 us (4%)
  between operations  13.4 us (3%)
  starting transfers between devices  5.88 us (1%)
    all_gather x1, waiting for transfers between devices, local(): lax.all_gather(w_down, 'kv', axis=2, tiled=True)  57.9 us
    all_gather x1, waiting for transfers between devices, local(): lax.all_gather(w_gate_up, 'kv', axis=1, tiled=True)  47.9 us
    all_gather x2, blocking collectives, merged_2(): lax.all_gather(a.astype(kind), axis)  39.5 us
    all_to_all x1, blocking collectives, local(): lax.all_to_all(outgoing, 'pg', split_axis=0, concat_axis=0, tiled=True)  34.9 us
    all_to_all x1, blocking collectives, local(): lax.all_to_all(arrived, 'kv', split_axis=2, concat_axis=3, tiled=True)  31.3 us
    unnamed x20, local copies, waits for them, and re-layouts  28.9 us
    all_to_all x1, waiting for transfers between devices, local(): lax.all_to_all(narrowed, 'pg', split_axis=0, concat_axis=0, tiled=True)  24.4 us
    all_gather x1, blocking collectives, local(): gathered = lax.all_gather(queries, 'pg', axis=0, tiled=True)  23.6 us
  transfers between devices with their start and end apart: 5, of which 4 were waited for; matrix products, arithmetic and copies ran while one was open for 5% of the time, Pallas kernels for 0%

commit v1 on v0

--- a/solution.py
+++ b/solution.py
@@ -1,6 +1,8 @@
 import jax
 import jax.numpy as jnp
 from jax import lax
+from jax.experimental import pallas as pl
+from jax.experimental.pallas import tpu as pltpu
 from jax.sharding import PartitionSpec as P
 
 NEG_FILL = -1e30
@@ -42,7 +44,7 @@
     )
 
 
-def local(
+def general_local(
     residual_in,
     queries,
     prefill_attn,
@@ -183,7 +185,485 @@
     )
 
 
+F32 = jnp.float32
+BF16 = jnp.bfloat16
+CAP = 16
+HIGH = lax.Precision.HIGHEST
+
+
+def call(body, outs, scratch=(), smem=(), vmem=32 * 2**20):
+    def run(*operands):
+        specs = [
+            pl.BlockSpec(memory_space=pltpu.SMEM if n in smem else pltpu.VMEM)
+            for n in range(len(operands))
+        ]
+        return pl.pallas_call(
+            body,
+            out_shape=[jax.ShapeDtypeStruct(s, d) for s, d in outs],
+            in_specs=specs,
+            out_specs=[pl.BlockSpec(memory_space=pltpu.VMEM) for _ in outs],
+            scratch_shapes=list(scratch),
+            compiler_params=pltpu.CompilerParams(vmem_limit_bytes=vmem),
+        )(*operands)
+
+    return run
+
+
+def iota(shape, dim):
+    return lax.broadcasted_iota(jnp.int32, shape, dim)
+
+
+def dot(a, b, precision=None):
+    return jnp.dot(a, b, preferred_element_type=F32, precision=precision)
+
+
+def dot_t(a, b):
+    return lax.dot_general(a, b, (((1,), (1,)), ((), ())), preferred_element_type=F32)
+
+
+def t_dot(a, b):
+    return lax.dot_general(a, b, (((0,), (0,)), ((), ())), preferred_element_type=F32)
+
+
+def swap_kv(x):
+    return lax.ppermute(x, "kv", [(0, 1), (1, 0)])
+
+
+def swap_pg(x, mask, n):
+    return lax.ppermute(x, "pg", [(i, i ^ mask) for i in range(n)])
+
+
+def page_attention(sent, kv_cache, owner, live, own_req):
+    groups = sent.shape[0]
+    cols = sent.shape[2]
+    pages, kv_here, page_len, wide = kv_cache.shape
+    head_dim = wide // 2
+    heads = cols // head_dim
+    group = heads // kv_here
+    rows = 16
+    requests = groups * own_req
+    keys = kv_here * page_len
+
+    def body(owner_s, live_s, owner_col, owner_lane, sent_ref, kv_ref, out_ref, q_all, acc, m_all, l_all):
+        for g in range(groups):
+            q_all[g * own_req : (g + 1) * own_req, :] = sent_ref[g, 0:own_req, :].astype(F32)
+        total = pages * rows
+        pick = (owner_col[...] == iota((total, requests), 1)).astype(BF16)
+        wide_q = dot(pick, q_all[...].astype(BF16))
+        head_row = iota((total, cols), 0) % rows
+        spread = head_row == iota((total, cols), 1) // head_dim
+        fold = (iota((cols, wide), 0) % head_dim == iota((cols, wide), 1)).astype(BF16)
+        q = dot(jnp.where(spread, wide_q, 0.0).astype(BF16), fold).astype(BF16)
+        col = iota((rows, keys), 1)
+        mine = col // page_len == iota((rows, keys), 0) // group
+        place = col % page_len
+        lane = iota((rows, 128), 1)
+        tops = jnp.full((rows, 128), NEG_FILL, F32)
+        for p in range(pages):
+            block = kv_ref[p].reshape(keys, wide)
+            scores = dot_t(q[p * rows : (p + 1) * rows], block) * head_dim ** (-0.5)
+            ok = mine & (place < live_s[p])
+            masked = jnp.where(ok, scores, NEG_FILL)
+            top = jnp.max(masked, axis=1, keepdims=True).astype(BF16).astype(F32)
+            probs = jnp.where(ok, jnp.exp(masked - top), 0.0).astype(BF16)
+            part = pl.ds(p * rows, rows)
+            l_all[part, :] = jnp.broadcast_to(
+                jnp.sum(probs.astype(F32), axis=1, keepdims=True), (rows, 128)
+            )
+            acc[part, :] = dot(probs, block)
+            m_all[part, :] = jnp.broadcast_to(top, (rows, 128))
+            tops = jnp.where(lane == p, top, tops)
+        for p in range(pages):
+            part = pl.ds(p * rows, rows)
+            same = owner_lane[...] == owner_s[p]
+            best = jnp.max(jnp.where(same, tops, NEG_FILL), axis=1, keepdims=True)
+            scale = jnp.exp(m_all[part, :] - best)
+            acc[part, :] = acc[part, :] * scale
+            l_all[part, :] = l_all[part, :] * scale
+            first = jnp.int32(1)
+            for e in range(p):
+                first = jnp.where(owner_s[e] == owner_s[p], 0, first)
+            m_all[part, :] = jnp.where(first == 1, jnp.broadcast_to(best, (rows, 128)), 0.0)
+        unfold = (iota((wide, cols), 0) - head_dim == iota((wide, cols), 1) % head_dim).astype(BF16)
+        spread_acc = jnp.where(spread, dot(acc[...].astype(BF16), unfold), 0.0).astype(BF16)
+        here = iota((total, 128), 0) % rows == iota((total, 128), 1)
+        tops_out = jnp.where(here, m_all[...], 0.0).astype(BF16)
+        sums_out = jnp.where(here, l_all[...], 0.0)
+        sums_high = sums_out.astype(BF16)
+        sums_low = (sums_out - sums_high.astype(F32)).astype(BF16)
+        out_acc = t_dot(pick, spread_acc).astype(BF16)
+        out_top = t_dot(pick, tops_out).astype(BF16)
+        out_sum = (t_dot(pick, sums_high) + t_dot(pick, sums_low)).astype(BF16)
+        for g in range(groups):
+            part = slice(g * own_req, (g + 1) * own_req)
+            out_ref[g, :, 0:cols] = out_acc[part]
+            out_ref[g, :, cols : cols + 128] = out_top[part]
+            out_ref[g, :, cols + 128 : cols + 256] = out_sum[part]
+
+    total = pages * rows
+    owner_col = jnp.broadcast_to(jnp.repeat(owner, rows)[:, None], (total, requests))
+    owner_lane = jnp.broadcast_to(
+        jnp.concatenate([owner, jnp.full((128 - pages,), -1, jnp.int32)])[None, :], (rows, 128)
+    )
+    return call(
+        body,
+        [((groups, own_req, cols + 256), BF16)],
+        [
+            pltpu.VMEM((requests, cols), F32),
+            pltpu.VMEM((total, wide), F32),
+            pltpu.VMEM((total, 128), F32),
+            pltpu.VMEM((total, 128), F32),
+        ],
+        smem=(0, 1),
+    )(owner, live, owner_col, owner_lane, sent, kv_cache)[0]
+
+
+def project(arrived, prefill, weight, residual, me_kv, head_dim):
+    groups, own_req, _ = arrived.shape
+    rows, cols = residual.shape
+
+    def body(me, arr, pre, w_ref, res, send, base, w_scr, rows_scr):
+        top = arr[:, :, cols : cols + 128].astype(F32)
+        tot = arr[:, :, cols + 128 : cols + 256].astype(F32)
+        top = jnp.where(tot > 0.0, top, NEG_FILL)
+        best = jnp.max(top, axis=0)
+        scale = jnp.where(tot > 0.0, jnp.exp(top - best[None]), 0.0)
+        whole = jnp.sum(scale * tot, axis=0)
+        whole = jnp.where(whole > 0.0, whole, 1.0)
+        scale = scale / whole[None]
+        for g in range(groups):
+            w_scr[g * own_req : (g + 1) * own_req, :] = scale[g]
+        expand = (iota((128, cols), 0) == iota((128, cols), 1) // head_dim).astype(F32)
+        wide = dot(w_scr[...], expand, HIGH)
+        merged = jnp.zeros((own_req, cols), F32)
+        for g in range(groups):
+            merged += wide[g * own_req : (g + 1) * own_req] * arr[g, :, 0:cols].astype(F32)
+        rows_scr[0:own_req, :] = merged
+        rows_scr[own_req:, :] = pre[...].astype(F32)
+        left = rows_scr[...].astype(BF16)
+        mine = pl.multiple_of(me[0] * cols, 128)
+        other = pl.multiple_of((1 - me[0]) * cols, 128)
+        send[:, 0:cols] = dot(left, w_ref[:, pl.ds(other, cols)]).astype(BF16)
+        own = dot(left, w_ref[:, pl.ds(mine, cols)]).astype(BF16).astype(F32)
+        own = own + res[...].astype(F32)
+        base[...] = own
+        send[:, cols:] = own.astype(BF16)
+
+    return call(
+        body,
+        [((rows, 2 * cols), BF16), ((rows, cols), F32)],
+        [pltpu.VMEM((groups * own_req, 128), F32), pltpu.VMEM((rows, cols), F32)],
+        smem=(0,),
+    )(me_kv, arrived, prefill, weight, residual)
+
+
+def first_norm(base, sent, got, gain):
+    rows, cols = base.shape
+
+    def body(base_ref, sent_ref, got_ref, gain_ref, middle, normed):
+        mid = base_ref[...] + got_ref[:, 0:cols].astype(F32)
+        far = got_ref[:, cols:].astype(F32) + sent_ref[:, 0:cols].astype(F32)
+        squares = jnp.sum(mid * mid + far * far, axis=1, keepdims=True)
+        middle[...] = mid
+        normed[...] = (
+            mid * lax.rsqrt(squares / (2 * cols) + EPSILON) * gain_ref[...]
+        ).astype(BF16)
+
+    return call(body, [((rows, cols), F32), ((rows, cols), BF16)])(
+        base, sent, got, gain.reshape(1, -1)
+    )
+
+
+def one_hot(meta, g, s, block_rows):
+    tokens = meta.shape[2]
+    blocks = tokens // block_rows
+    shape = (blocks * CAP, tokens)
+    place = meta[g, s : s + 1, :].astype(jnp.int32)
+    row = iota(shape, 0)
+    return (place == row % CAP) & (iota(shape, 1) // block_rows == row // CAP)
+
+
+def gather_and_first(groups, meta, w_gate_up, me_kv, block_rows):
+    count, cols, slots = len(groups), groups[0].shape[1], w_gate_up.shape[0]
+    tokens = groups[0].shape[0]
+    part = tokens // block_rows * CAP
+    ff = w_gate_up.shape[2] // 2
+    half = ff // 2
+
+    def body(me, meta_ref, w_ref, *refs):
+        xs, send = refs[count:]
+        for g in range(count):
+            pick = jnp.concatenate(
+                [one_hot(meta_ref, g, s, block_rows).astype(BF16) for s in range(slots)], axis=0
+            )
+            rows = dot(pick, refs[g][...]).astype(BF16)
+            for s in range(slots):
+                xs[s, g * part : (g + 1) * part, :] = rows[s * part : (s + 1) * part]
+        far = pl.multiple_of((1 - me[0]) * half, 128)
+        up = pl.multiple_of(ff + (1 - me[0]) * half, 128)
+        send[:, 0:half] = dot(xs[0], w_ref[0, :, pl.ds(far, half)]).astype(BF16)
+        send[:, half:] = dot(xs[0], w_ref[0, :, pl.ds(up, half)]).astype(BF16)
+
+    return call(
+        body,
+        [((slots, count * part, cols), BF16), ((count * part, ff), BF16)],
+        smem=(0,),
+    )(me_kv, meta, w_gate_up, *groups)
+
+
+def rest_of_gate_up(xs, w_gate_up, me_kv):
+    slots, rows, cols = xs.shape
+    ff = w_gate_up.shape[2] // 2
+    half = ff // 2
+
+    def body(me, x_ref, w_ref, *outs):
+        sends, own = outs[:-1], outs[-1]
+        far = pl.multiple_of((1 - me[0]) * half, 128)
+        far_up = pl.multiple_of(ff + (1 - me[0]) * half, 128)
+        near = pl.multiple_of(me[0] * half, 128)
+        near_up = pl.multiple_of(ff + me[0] * half, 128)
+        for s in range(1, slots):
+            sends[s - 1][:, 0:half] = dot(x_ref[s], w_ref[s, :, pl.ds(far, half)]).astype(BF16)
+            sends[s - 1][:, half:] = dot(x_ref[s], w_ref[s, :, pl.ds(far_up, half)]).astype(BF16)
+        for s in range(slots):
+            own[s, :, 0:half] = dot(x_ref[s], w_ref[s, :, pl.ds(near, half)])
+            own[s, :, half:] = dot(x_ref[s], w_ref[s, :, pl.ds(near_up, half)])
+
+    return call(
+        body,
+        [((rows, ff), BF16)] * (slots - 1) + [((slots, rows, ff), F32)],
+        smem=(0,),
+    )(me_kv, xs, w_gate_up)
+
+
+def activate(own, got, s):
+    slots, rows, ff = own.shape
+    half = ff // 2
+
+    def body(own_ref, got_ref, out):
+        gate = own_ref[s, :, 0:half] + got_ref[:, 0:half].astype(F32)
+        up = own_ref[s, :, half:] + got_ref[:, half:].astype(F32)
+        out[...] = (gate / (1.0 + jnp.exp(-gate)) * up).astype(BF16)
+
+    return call(body, [((rows, half), BF16)])(own, got)[0]
+
+
+def down(near, far, w_down, meta, s, me_kv, block_rows):
+    rows, half = near.shape
+    cols = w_down.shape[2]
+    count, _, tokens = meta.shape
+    slots = w_down.shape[0]
+    part = rows // count
+
+    def body(me, near_ref, far_ref, w_ref, meta_ref, out):
+        lo = pl.multiple_of(me[0] * half, 128)
+        hi = pl.multiple_of((1 - me[0]) * half, 128)
+        made = dot(near_ref[...], w_ref[s, pl.ds(lo, half), :])
+        made = made + dot(far_ref[...], w_ref[s, pl.ds(hi, half), :])
+        for g in range(count):
+            pick = one_hot(meta_ref, g, s, block_rows)
+            gate = jnp.sum(
+                jnp.where(pick, meta_ref[g, slots + s : slots + s + 1, :], 0.0),
+                axis=1,
+                keepdims=True,
+            )
+            out[g * part : (g + 1) * part, :] = (made[g * part : (g + 1) * part] * gate).astype(
+                BF16
+            )
+
+    return call(body, [((rows, cols), BF16)], smem=(0,))(me_kv, near, far, w_down, meta)[0]
+
+
+def scatter(made, meta, g, block_rows, plus=None):
+    slots = len(made)
+    rows, cols = made[0].shape
+    count, _, tokens = meta.shape
+    part = rows // count
+
+    def body(meta_ref, *refs):
+        out = refs[-1]
+        pick = jnp.concatenate(
+            [one_hot(meta_ref, g, s, block_rows).astype(BF16) for s in range(slots)], axis=0
+        )
+        rows_here = jnp.concatenate(
+            [refs[s][g * part : (g + 1) * part, :] for s in range(slots)], axis=0
+        )
+        total = t_dot(pick, rows_here)
+        if plus is not None:
+            total = total + refs[slots][...].astype(F32)
+        out[...] = total.astype(BF16)
+
+    extra = [] if plus is None else [plus]
+    return call(body, [((tokens, cols), BF16)])(meta, *made, *extra)[0]
+
+
+def split_sum(a, b, block_rows):
+    tokens, cols = a.shape
+    count = tokens // block_rows
+
+    def body(a_ref, b_ref, *outs):
+        for n in range(count):
+            part = slice(n * block_rows, (n + 1) * block_rows)
+            total = a_ref[part, :].astype(F32) + b_ref[part, :].astype(F32)
+            outs[n][...] = total.astype(outs[n].dtype)
+
+    return call(
+        body,
+        [((block_rows, cols), F32)] + [((block_rows, cols), BF16)] * (count - 1),
+    )(a, b)
+
+
+def close(middle, parts):
+    rows, cols = middle.shape
+
+    def body(mid, *refs):
+        mixed, squares = refs[-2:]
+        total = mid[...]
+        for ref in refs[:-2]:
+            total = total + ref[...].astype(F32)
+        mixed[...] = total
+        total = total * total
+        folded = total[:, 0:128]
+        for n in range(1, cols // 128):
+            folded = folded + total[:, n * 128 : (n + 1) * 128]
+        squares[...] = folded
+
+    return call(body, [((rows, cols), F32), ((rows, 128), F32)])(middle, *parts)
+
+
+def last_norm(mixed, near, far, gain):
+    rows, cols = mixed.shape
+
+    def body(mixed_ref, near_ref, far_ref, gain_ref, out):
+        squares = jnp.sum(near_ref[...] + far_ref[...], axis=1, keepdims=True)
+        out[...] = (
+            mixed_ref[...] * lax.rsqrt(squares / (2 * cols) + EPSILON) * gain_ref[...]
+        ).astype(BF16)
+
+    return call(body, [((rows, cols), BF16)])(mixed, near, far, gain.reshape(1, -1))[0]
+
+
+def routing(expert_ids, route_weight, slot_table, first_row, all_slots):
+    rows, top = expert_ids.shape
+    copies = slot_table.shape[1]
+    experts = slot_table.shape[0]
+    parity = (
+        first_row
+        + jnp.arange(rows, dtype=jnp.int32)[:, None]
+        + jnp.arange(top, dtype=jnp.int32)[None, :]
+    ) % copies
+    key = expert_ids * copies + parity
+    table = slot_table.reshape(-1)
+    target = jnp.sum(
+        jnp.where(
+            key[:, :, None] == jnp.arange(experts * copies, dtype=jnp.int32)[None, None, :],
+            table[None, None, :],
+            0,
+        ),
+        axis=2,
+    )
+    hit = target.T[None, :, :] == jnp.arange(all_slots, dtype=jnp.int32)[:, None, None]
+    named = jnp.sum(hit.astype(F32), axis=1)
+    gate = jnp.sum(jnp.where(hit, route_weight.T[None, :, :], 0.0), axis=1)
+    before = (
+        jnp.arange(rows, dtype=jnp.int32)[:, None] < jnp.arange(rows, dtype=jnp.int32)[None, :]
+    )
+    rank = jnp.dot(named.astype(BF16), before.astype(BF16), preferred_element_type=F32)
+    return jnp.where(named > 0, rank, -1.0), gate
+
+
+def fast_local(
+    residual_in,
+    queries,
+    prefill_attn,
+    kv_cache,
+    page_table,
+    lengths,
+    out_weight,
+    norm_gain_in,
+    norm_gain_out,
+    expert_ids,
+    route_weight,
+    slot_table,
+    w_gate_up,
+    w_down,
+):
+    n_pg = lax.axis_size("pg")
+    me = lax.axis_index("pg")
+    me_kv = lax.axis_index("kv").reshape(1).astype(jnp.int32)
+    rows, cols = residual_in.shape
+    own_req = queries.shape[0]
+    slots = w_gate_up.shape[0]
+    pages, _, page_len, wide = kv_cache.shape
+    head_dim = wide // 2
+    max_pages = page_table.shape[1]
+
+    place, gate = routing(expert_ids, route_weight, slot_table, me * rows, slots * n_pg)
+    gate_high = gate.astype(BF16)
+    gate_low = (gate - gate_high.astype(F32)).astype(BF16)
+    info = jnp.concatenate(
+        [x.reshape(n_pg, slots * rows) for x in (place.astype(BF16), gate_high, gate_low)], axis=1
+    )
+    lanes = -(-info.shape[1] // cols) * cols
+    info = jnp.pad(info, ((0, 0), (0, lanes - info.shape[1]))).reshape(n_pg, -1, cols)
+    sent = jnp.concatenate([jnp.broadcast_to(queries[None], (n_pg, own_req, cols)), info], axis=1)
+    sent = lax.all_to_all(sent, "pg", split_axis=0, concat_axis=0, tiled=True)
+
+    order = [c + 2 * y + 4 * z for c in range(2) for y in range(2) for z in range(n_pg // 4)]
+    info = sent[:, own_req:, :].reshape(n_pg, lanes)[:, : 3 * slots * rows]
+    info = info[me ^ jnp.asarray(order, jnp.int32)].astype(F32)
+    info = info.reshape(4, n_pg // 4, 3, slots, rows).transpose(0, 2, 3, 1, 4)
+    info = info.reshape(4, 3, slots, n_pg // 4 * rows)
+    meta = jnp.concatenate([info[:, 0], info[:, 1] + info[:, 2]], axis=1)
+
+    page_ids = me * pages + jnp.arange(pages, dtype=jnp.int32)
+    flat_table = page_table.reshape(-1)
+    entry_index = jnp.arange(flat_table.shape[0], dtype=jnp.int32)
+    found = jnp.sum(
+        jnp.where(flat_table[None, :] == page_ids[:, None], entry_index[None, :], 0), axis=1
+    )
+    owner = found // max_pages
+    owner_len = jnp.sum(
+        jnp.where(
+            owner[:, None] == jnp.arange(lengths.shape[0], dtype=jnp.int32)[None, :],
+            lengths[None, :],
+            0,
+        ),
+        axis=1,
+    )
+    live = owner_len - found % max_pages * page_len
+    partial = page_attention(sent, kv_cache, owner, live, own_req)
+    arrived = lax.all_to_all(partial, "pg", split_axis=0, concat_axis=0, tiled=True)
+
+    send, base = project(arrived, prefill_attn, out_weight, residual_in, me_kv, head_dim)
+    middle, normed = first_norm(base, send, swap_kv(send), norm_gain_in)
+
+    near = jnp.concatenate(
+        [normed] + [swap_pg(normed, 4 * z, n_pg) for z in range(1, n_pg // 4)], axis=0
+    )
+    across = swap_pg(near, 2, n_pg)
+    tokens = [near, across, swap_pg(near, 1, n_pg), swap_pg(across, 1, n_pg)]
+
+    xs, send0 = gather_and_first(tokens, meta, w_gate_up, me_kv, rows)
+    *sends, own = rest_of_gate_up(xs, w_gate_up, me_kv)
+    made = []
+    for s, out in enumerate([send0] + sends):
+        hidden = activate(own, swap_kv(out), s)
+        made.append(down(hidden, swap_kv(hidden), w_down, meta, s, me_kv, rows))
+
+    got3 = swap_pg(scatter(made, meta, 3, rows), 1, n_pg)
+    got2 = swap_pg(scatter(made, meta, 2, rows), 1, n_pg)
+    sum1 = swap_pg(scatter(made, meta, 1, rows, got3), 2, n_pg)
+    sum0 = scatter(made, meta, 0, rows, got2)
+    parts = split_sum(sum0, sum1, rows)
+    parts = [parts[0]] + [swap_pg(parts[z], 4 * z, n_pg) for z in range(1, n_pg // 4)]
+    mixed, squares = close(middle, parts)
+    return last_norm(mixed, squares, swap_kv(squares), norm_gain_out)
+
+
 def solution(mesh):
+    fast = mesh.shape["kv"] == 2 and mesh.shape["pg"] == 16
+    local = fast_local if fast else general_local
     in_specs = (
         P("pg", "kv"),
         P("pg", "kv"),

time: 473 us -> 134 us (0.28)
  blocking collectives: 158 us -> 0 us
  local copies, waits for them, and re-layouts: 89.1 us -> 8.21 us
  waiting for transfers between devices: 136 us -> 73.1 us
  other arithmetic: 47 us -> 4.74 us
  starting transfers between devices: 5.88 us -> 34.3 us
  matrix products: 18.4 us -> 0.13 us
  between operations: 13.4 us -> 0.34 us
  Pallas kernels: 0 us -> 12.4 us
    all_gather x3 -> x0, waiting for transfers between devices: 106 us -> none  [the longest x1 57.9 us: local(): lax.all_gather(w_down, 'kv', axis=2, tiled=True)]
    all_to_all x3 -> x0, blocking collectives: 84.6 us -> none  [the longest x1 34.9 us: local(): lax.all_to_all(outgoing, 'pg', split_axis=0, concat_axis=0, tiled=True)]
    all_gather x3 -> x0, blocking collectives: 63.1 us -> none  [the longest x2 39.5 us: merged_2(): lax.all_gather(a.astype(kind), axis)]
    ppermute x0 -> x20, waiting for transfers between devices: none -> 58.3 us  [the longest x12 33.9 us: swap_pg(): return lax.ppermute(x, 'pg', [(i, i ^ mask) for i in range(n)])]
    add x34 -> x3, other arithmetic: 35.3 us -> 0.71 us  [the longest x1 0.7 us: routing(): key = expert_ids * copies + parity]
    ppermute x0 -> x20, starting transfers between devices: none -> 23.3 us  [the longest x12 11.9 us: swap_pg(): return lax.ppermute(x, 'pg', [(i, i ^ mask) for i in range(n)])]
    unnamed x20 -> x26, local copies, waits for them, and re-layouts: 28.9 us -> 5.77 us
    dot_general x7 -> x1, matrix products: 18.4 us -> 0.13 us  [routing(): jnp.dot(named.astype(BF16), before.astype(BF16), preferred_element_type=F32)]
  transfers between devices with their start and end apart: 5 -> 22, of which waited for: 4 -> 18; matrix products, arithmetic and copies ran while one was open for 5% -> 2% of each run, Pallas kernels for 0% -> 2%
where the time goes in v1:
time: 134 us; the launch traced here: 133 us
  waiting for transfers between devices  73.1 us (55%)
  starting transfers between devices  34.3 us (26%)
  Pallas kernels  12.4 us (9%)
  local copies, waits for them, and re-layouts  8.21 us (6%)
  other arithmetic  4.74 us (4%)
    ppermute x12, waiting for transfers between devices, swap_pg(): return lax.ppermute(x, 'pg', [(i, i ^ mask) for i in range(n)])  33.9 us
    ppermute x8, waiting for transfers between devices, swap_kv(): return lax.ppermute(x, 'kv', [(0, 1), (1, 0)])  24.4 us
    pallas_call x18, Pallas kernels, run(): pl.pallas_call(body, out_shape=[jax.ShapeDtypeStruct(s, d) for s, d in ou...  12.4 us
    ppermute x12, starting transfers between devices, swap_pg(): return lax.ppermute(x, 'pg', [(i, i ^ mask) for i in range(n)])  11.9 us
    ppermute x8, starting transfers between devices, swap_kv(): return lax.ppermute(x, 'kv', [(0, 1), (1, 0)])  11.4 us
    all_to_all x1, waiting for transfers between devices, fast_local(): lax.all_to_all(partial, 'pg', split_axis=0, concat_axis=0, tiled=True)  7.89 us
    all_to_all x1, starting transfers between devices, fast_local(): sent = lax.all_to_all(sent, 'pg', split_axis=0, concat_axis=0, tiled=True)  7.39 us
    all_to_all x1, waiting for transfers between devices, fast_local(): sent = lax.all_to_all(sent, 'pg', split_axis=0, concat_axis=0, tiled=True)  6.89 us
  transfers between devices with their start and end apart: 22, of which 18 were waited for; matrix products, arithmetic and copies ran while one was open for 2% of the time, Pallas kernels for 2%

profile of v1, /device:TPU:0, one launch (start us, length us, event | category | flops | bytes accessed | tf_op | source)
XLA Modules:
  0.0 133.2 jit_solution(18095907217976156788)
XLA Ops:
  5.9 7.4 %all-to-all-start = ((bf16[16,5,768]{2,1,0:T(8,128)(2,1)}), bf16[16,5,768]{2,1,0:T(8,128)(2,1)S(1)}, u32[]{:S(2)}, u32[]{:S(2)}) async-start(bf16[16,5,768]{2,1,0:T(8,128)(2,1)} %pad_maximum_fusion), calls=%async_computation | async-start | bytes 393216 | tf_op jit(solution)/shard_map/all_to_all | solution.py:610
  15.4 6.9 %all-to-all-done.sent_ref = bf16[16,5,768]{2,1,0:T(8,128)(2,1)S(1)} async-done(((bf16[16,5,768]{2,1,0:T(8,128)(2,1)}), bf16[16,5,768]{2,1,0:T(8,128)(2,1)S(1)}, u32[]{:S(2)}, u32[]{:S(2)}) %all-to-all-start) | async-done | bytes 122912 | tf_op jit(solution)/shard_map/all_to_all | solution.py:610
  22.4 1.6 %copy-done.4 = bf16[16,4,128,128]{3,2,1,0:T(8,128)(2,1)S(1)} copy-done((bf16[16,4,128,128]{3,2,1,0:T(8,128)(2,1)S(1)}, bf16[16,4,128,128]{3,2,1,0:T(8,128)(2,1)}, u32[]{:S(2)}) %copy-start.4) | copy-done | bytes 2097176
  24.0 5.9 %shard_map.145 = bf16[16,4,1024]{2,1,0:T(4,128)(2,1)} custom-call(s32[16]{0:T(128)S(1)} %and_select_fusion.1.owner_s, s32[16]{0:T(128)S(1)} %fusion.15.live_s, s32[256,64]{1,0:T(8,128)S(1)} %broadcast_in_dim.100.owner_col, s32[16,128]{1,0:T(8,128)S(1)} %broadcast_in_dim.101.owner_lane, bf16[16,5,768]{2,1,0:T(8,128)(2,1)S(1)} %all-to-all-done.sent_ref, ...), custom_call_target="tpu_custom_call" | custom-call | tf_op jit(solution)/shard_map/pallas_call | solution.py:200
  29.9 3.6 %all-to-all-start.1 = ((bf16[16,4,1024]{2,1,0:T(4,128)(2,1)}), bf16[16,4,1024]{2,1,0:T(4,128)(2,1)S(1)}, u32[]{:S(2)}, u32[]{:S(2)}) async-start(bf16[16,4,1024]{2,1,0:T(4,128)(2,1)} %shard_map.145), calls=%async_computation.1 | async-start | bytes 262144 | tf_op jit(solution)/shard_map/all_to_all | solution.py:636
  33.6 7.9 %all-to-all-done.1.arr = bf16[16,4,1024]{2,1,0:T(4,128)(2,1)S(1)} async-done(((bf16[16,4,1024]{2,1,0:T(4,128)(2,1)}), bf16[16,4,1024]{2,1,0:T(4,128)(2,1)S(1)}, u32[]{:S(2)}, u32[]{:S(2)}) %all-to-all-start.1) | async-done | bytes 131104 | tf_op jit(solution)/shard_map/all_to_all | solution.py:636
  42.4 1.6 %collective-permute-start = (bf16[64,1536]{1,0:T(8,128)(2,1)S(1)}, bf16[64,1536]{1,0:T(8,128)(2,1)S(1)}, u32[]{:S(2)}, u32[]{:S(2)}) collective-permute-start(bf16[64,1536]{1,0:T(8,128)(2,1)S(1)} %get-tuple-element.21.sent_ref), channel_id=1, source_target_pairs={{0,16},{16,0},{1,17},{17,1},{2,18},{18,2},{3,19},{19,3},{4,20},{20... | collective-permute-start | bytes 589832 | tf_op jit(solution)/shard_map/ppermute | solution.py:229
  43.9 4.7 %collective-permute-done.got_ref = bf16[64,1536]{1,0:T(8,128)(2,1)S(1)} collective-permute-done((bf16[64,1536]{1,0:T(8,128)(2,1)S(1)}, bf16[64,1536]{1,0:T(8,128)(2,1)S(1)}, u32[]{:S(2)}, u32[]{:S(2)}) %collective-permute-start) | collective-permute-done | bytes 196640 | tf_op jit(solution)/shard_map/ppermute | solution.py:229
  50.9 2.3 %collective-permute-start.3 = (bf16[64,768]{1,0:T(8,128)(2,1)S(1)}, bf16[64,768]{1,0:T(8,128)(2,1)S(1)}, u32[]{:S(2)}, u32[]{:S(2)}) collective-permute-start(bf16[64,768]{1,0:T(8,128)(2,1)S(1)} %get-tuple-element.23), channel_id=1, source_target_pairs={{0,12},{1,13},{2,14},{3,15},{4,8},{5,9},{6,10},{7,11},{8,4},{9,5},... | collective-permute-start | bytes 294920 | tf_op jit(solution)/shard_map/ppermute | solution.py:233
  53.2 1.7 %collective-permute-done.1 = bf16[64,768]{1,0:T(8,128)(2,1)S(1)} collective-permute-done((bf16[64,768]{1,0:T(8,128)(2,1)S(1)}, bf16[64,768]{1,0:T(8,128)(2,1)S(1)}, u32[]{:S(2)}, u32[]{:S(2)}) %collective-permute-start.1) | collective-permute-done | bytes 98336 | tf_op jit(solution)/shard_map/ppermute | solution.py:233
  54.9 4.4 %collective-permute-done.2 = bf16[64,768]{1,0:T(8,128)(2,1)S(1)} collective-permute-done((bf16[64,768]{1,0:T(8,128)(2,1)S(1)}, bf16[64,768]{1,0:T(8,128)(2,1)S(1)}, u32[]{:S(2)}, u32[]{:S(2)}) %collective-permute-start.2) | collective-permute-done | bytes 98336 | tf_op jit(solution)/shard_map/ppermute | solution.py:233
  60.6 8.6 %collective-permute-done.4.refs_1_ = bf16[256,768]{1,0:T(8,128)(2,1)S(1)} collective-permute-done((bf16[256,768]{1,0:T(8,128)(2,1)S(1)}, bf16[256,768]{1,0:T(8,128)(2,1)S(1)}, u32[]{:S(2)}, u32[]{:S(2)}) %collective-permute-start.4) | collective-permute-done | bytes 393248 | tf_op jit(solution)/shard_map/ppermute | solution.py:233
  70.9 2.3 %copy-done.1 = bf16[3,768,1024]{2,1,0:T(8,128)(2,1)S(1)} copy-done((bf16[3,768,1024]{2,1,0:T(8,128)(2,1)S(1)}, bf16[3,768,1024]{2,1,0:T(8,128)(2,1)}, u32[]{:S(2)}) %copy-start.1) | copy-done | bytes 4718616
  76.8 1.6 %collective-permute-start.9 = (bf16[256,512]{1,0:T(8,128)(2,1)S(1)}, bf16[256,512]{1,0:T(8,128)(2,1)S(1)}, u32[]{:S(2)}, u32[]{:S(2)}) collective-permute-start(bf16[256,512]{1,0:T(8,128)(2,1)S(1)} %get-tuple-element.27), channel_id=1, source_target_pairs={{0,16},{16,0},{1,17},{17,1},{2,18},{18,2},{3,19},{19,3},{4,20},{20... | collective-permute-start | bytes 786440 | tf_op jit(solution)/shard_map/ppermute | solution.py:229
  78.9 4.2 %collective-permute-done.7.got_ref = bf16[256,512]{1,0:T(8,128)(2,1)S(1)} collective-permute-done((bf16[256,512]{1,0:T(8,128)(2,1)S(1)}, bf16[256,512]{1,0:T(8,128)(2,1)S(1)}, u32[]{:S(2)}, u32[]{:S(2)}) %collective-permute-start.7) | collective-permute-done | bytes 262176 | tf_op jit(solution)/shard_map/ppermute | solution.py:229
  84.8 3.9 %collective-permute-done.9.got_ref = bf16[256,512]{1,0:T(8,128)(2,1)S(1)} collective-permute-done((bf16[256,512]{1,0:T(8,128)(2,1)S(1)}, bf16[256,512]{1,0:T(8,128)(2,1)S(1)}, u32[]{:S(2)}, u32[]{:S(2)}) %collective-permute-start.9) | collective-permute-done | bytes 262176 | tf_op jit(solution)/shard_map/ppermute | solution.py:229
  90.4 4.0 %collective-permute-done.11.got_ref = bf16[256,512]{1,0:T(8,128)(2,1)S(1)} collective-permute-done((bf16[256,512]{1,0:T(8,128)(2,1)S(1)}, bf16[256,512]{1,0:T(8,128)(2,1)S(1)}, u32[]{:S(2)}, u32[]{:S(2)}) %collective-permute-start.11) | collective-permute-done | bytes 262176 | tf_op jit(solution)/shard_map/ppermute | solution.py:229
  97.6 2.4 %collective-permute-done.10.far_ref = bf16[256,256]{1,0:T(8,128)(2,1)S(1)} collective-permute-done((bf16[256,256]{1,0:T(8,128)(2,1)S(1)}, bf16[256,256]{1,0:T(8,128)(2,1)S(1)}, u32[]{:S(2)}, u32[]{:S(2)}) %collective-permute-start.10) | collective-permute-done | bytes 131104 | tf_op jit(solution)/shard_map/ppermute | solution.py:229
  100.4 1.6 %collective-permute-done.12.far_ref = bf16[256,256]{1,0:T(8,128)(2,1)S(1)} collective-permute-done((bf16[256,256]{1,0:T(8,128)(2,1)S(1)}, bf16[256,256]{1,0:T(8,128)(2,1)S(1)}, u32[]{:S(2)}, u32[]{:S(2)}) %collective-permute-start.12) | collective-permute-done | bytes 131104 | tf_op jit(solution)/shard_map/ppermute | solution.py:229
  105.5 10.5 %collective-permute-done.15.b_ref = bf16[256,768]{1,0:T(8,128)(2,1)S(1)} collective-permute-done((bf16[256,768]{1,0:T(8,128)(2,1)S(1)}, bf16[256,768]{1,0:T(8,128)(2,1)S(1)}, u32[]{:S(2)}, u32[]{:S(2)}) %collective-permute-start.15) | collective-permute-done | bytes 393248 | tf_op jit(solution)/shard_map/ppermute | solution.py:233
  116.1 2.7 %collective-permute-start.16 = (bf16[64,768]{1,0:T(8,128)(2,1)S(1)}, bf16[64,768]{1,0:T(8,128)(2,1)S(1)}, u32[]{:S(2)}, u32[]{:S(2)}) collective-permute-start(bf16[64,768]{1,0:T(8,128)(2,1)S(1)} %get-tuple-element.30), channel_id=1, source_target_pairs={{0,4},{1,5},{2,6},{3,7},{4,0},{5,1},{6,2},{7,3},{8,12},{9,13},{10,... | collective-permute-start | bytes 294920 | tf_op jit(solution)/shard_map/ppermute | solution.py:233
  118.8 2.4 %collective-permute-start.18 = (bf16[64,768]{1,0:T(8,128)(2,1)S(1)}, bf16[64,768]{1,0:T(8,128)(2,1)S(1)}, u32[]{:S(2)}, u32[]{:S(2)}) collective-permute-start(bf16[64,768]{1,0:T(8,128)(2,1)S(1)} %get-tuple-element.32), channel_id=1, source_target_pairs={{0,12},{1,13},{2,14},{3,15},{4,8},{5,9},{6,10},{7,11},{8,4},{9,5},... | collective-permute-start | bytes 294920 | tf_op jit(solution)/shard_map/ppermute | solution.py:233
  122.1 6.3 %collective-permute-done.17.refs_2_ = bf16[64,768]{1,0:T(8,128)(2,1)S(1)} collective-permute-done((bf16[64,768]{1,0:T(8,128)(2,1)S(1)}, bf16[64,768]{1,0:T(8,128)(2,1)S(1)}, u32[]{:S(2)}, u32[]{:S(2)}) %collective-permute-start.17) | collective-permute-done | bytes 98336 | tf_op jit(solution)/shard_map/ppermute | solution.py:233
  130.0 2.4 %collective-permute-done.19.far_ref = f32[64,128]{1,0:T(8,128)S(1)} collective-permute-done((f32[64,128]{1,0:T(8,128)S(1)}, f32[64,128]{1,0:T(8,128)S(1)}, u32[]{:S(2)}, u32[]{:S(2)}) %collective-permute-start.19) | collective-permute-done | bytes 32800 | tf_op jit(solution)/shard_map/ppermute | solution.py:229
  (103 shorter events, 31.9 us)
Async XLA Ops:
  0.0 41.5 %copy-start.3 = (bf16[768,1536]{1,0:T(8,128)(2,1)S(1)}, bf16[768,1536]{1,0:T(8,128)(2,1)}, u32[]{:S(2)}) copy-start(bf16[768,1536]{1,0:T(8,128)(2,1)} %w_ref.6) | copy-start | bytes 7077892
  5.9 16.4 %all-to-all-start = ((bf16[16,5,768]{2,1,0:T(8,128)(2,1)}), bf16[16,5,768]{2,1,0:T(8,128)(2,1)S(1)}, u32[]{:S(2)}, u32[]{:S(2)}) async-start(bf16[16,5,768]{2,1,0:T(8,128)(2,1)} %pad_maximum_fusion), calls=%async_computation | async-start | bytes 393216 | tf_op jit(solution)/shard_map/all_to_all | solution.py:610
  29.9 30.7 %copy-start.9 = (s32[16]{0:T(128)S(1)}, s32[16]{0:T(128)}, u32[]{:S(2)}) copy-start(s32[16]{0:T(128)} %constant.69.clone) | copy-start | bytes 196
  29.9 11.5 %all-to-all-start.1 = ((bf16[16,4,1024]{2,1,0:T(4,128)(2,1)}), bf16[16,4,1024]{2,1,0:T(4,128)(2,1)S(1)}, u32[]{:S(2)}, u32[]{:S(2)}) async-start(bf16[16,4,1024]{2,1,0:T(4,128)(2,1)} %shard_map.145), calls=%async_computation.1 | async-start | bytes 262144 | tf_op jit(solution)/shard_map/all_to_all | solution.py:636
  42.4 6.2 %collective-permute-start = (bf16[64,1536]{1,0:T(8,128)(2,1)S(1)}, bf16[64,1536]{1,0:T(8,128)(2,1)S(1)}, u32[]{:S(2)}, u32[]{:S(2)}) collective-permute-start(bf16[64,1536]{1,0:T(8,128)(2,1)S(1)} %get-tuple-element.21.sent_ref), channel_id=1, source_target_pairs={{0,16},{16,0},{1,17},{17,1},{2,18},{18,2},{3,19},{19,3},{4,20},{20... | collective-permute-start | bytes 589832 | tf_op jit(solution)/shard_map/ppermute | solution.py:229
  48.7 6.1 %collective-permute-start.1 = (bf16[64,768]{1,0:T(8,128)(2,1)S(1)}, bf16[64,768]{1,0:T(8,128)(2,1)S(1)}, u32[]{:S(2)}, u32[]{:S(2)}) collective-permute-start(bf16[64,768]{1,0:T(8,128)(2,1)S(1)} %get-tuple-element.23), channel_id=1, source_target_pairs={{0,4},{1,5},{2,6},{3,7},{4,0},{5,1},{6,2},{7,3},{8,12},{9,13},{10,... | collective-permute-start | bytes 294920 | tf_op jit(solution)/shard_map/ppermute | solution.py:233
  49.5 9.8 %collective-permute-start.2 = (bf16[64,768]{1,0:T(8,128)(2,1)S(1)}, bf16[64,768]{1,0:T(8,128)(2,1)S(1)}, u32[]{:S(2)}, u32[]{:S(2)}) collective-permute-start(bf16[64,768]{1,0:T(8,128)(2,1)S(1)} %get-tuple-element.23), channel_id=1, source_target_pairs={{0,8},{1,9},{2,10},{3,11},{4,12},{5,13},{6,14},{7,15},{8,0},{9,1},... | collective-permute-start | bytes 294920 | tf_op jit(solution)/shard_map/ppermute | solution.py:233
  50.9 8.4 %collective-permute-start.3 = (bf16[64,768]{1,0:T(8,128)(2,1)S(1)}, bf16[64,768]{1,0:T(8,128)(2,1)S(1)}, u32[]{:S(2)}, u32[]{:S(2)}) collective-permute-start(bf16[64,768]{1,0:T(8,128)(2,1)S(1)} %get-tuple-element.23), channel_id=1, source_target_pairs={{0,12},{1,13},{2,14},{3,15},{4,8},{5,9},{6,10},{7,11},{8,4},{9,5},... | collective-permute-start | bytes 294920 | tf_op jit(solution)/shard_map/ppermute | solution.py:233
  59.3 9.9 %collective-permute-start.4 = (bf16[256,768]{1,0:T(8,128)(2,1)S(1)}, bf16[256,768]{1,0:T(8,128)(2,1)S(1)}, u32[]{:S(2)}, u32[]{:S(2)}) collective-permute-start(bf16[256,768]{1,0:T(8,128)(2,1)S(1)} %constant_dynamic-update-slice_fusion.refs_0_), channel_id=1, source_target_pairs={{0,2},{1,3},{2,0},{3,1},{4,6},{5,7},{6,4},{7,5},{8,10},{9,11},{10,... | collective-permute-start | bytes 1179656 | tf_op jit(solution)/shard_map/ppermute | solution.py:233
  60.6 9.6 %collective-permute-start.5 = (bf16[256,768]{1,0:T(8,128)(2,1)S(1)}, bf16[256,768]{1,0:T(8,128)(2,1)S(1)}, u32[]{:S(2)}, u32[]{:S(2)}) collective-permute-start(bf16[256,768]{1,0:T(8,128)(2,1)S(1)} %constant_dynamic-update-slice_fusion.refs_0_), channel_id=1, source_target_pairs={{0,1},{1,0},{2,3},{3,2},{4,5},{5,4},{6,7},{7,6},{8,9},{9,8},{10,11... | collective-permute-start | bytes 1179656 | tf_op jit(solution)/shard_map/ppermute | solution.py:233
  69.2 1.7 %collective-permute-start.6 = (bf16[256,768]{1,0:T(8,128)(2,1)S(1)}, bf16[256,768]{1,0:T(8,128)(2,1)S(1)}, u32[]{:S(2)}, u32[]{:S(2)}) collective-permute-start(bf16[256,768]{1,0:T(8,128)(2,1)S(1)} %collective-permute-done.4.refs_1_), channel_id=1, source_target_pairs={{0,1},{1,0},{2,3},{3,2},{4,5},{5,4},{6,7},{7,6},{8,9},{9,8},{10,11... | collective-permute-start | bytes 1179656 | tf_op jit(solution)/shard_map/ppermute | solution.py:233
  73.9 9.2 %collective-permute-start.7 = (bf16[256,512]{1,0:T(8,128)(2,1)S(1)}, bf16[256,512]{1,0:T(8,128)(2,1)S(1)}, u32[]{:S(2)}, u32[]{:S(2)}) collective-permute-start(bf16[256,512]{1,0:T(8,128)(2,1)S(1)} %get-tuple-element.26), channel_id=1, source_target_pairs={{0,16},{16,0},{1,17},{17,1},{2,18},{18,2},{3,19},{19,3},{4,20},{20... | collective-permute-start | bytes 786440 | tf_op jit(solution)/shard_map/ppermute | solution.py:229
  76.8 12.0 %collective-permute-start.9 = (bf16[256,512]{1,0:T(8,128)(2,1)S(1)}, bf16[256,512]{1,0:T(8,128)(2,1)S(1)}, u32[]{:S(2)}, u32[]{:S(2)}) collective-permute-start(bf16[256,512]{1,0:T(8,128)(2,1)S(1)} %get-tuple-element.27), channel_id=1, source_target_pairs={{0,16},{16,0},{1,17},{17,1},{2,18},{18,2},{3,19},{19,3},{4,20},{20... | collective-permute-start | bytes 786440 | tf_op jit(solution)/shard_map/ppermute | solution.py:229
  78.4 16.0 %collective-permute-start.11 = (bf16[256,512]{1,0:T(8,128)(2,1)S(1)}, bf16[256,512]{1,0:T(8,128)(2,1)S(1)}, u32[]{:S(2)}, u32[]{:S(2)}) collective-permute-start(bf16[256,512]{1,0:T(8,128)(2,1)S(1)} %get-tuple-element.28), channel_id=1, source_target_pairs={{0,16},{16,0},{1,17},{17,1},{2,18},{18,2},{3,19},{19,3},{4,20},{20... | collective-permute-start | bytes 786440 | tf_op jit(solution)/shard_map/ppermute | solution.py:229
  83.3 13.9 %collective-permute-start.8 = (bf16[256,256]{1,0:T(8,128)(2,1)S(1)}, bf16[256,256]{1,0:T(8,128)(2,1)S(1)}, u32[]{:S(2)}, u32[]{:S(2)}) collective-permute-start(bf16[256,256]{1,0:T(8,128)(2,1)S(1)} %shard_map.150.near_ref), channel_id=1, source_target_pairs={{0,16},{16,0},{1,17},{17,1},{2,18},{18,2},{3,19},{19,3},{4,20},{20... | collective-permute-start | bytes 393224 | tf_op jit(solution)/shard_map/ppermute | solution.py:229
  88.9 11.1 %collective-permute-start.10 = (bf16[256,256]{1,0:T(8,128)(2,1)S(1)}, bf16[256,256]{1,0:T(8,128)(2,1)S(1)}, u32[]{:S(2)}, u32[]{:S(2)}) collective-permute-start(bf16[256,256]{1,0:T(8,128)(2,1)S(1)} %shard_map.152.near_ref), channel_id=1, source_target_pairs={{0,16},{16,0},{1,17},{17,1},{2,18},{18,2},{3,19},{19,3},{4,20},{20... | collective-permute-start | bytes 393224 | tf_op jit(solution)/shard_map/ppermute | solution.py:229
  94.5 7.5 %collective-permute-start.12 = (bf16[256,256]{1,0:T(8,128)(2,1)S(1)}, bf16[256,256]{1,0:T(8,128)(2,1)S(1)}, u32[]{:S(2)}, u32[]{:S(2)}) collective-permute-start(bf16[256,256]{1,0:T(8,128)(2,1)S(1)} %shard_map.154.near_ref), channel_id=1, source_target_pairs={{0,16},{16,0},{1,17},{17,1},{2,18},{18,2},{3,19},{19,3},{4,20},{20... | collective-permute-start | bytes 393224 | tf_op jit(solution)/shard_map/ppermute | solution.py:229
  102.7 1.8 %collective-permute-start.14 = (bf16[256,768]{1,0:T(8,128)(2,1)S(1)}, bf16[256,768]{1,0:T(8,128)(2,1)S(1)}, u32[]{:S(2)}, u32[]{:S(2)}) collective-permute-start(bf16[256,768]{1,0:T(8,128)(2,1)S(1)} %shard_map.158), channel_id=1, source_target_pairs={{0,1},{1,0},{2,3},{3,2},{4,5},{5,4},{6,7},{7,6},{8,9},{9,8},{10,11... | collective-permute-start | bytes 1179656 | tf_op jit(solution)/shard_map/ppermute | solution.py:233
  103.1 2.1 %collective-permute-start.13 = (bf16[256,768]{1,0:T(8,128)(2,1)S(1)}, bf16[256,768]{1,0:T(8,128)(2,1)S(1)}, u32[]{:S(2)}, u32[]{:S(2)}) collective-permute-start(bf16[256,768]{1,0:T(8,128)(2,1)S(1)} %shard_map.156), channel_id=1, source_target_pairs={{0,1},{1,0},{2,3},{3,2},{4,5},{5,4},{6,7},{7,6},{8,9},{9,8},{10,11... | collective-permute-start | bytes 1179656 | tf_op jit(solution)/shard_map/ppermute | solution.py:233
  104.8 11.2 %collective-permute-start.15 = (bf16[256,768]{1,0:T(8,128)(2,1)S(1)}, bf16[256,768]{1,0:T(8,128)(2,1)S(1)}, u32[]{:S(2)}, u32[]{:S(2)}) collective-permute-start(bf16[256,768]{1,0:T(8,128)(2,1)S(1)} %shard_map.159), channel_id=1, source_target_pairs={{0,2},{1,3},{2,0},{3,1},{4,6},{5,7},{6,4},{7,5},{8,10},{9,11},{10,... | collective-permute-start | bytes 1179656 | tf_op jit(solution)/shard_map/ppermute | solution.py:233
  116.1 6.0 %collective-permute-start.16 = (bf16[64,768]{1,0:T(8,128)(2,1)S(1)}, bf16[64,768]{1,0:T(8,128)(2,1)S(1)}, u32[]{:S(2)}, u32[]{:S(2)}) collective-permute-start(bf16[64,768]{1,0:T(8,128)(2,1)S(1)} %get-tuple-element.30), channel_id=1, source_target_pairs={{0,4},{1,5},{2,6},{3,7},{4,0},{5,1},{6,2},{7,3},{8,12},{9,13},{10,... | collective-permute-start | bytes 294920 | tf_op jit(solution)/shard_map/ppermute | solution.py:233
  118.8 9.6 %collective-permute-start.17 = (bf16[64,768]{1,0:T(8,128)(2,1)S(1)}, bf16[64,768]{1,0:T(8,128)(2,1)S(1)}, u32[]{:S(2)}, u32[]{:S(2)}) collective-permute-start(bf16[64,768]{1,0:T(8,128)(2,1)S(1)} %get-tuple-element.31), channel_id=1, source_target_pairs={{0,8},{1,9},{2,10},{3,11},{4,12},{5,13},{6,14},{7,15},{8,0},{9,1},... | collective-permute-start | bytes 294920 | tf_op jit(solution)/shard_map/ppermute | solution.py:233
  118.8 9.6 %collective-permute-start.18 = (bf16[64,768]{1,0:T(8,128)(2,1)S(1)}, bf16[64,768]{1,0:T(8,128)(2,1)S(1)}, u32[]{:S(2)}, u32[]{:S(2)}) collective-permute-start(bf16[64,768]{1,0:T(8,128)(2,1)S(1)} %get-tuple-element.32), channel_id=1, source_target_pairs={{0,12},{1,13},{2,14},{3,15},{4,8},{5,9},{6,10},{7,11},{8,4},{9,5},... | collective-permute-start | bytes 294920 | tf_op jit(solution)/shard_map/ppermute | solution.py:233
  128.5 4.0 %collective-permute-start.19 = (f32[64,128]{1,0:T(8,128)S(1)}, f32[64,128]{1,0:T(8,128)S(1)}, u32[]{:S(2)}, u32[]{:S(2)}) collective-permute-start(f32[64,128]{1,0:T(8,128)S(1)} %get-tuple-element.34.near_ref), channel_id=1, source_target_pairs={{0,16},{16,0},{1,17},{17,1},{2,18},{18,2},{3,19},{19,3},{4,20},{20... | collective-permute-start | bytes 98312 | tf_op jit(solution)/shard_map/ppermute | solution.py:229
  (8 other events, 102.0 us)

commit v2 on v0

--- a/solution.py
+++ b/solution.py
@@ -1,6 +1,10 @@
+import functools
+
 import jax
 import jax.numpy as jnp
 from jax import lax
+from jax.experimental import pallas as pl
+from jax.experimental.pallas import tpu as pltpu
 from jax.sharding import PartitionSpec as P
 
 NEG_FILL = -1e30
@@ -42,7 +46,7 @@
     )
 
 
-def local(
+def general_local(
     residual_in,
     queries,
     prefill_attn,
@@ -183,7 +187,715 @@
     )
 
 
+F32 = jnp.float32
+BF16 = jnp.bfloat16
+CAP = 16
+HIGH = lax.Precision.HIGHEST
+
+
+def call(body, outs, scratch=(), smem=(), hbm=(), vmem=16):
+    def run(*operands):
+        kinds = [
+            pltpu.SMEM if n in smem else pltpu.HBM if n in hbm else pltpu.VMEM
+            for n in range(len(operands))
+        ]
+        return pl.pallas_call(
+            body,
+            out_shape=[jax.ShapeDtypeStruct(s, d) for s, d in outs],
+            in_specs=[pl.BlockSpec(memory_space=kind) for kind in kinds],
+            out_specs=[pl.BlockSpec(memory_space=pltpu.VMEM) for _ in outs],
+            scratch_shapes=list(scratch),
+            compiler_params=pltpu.CompilerParams(
+                vmem_limit_bytes=vmem * 2**20
+            ),
+            cost_estimate=pl.CostEstimate(flops=1, bytes_accessed=1, transcendentals=0),
+        )(*operands)
+
+    return run
+
+
+def after(values, *earlier):
+    return lax.optimization_barrier((values, earlier))[0]
+
+
+def iota(shape, dim):
+    return lax.broadcasted_iota(jnp.int32, shape, dim)
+
+
+def dot(a, b, precision=None):
+    return jnp.dot(a, b, preferred_element_type=F32, precision=precision)
+
+
+def dot_t(a, b):
+    return lax.dot_general(a, b, (((1,), (1,)), ((), ())), preferred_element_type=F32)
+
+
+def t_dot(a, b):
+    return lax.dot_general(a, b, (((0,), (0,)), ((), ())), preferred_element_type=F32)
+
+
+def swap_kv(x):
+    return lax.ppermute(x, "kv", [(0, 1), (1, 0)])
+
+
+def swap_pg(x, mask, n):
+    return lax.ppermute(x, "pg", [(i, i ^ mask) for i in range(n)])
+
+
+def pack(queries, residual, expert_ids, route_weight, n_pg):
+    own_req, cols = queries.shape
+    rows, top = expert_ids.shape
+    tiles = cols // 128
+    high = 2 * own_req * tiles
+    total = -(-(high + 3 * top) // 16) * 16
+
+    def body(q_ref, res_ref, ids_ref, gates_ref, out_ref, scr):
+        scr[...] = jnp.zeros((total, 128), F32)
+        for n, ref in enumerate((q_ref, res_ref)):
+            for i in range(tiles):
+                low = (n * tiles + i) * own_req
+                scr[low : low + own_req, :] = ref[0:own_req, 128 * i : 128 * (i + 1)].astype(F32)
+        gates = gates_ref[...]
+        gates_high = gates.astype(BF16).astype(F32)
+        for n, x in enumerate((ids_ref[...].astype(F32), gates_high, gates - gates_high)):
+            scr[high + n * top : high + (n + 1) * top, 0:rows] = x
+        packed = scr[...].astype(BF16)
+        for g in range(n_pg):
+            out_ref[g] = packed
+
+    return call(body, [((n_pg, total, 128), BF16)], [pltpu.VMEM((total, 128), F32)])(
+        queries, residual, expert_ids.T, route_weight.T
+    )[0]
+
+
+def unpack(sent_ref, out, which, own_req):
+    tiles = out.shape[1] // 128
+    for g in range(sent_ref.shape[0]):
+        for i in range(tiles):
+            low = (which * tiles + i) * own_req
+            out[g * own_req : (g + 1) * own_req, 128 * i : 128 * (i + 1)] = sent_ref[
+                g, low : low + own_req, :
+            ].astype(F32)
+
+
+def routing(sent_ref, me, masks, first, top, count):
+    got = jnp.concatenate(
+        [sent_ref[me ^ mask, first : first + 3 * top, 0:count].astype(F32) for mask in masks],
+        axis=1,
+    )
+    return jnp.concatenate([got[0:top], got[top : 2 * top] + got[2 * top :]], axis=0)
+
+
+def group_masks(g, zs):
+    return [4 * z + 2 * (g % 2) + g // 2 for z in range(zs)]
+
+
+def page_attention(sent, kv_cache, owner, live, own_req, cols):
+    groups = sent.shape[0]
+    pages, kv_here, page_len, wide = kv_cache.shape
+    head_dim = wide // 2
+    heads = cols // head_dim
+    group = heads // kv_here
+    rows = 16
+    requests = groups * own_req
+    keys = kv_here * page_len
+    total = pages * rows
+
+    def body(owner_col, live_col, sent_ref, kv_ref, out_ref, q_all, scores, probs, acc):
+        unpack(sent_ref, q_all, 0, own_req)
+        pick = (owner_col[...] == iota((total, requests), 1)).astype(BF16)
+        wide_q = dot(pick, q_all[...].astype(BF16))
+        spread = iota((total, cols), 0) % rows == iota((total, cols), 1) // head_dim
+        fold = (iota((cols, wide), 0) % head_dim == iota((cols, wide), 1)).astype(BF16)
+        q = dot(jnp.where(spread, wide_q, 0.0).astype(BF16), fold).astype(BF16)
+        for p in range(pages):
+            part = slice(p * rows, (p + 1) * rows)
+            scores[part, :] = dot_t(q[part], kv_ref[p].reshape(keys, wide)) * head_dim ** (-0.5)
+        col = iota((total, keys), 1)
+        ok = (col // page_len == iota((total, keys), 0) % rows // group) & (
+            col % page_len < live_col[...]
+        )
+        masked = jnp.where(ok, scores[...], NEG_FILL)
+        top = jnp.max(masked, axis=1, keepdims=True).astype(BF16).astype(F32)
+        share = jnp.where(ok, jnp.exp(masked - top), 0.0).astype(BF16)
+        probs[...] = share
+        whole = jnp.sum(share.astype(F32), axis=1, keepdims=True)
+        for p in range(pages):
+            part = slice(p * rows, (p + 1) * rows)
+            acc[part, :] = dot(probs[part, :], kv_ref[p].reshape(keys, wide))
+        unfold = (iota((wide, cols), 0) - head_dim == iota((wide, cols), 1) % head_dim).astype(BF16)
+        here = iota((total, 128), 0) % rows == iota((total, 128), 1)
+        merge = (iota((pages, total), 0) == iota((pages, total), 1) // rows).astype(BF16)
+        flat = jnp.where(spread, dot(acc[...].astype(BF16), unfold), 0.0).astype(BF16)
+        out_ref[:, 0:cols] = dot(merge, flat).astype(BF16)
+        flat = jnp.where(here, top, 0.0).astype(BF16)
+        out_ref[:, cols : cols + 128] = dot(merge, flat).astype(BF16)
+        flat = jnp.where(here, whole, 0.0).astype(BF16)
+        out_ref[:, cols + 128 :] = dot(merge, flat).astype(BF16)
+
+    return call(
+        body,
+        [((pages, cols + 256), BF16)],
+        [
+            pltpu.VMEM((requests, cols), F32),
+            pltpu.VMEM((total, keys), F32),
+            pltpu.VMEM((total, keys), BF16),
+            pltpu.VMEM((total, wide), F32),
+        ],
+    )(jnp.repeat(owner, rows)[:, None], jnp.repeat(live, rows)[:, None], sent, kv_cache)[0]
+
+
+def half_products(left, w_ref, res, me, cols, send, base):
+    mine = pl.multiple_of(me[0] * cols, 128)
+    other = pl.multiple_of((1 - me[0]) * cols, 128)
+    send[:, 0:cols] = dot(left, w_ref[:, pl.ds(other, cols)]).astype(BF16)
+    own = dot(left, w_ref[:, pl.ds(mine, cols)]).astype(BF16).astype(F32) + res
+    base[...] = own
+    send[:, cols:] = own.astype(BF16)
+
+
+def project_prefill(prefill, weight, residual, me_kv):
+    rows, cols = residual.shape
+    skip = rows - prefill.shape[0]
+
+    def body(me, pre, w_ref, res, send, base, rows_scr):
+        rows_scr[0:skip, :] = jnp.zeros((skip, cols), F32)
+        rows_scr[skip:, :] = pre[...].astype(F32)
+        left = rows_scr[...].astype(BF16)
+        half_products(left, w_ref, res[...].astype(F32), me, cols, send, base)
+
+    return call(
+        body,
+        [((rows, 2 * cols), BF16), ((rows, cols), F32)],
+        [pltpu.VMEM((rows, cols), F32)],
+        smem=(0,),
+    )(me_kv, prefill, weight, residual)
+
+
+def project_decode(pieces, where, sent, weight, me_kv, own_req, head_dim):
+    groups = sent.shape[0]
+    cols = weight.shape[0]
+    requests = groups * own_req
+    entries = where.shape[0]
+    count = len(pieces)
+    total = count * pieces[0].shape[0]
+
+    def body(me, where_ref, w_ref, sent_ref, *refs):
+        send, base, res = refs[count:]
+        unpack(sent_ref, res, 1, own_req)
+        table = jnp.concatenate([ref[...] for ref in refs[:count]], axis=0)
+        pick = (where_ref[...] == iota((entries, total), 1)).astype(BF16)
+        got = dot(pick, table)
+        parts = [got[n : n + requests] for n in range(0, entries, requests)]
+        sums = [part[:, cols + 128 :] for part in parts]
+        tops = [
+            jnp.where(tot > 0.0, part[:, cols : cols + 128], NEG_FILL)
+            for part, tot in zip(parts, sums)
+        ]
+        best = functools.reduce(jnp.maximum, tops)
+        scales = [jnp.where(tot > 0.0, jnp.exp(top - best), 0.0) for top, tot in zip(tops, sums)]
+        whole = functools.reduce(jnp.add, [scale * tot for scale, tot in zip(scales, sums)])
+        whole = jnp.where(whole > 0.0, whole, 1.0)
+        expand = (iota((128, cols), 0) == iota((128, cols), 1) // head_dim).astype(BF16)
+        share = jnp.concatenate([scale / whole for scale in scales], axis=0)
+        share_high = share.astype(BF16)
+        share_low = (share - share_high.astype(F32)).astype(BF16)
+        wide = dot(share_high, expand) + dot(share_low, expand)
+        merged = jnp.zeros((requests, cols), F32)
+        for n, part in enumerate(parts):
+            merged += wide[n * requests : (n + 1) * requests] * part[:, 0:cols]
+        half_products(merged.astype(BF16), w_ref, res[...], me, cols, send, base)
+
+    return call(
+        body,
+        [((requests, 2 * cols), BF16), ((requests, cols), F32)],
+        [pltpu.VMEM((requests, cols), F32)],
+        smem=(0,),
+    )(me_kv, where, weight, sent, *pieces)
+
+
+def norm_and_pages(base, sent, got, gain, pages):
+    rows, cols = base.shape
+    count, wide = pages.shape
+    lanes = wide * count // rows
+
+    def body(base_ref, sent_ref, got_ref, gain_ref, pages_ref, middle, out):
+        mid = base_ref[...] + got_ref[:, 0:cols].astype(F32)
+        far = got_ref[:, cols:].astype(F32) + sent_ref[:, 0:cols].astype(F32)
+        squares = jnp.sum(mid * mid + far * far, axis=1, keepdims=True)
+        middle[...] = mid
+        out[:, 0:cols] = (
+            mid * lax.rsqrt(squares / (2 * cols) + EPSILON) * gain_ref[...]
+        ).astype(BF16)
+        for n in range(rows // count):
+            out[n * count : (n + 1) * count, cols:] = pages_ref[:, n * lanes : (n + 1) * lanes]
+
+    return call(body, [((rows, cols), F32), ((rows, cols + lanes), BF16)])(
+        base, sent, got, gain.reshape(1, -1), pages
+    )
+
+
+def join(parts, cols, pages):
+    rows, wide = parts[0].shape
+    lanes = wide - cols
+    count = len(parts)
+    quarters = rows // pages
+
+    def body(*refs):
+        outs, out_pages = refs[-3:-1], refs[-1]
+        for n in range(count):
+            low = n % (count // 2) * rows
+            outs[n // (count // 2)][low : low + rows, :] = refs[n][:, 0:cols]
+            for k in range(quarters):
+                out_pages[n * pages : (n + 1) * pages, k * lanes : (k + 1) * lanes] = refs[n][
+                    k * pages : (k + 1) * pages, cols:
+                ]
+
+    return call(
+        body,
+        [((count // 2 * rows, cols), BF16)] * 2 + [((count * pages, quarters * lanes), BF16)],
+    )(*parts)
+
+
+def first_norm(base, sent, got, gain):
+    rows, cols = base.shape
+
+    def body(base_ref, sent_ref, got_ref, gain_ref, middle, normed):
+        mid = base_ref[...] + got_ref[:, 0:cols].astype(F32)
+        far = got_ref[:, cols:].astype(F32) + sent_ref[:, 0:cols].astype(F32)
+        squares = jnp.sum(mid * mid + far * far, axis=1, keepdims=True)
+        middle[...] = mid
+        normed[...] = (
+            mid * lax.rsqrt(squares / (2 * cols) + EPSILON) * gain_ref[...]
+        ).astype(BF16)
+
+    return call(body, [((rows, cols), F32), ((rows, cols), BF16)])(
+        base, sent, got, gain.reshape(1, -1)
+    )
+
+
+def routes(info, experts, slots, block_rows, skip):
+    top = info.shape[0] // 2
+    tokens = info.shape[1]
+    token = iota((top, tokens), 1) % block_rows
+    odd = (token + iota((top, tokens), 0)) % 2 == 1
+    hits, gates = [], []
+    for s in range(slots):
+        wanted = jnp.where(odd, experts[1, s], experts[0, s]).astype(F32)
+        hit = (info[0:top] == wanted) & (token >= skip)
+        hits.append(jnp.sum(hit.astype(F32), axis=0, keepdims=True))
+        gates.append(jnp.sum(jnp.where(hit, info[top:], 0.0), axis=0, keepdims=True))
+    fill = [jnp.zeros((8 - slots, tokens), F32)] if slots < 8 else []
+    stacked = jnp.concatenate(hits + fill, axis=0)
+    row, col = iota((tokens, tokens), 0), iota((tokens, tokens), 1)
+    before = ((row < col) & (row // block_rows == col // block_rows)).astype(BF16)
+    ranks = dot(stacked.astype(BF16), before).astype(jnp.int32)
+    places = [jnp.where(hits[s] > 0.0, ranks[s : s + 1], -1) for s in range(slots)]
+    return places, gates
+
+
+def one_hot(place, block_rows):
+    tokens = place.shape[1]
+    shape = (tokens // block_rows * CAP, tokens)
+    row = iota(shape, 0)
+    return (place == row % CAP) & (iota(shape, 1) // block_rows == row // CAP)
+
+
+def plan(sent, first, top, experts, me_pg, slots, rows, skip, zs):
+    part = zs * CAP
+    tokens = zs * rows
+
+    def body(pg, es, sent_ref, picks, gates, dec_gates):
+        for g in range(4):
+            info = routing(sent_ref, pg[0], group_masks(g, zs), first, top, rows)
+            places, shares = routes(info, es, slots, rows, 0 if g % 2 else skip)
+            for s in range(slots):
+                hot = one_hot(places[s], rows)
+                low = s * part
+                picks[g, low : low + part, :] = hot.astype(BF16)
+                gates[g, low : low + part, :] = jnp.broadcast_to(
+                    jnp.sum(jnp.where(hot, shares[s], 0.0), axis=1, keepdims=True), (part, 128)
+                )
+        masks = group_masks(0, zs) + group_masks(2, zs)
+        count = len(masks) * skip
+        info = routing(sent_ref, pg[0], masks, first, top, skip)
+        ids, shares = info[0:top], info[top:]
+        odd = (iota((top, count), 1) % skip + iota((top, count), 0)) % 2 == 1
+        eye = iota((count, count), 0) == iota((count, count), 1)
+        for s in range(slots):
+            wanted = jnp.where(odd, es[1, s], es[0, s]).astype(F32)
+            share = jnp.sum(jnp.where(ids == wanted, shares, 0.0), axis=0, keepdims=True)
+            dec_gates[s * count : (s + 1) * count, :] = jnp.broadcast_to(
+                jnp.sum(jnp.where(eye, share, 0.0), axis=1, keepdims=True), (count, 128)
+            )
+
+    return call(
+        body,
+        [
+            ((4, slots * part, tokens), BF16),
+            ((4, slots * part, 128), F32),
+            ((slots * 2 * zs * skip, 128), F32),
+        ],
+        smem=(0, 1),
+    )(me_pg, experts, sent)
+
+
+def load(arrays):
+    count = len(arrays)
+
+    def body(*refs):
+        sems = refs[-1]
+        copies = [
+            pltpu.make_async_copy(refs[n].at[s], refs[count + n].at[s], sems.at[n, s])
+            for n in range(count)
+            for s in range(arrays[n].shape[0])
+        ]
+        for copy in copies:
+            copy.start()
+        for copy in copies:
+            copy.wait()
+
+    return call(
+        body,
+        [(x.shape, x.dtype) for x in arrays],
+        [pltpu.SemaphoreType.DMA((count, arrays[0].shape[0]))],
+        hbm=tuple(range(count)),
+        vmem=44,
+    )(*arrays)
+
+
+def products(xs, w_ref, side, out):
+    half = out.shape[2] // 2
+    for s in range(out.shape[0]):
+        x = xs[s] if len(xs.shape) == 3 else xs[...]
+        for k in range(2):
+            low = pl.multiple_of(k * 2 * half + side * half, 128)
+            out[s, :, k * half : (k + 1) * half] = dot(x, w_ref[s, :, pl.ds(low, half)]).astype(
+                out.dtype
+            )
+
+
+def gather(groups, which, picks, w, me_kv, me_pg, rows, skip, decode=None):
+    count, slots = len(groups), w.shape[0]
+    pieces = len(groups[0])
+    cols = w.shape[1]
+    tokens = pieces * groups[0][0].shape[0]
+    zs = tokens // rows
+    part = zs * CAP
+    ff = w.shape[2] // 2
+
+    def body(me, pg, w_ref, picks_ref, *refs):
+        xs, send = refs[-2:]
+        for n, g in enumerate(which):
+            x = jnp.concatenate(
+                [ref[...] for ref in refs[n * pieces : (n + 1) * pieces]], axis=0
+            )
+            if decode is not None:
+                dec = refs[count * pieces][...]
+                shape = (tokens, dec.shape[0])
+                row = iota(shape, 0)
+                source = jnp.zeros(shape, jnp.int32)
+                for z, mask in enumerate(group_masks(g, zs)):
+                    source = jnp.where(row // rows == z, (pg[0] ^ mask) * skip, source)
+                late = row % rows < skip
+                put = late & (iota(shape, 1) == source + row % rows)
+                x = jnp.where(
+                    iota((tokens, cols), 0) % rows < skip,
+                    dot(put.astype(BF16), dec),
+                    x.astype(F32),
+                ).astype(BF16)
+            got = dot(picks_ref[g], x).astype(BF16)
+            for s in range(slots):
+                xs[s, n * part : (n + 1) * part, :] = got[s * part : (s + 1) * part]
+        products(xs, w_ref, 1 - me[0], send)
+
+    more = [] if decode is None else [decode]
+    return call(
+        body,
+        [((slots, count * part, cols), BF16), ((slots, count * part, ff), BF16)],
+        smem=(0, 1),
+    )(me_kv, me_pg, w, picks, *[x for group in groups for x in group], *more)
+
+
+def pick_decode(normed, w, me_kv, me_pg, skip, zs):
+    slots = w.shape[0]
+    total, cols = normed.shape
+    masks = group_masks(0, zs) + group_masks(2, zs)
+    rows = len(masks) * skip
+
+    def body(me, pg, w_ref, x_ref, xs, send):
+        row = iota((rows, total), 0)
+        source = jnp.zeros((rows, total), jnp.int32)
+        for n, mask in enumerate(masks):
+            source = jnp.where(row // skip == n, (pg[0] ^ mask) * skip, source)
+        put = iota((rows, total), 1) == source + row % skip
+        xs[...] = dot(put.astype(BF16), x_ref[...]).astype(BF16)
+        products(xs, w_ref, 1 - me[0], send)
+
+    return call(
+        body, [((rows, cols), BF16), ((slots, rows, w.shape[2] // 2), BF16)], smem=(0, 1)
+    )(me_kv, me_pg, w, normed)
+
+
+def own_products(xs, w, me_kv):
+    def body(me, w_ref, x_ref, out):
+        products(x_ref, w_ref, me[0], out)
+
+    return call(body, [((w.shape[0], xs.shape[-2], w.shape[2] // 2), F32)], smem=(0,))(
+        me_kv, w, xs
+    )[0]
+
+
+def activate(own, got):
+    slots, rows, ff = own.shape
+    half = ff // 2
+
+    def body(own_ref, got_ref, out):
+        gate = own_ref[:, :, 0:half] + got_ref[:, :, 0:half].astype(F32)
+        up = own_ref[:, :, half:] + got_ref[:, :, half:].astype(F32)
+        out[...] = (gate / (1.0 + jnp.exp(-gate)) * up).astype(BF16)
+
+    return call(body, [((slots, rows, half), BF16)])(own, got)[0]
+
+
+def outputs(near_ref, far_ref, w_ref, me, s):
+    half = near_ref.shape[2]
+    made = dot(near_ref[s], w_ref[s, pl.ds(pl.multiple_of(me * half, 128), half), :])
+    return made + dot(far_ref[s], w_ref[s, pl.ds(pl.multiple_of((1 - me) * half, 128), half), :])
+
+
+def down_decode(near, far, w_down, gates, me_kv):
+    slots, rows, _ = near.shape
+    cols = w_down.shape[2]
+
+    def body(me, w_ref, near_ref, far_ref, gates_ref, out):
+        total = jnp.zeros((rows, cols), F32)
+        for s in range(slots):
+            made = outputs(near_ref, far_ref, w_ref, me[0], s)
+            gate = gates_ref[s * rows : (s + 1) * rows, 0:1]
+            total = total + made.astype(BF16).astype(F32) * gate
+        out[...] = total
+
+    return call(body, [((rows, cols), F32)], smem=(0,))(me_kv, w_down, near, far, gates)[0]
+
+
+def down(near, far, w_down, which, picks, gates, me_kv, rows, skip, decode=None):
+    slots, total_rows, _ = near.shape
+    cols = w_down.shape[2]
+    count = len(which)
+    part = total_rows // count
+    blocks = part // CAP
+
+    def body(me, w_ref, near_ref, far_ref, picks_ref, gates_ref, *refs):
+        outs = refs[-count:]
+        made = [outputs(near_ref, far_ref, w_ref, me[0], s) for s in range(slots)]
+        for n, g in enumerate(which):
+            parts = jnp.concatenate(
+                [made[s][n * part : (n + 1) * part] for s in range(slots)], axis=0
+            )
+            parts = (parts * gates_ref[g, :, 0:1]).astype(BF16)
+            total = t_dot(picks_ref[g], parts)
+            outs[n][...] = total.astype(BF16)
+            if decode is None:
+                continue
+            for b in range(blocks):
+                late = (n * blocks + b) * skip
+                late = jnp.concatenate(
+                    [refs[0][late : late + skip, :], total[b * rows + skip : b * rows + 16]], axis=0
+                )
+                outs[n][b * rows : b * rows + 16, :] = late.astype(BF16)
+
+    more = [] if decode is None else [decode]
+    return call(body, [((blocks * rows, cols), BF16)] * count, smem=(0,))(
+        me_kv, w_down, near, far, picks, gates, *more
+    )
+
+
+def split_sum(a, b, blocks, first=BF16):
+    tokens, cols = a.shape
+    high = tokens // blocks
+
+    def body(a_ref, b_ref, *outs):
+        for n in range(blocks):
+            part = slice(n * high, (n + 1) * high)
+            total = a_ref[part, :].astype(F32) + b_ref[part, :].astype(F32)
+            outs[n][...] = total.astype(outs[n].dtype)
+
+    return call(body, [((high, cols), first)] + [((high, cols), BF16)] * (blocks - 1))(a, b)
+
+
+def line_base(middle, decode_middle, own, parts, me_pg, skip):
+    rows, cols = middle.shape
+
+    def body(pg, mid, dec, *refs):
+        out = refs[-1]
+        total = refs[0][...]
+        for ref in refs[1:-1]:
+            total = total + ref[...].astype(F32)
+        out[...] = total + mid[...]
+        put = iota((8, dec.shape[0]), 1) == pg[0] * skip + iota((8, dec.shape[0]), 0)
+        put = put & (iota((8, dec.shape[0]), 0) < skip)
+        stream = dot(put.astype(F32), dec[...], HIGH)
+        stream = jnp.where(iota((8, cols), 0) < skip, stream, mid[0:8, :])
+        out[0:8, :] = total[0:8] + stream
+
+    return call(body, [((rows, cols), F32)], smem=(0,))(
+        me_pg, middle, decode_middle, own, *parts
+    )[0]
+
+
+def close(base, parts):
+    rows, cols = base.shape
+
+    def body(base_ref, *refs):
+        mixed, squares = refs[-2:]
+        total = base_ref[...]
+        for ref in refs[:-2]:
+            total = total + ref[...].astype(F32)
+        mixed[...] = total
+        total = total * total
+        folded = total[:, 0:128]
+        for n in range(1, cols // 128):
+            folded = folded + total[:, n * 128 : (n + 1) * 128]
+        squares[...] = folded
+
+    return call(body, [((rows, cols), F32), ((rows, 128), F32)])(base, *parts)
+
+
+def last_norm(mixed, near, far, gain):
+    rows, cols = mixed.shape
+
+    def body(mixed_ref, near_ref, far_ref, gain_ref, out):
+        squares = jnp.sum(near_ref[...] + far_ref[...], axis=1, keepdims=True)
+        out[...] = (
+            mixed_ref[...] * lax.rsqrt(squares / (2 * cols) + EPSILON) * gain_ref[...]
+        ).astype(BF16)
+
+    return call(body, [((rows, cols), BF16)])(mixed, near, far, gain.reshape(1, -1))[0]
+
+
+def line_pg(x, n_pg):
+    return [x] + [swap_pg(x, 4 * z, n_pg) for z in range(1, n_pg // 4)]
+
+
+def fast_local(
+    residual_in,
+    queries,
+    prefill_attn,
+    kv_cache,
+    page_table,
+    lengths,
+    out_weight,
+    norm_gain_in,
+    norm_gain_out,
+    expert_ids,
+    route_weight,
+    slot_table,
+    w_gate_up,
+    w_down,
+):
+    n_pg = lax.axis_size("pg")
+    me = lax.axis_index("pg")
+    me_kv = lax.axis_index("kv").reshape(1).astype(jnp.int32)
+    me_pg = me.reshape(1).astype(jnp.int32)
+    rows, cols = residual_in.shape
+    own_req = queries.shape[0]
+    slots = w_gate_up.shape[0]
+    pages, _, page_len, wide = kv_cache.shape
+    head_dim = wide // 2
+    max_pages = page_table.shape[1]
+    top = expert_ids.shape[1]
+    zs = n_pg // 4
+    first = 2 * own_req * cols // 128
+
+    packed = pack(queries, residual_in, expert_ids, route_weight, n_pg)
+    sent = lax.all_to_all(packed, "pg", split_axis=0, concat_axis=0, tiled=True)
+    send, base = project_prefill(after(prefill_attn, packed), out_weight, residual_in, me_kv)
+
+    mine = me * slots + jnp.arange(slots, dtype=jnp.int32)
+    expert = jnp.arange(slot_table.shape[0], dtype=jnp.int32)
+    experts = jnp.max(
+        jnp.where(slot_table[:, :, None] == mine[None, None, :], expert[:, None, None], -1), axis=0
+    )
+    page_ids = me * pages + jnp.arange(pages, dtype=jnp.int32)
+    flat_table = page_table.reshape(-1)
+    entry_index = jnp.arange(flat_table.shape[0], dtype=jnp.int32)
+    found = jnp.sum(
+        jnp.where(flat_table[None, :] == page_ids[:, None], entry_index[None, :], 0), axis=1
+    )
+    owner = found // max_pages
+    owner_len = jnp.sum(
+        jnp.where(
+            owner[:, None] == jnp.arange(lengths.shape[0], dtype=jnp.int32)[None, :],
+            lengths[None, :],
+            0,
+        ),
+        axis=1,
+    )
+    live = owner_len - found % max_pages * page_len
+    partial = page_attention(sent, kv_cache, owner, live, own_req, cols)
+    middle, payload = norm_and_pages(
+        base, send, after(swap_kv(send), partial), norm_gain_in, partial
+    )
+    line = [swap_pg(payload, 4 * z, n_pg) for z in range(1, zs)]
+    picks, gates, dec_gates = plan(
+        after(sent, payload), first, top, experts, me_pg, slots, rows, own_req, zs
+    )
+    w_units, w_rows = load(after([w_gate_up, w_down], picks))
+    *near, near_pages = join([payload] + after(line, w_units), cols, pages)
+    across_pages = swap_pg(near_pages, 2, n_pg)
+    near_pages_core = swap_pg(near_pages, 1, n_pg)
+
+    def swap_halves(halves, mask):
+        return [swap_pg(x, mask, n_pg) for x in halves]
+
+    def gathered(which, groups, decode=None):
+        return gather(groups, which, picks, w_units, me_kv, me_pg, rows, own_req, decode)
+
+    xs0, out0 = gathered([0, 2], [near, swap_halves(near, 1)])
+    got0 = swap_kv(out0)
+    across = swap_halves(near, 2)
+    across_pages = after(across_pages, out0)
+    pieces = [near_pages, across_pages, near_pages_core, swap_pg(across_pages, 1, n_pg)]
+    away = (page_table.T // pages) ^ me
+    where = ((away % 2) * 2 + away // 2 % 2) * zs + away // 4
+    where = (where * pages + page_table.T % pages).reshape(-1, 1)
+    dec_send, dec_base = project_decode(
+        pieces, where, sent, out_weight, me_kv, own_req, head_dim
+    )
+    dec_got = swap_kv(dec_send)
+    across = after(across, dec_send)
+    across_core = swap_halves(across, 1)
+    near0 = activate(own_products(xs0, w_units, me_kv), after(got0, across))
+    far0 = swap_kv(near0)
+    dec_middle, dec_normed = first_norm(dec_base, dec_send, after(dec_got, near0), norm_gain_in)
+    xs2, out2 = pick_decode(dec_normed, w_units, me_kv, me_pg, own_req, zs)
+    got2 = swap_kv(out2)
+    xs1, out1 = gathered([1, 3], after([across, across_core], out2), dec_normed)
+    got1 = swap_kv(out1)
+    own1 = own_products(xs1, w_units, me_kv)
+    own2 = own_products(xs2, w_units, me_kv)
+    near2 = activate(own2, after(got2, out1))
+    far2 = swap_kv(near2)
+    decode = down_decode(near2, after(far2, far0), w_rows, dec_gates, me_kv)
+    keep0, give0 = down(
+        near0, far0, w_rows, [0, 2], picks, gates, me_kv, rows, own_req, decode
+    )
+    back0 = swap_pg(give0, 1, n_pg)
+    near1 = activate(own1, after(got1, give0))
+    far1 = swap_kv(near1)
+    parts0 = split_sum(keep0, after(back0, near1), zs, F32)
+    lines0 = [swap_pg(parts0[z], 4 * z, n_pg) for z in range(1, zs)]
+    base = line_base(middle, dec_middle, parts0[0], lines0, me_pg, own_req)
+    keep1, give1 = down(near1, after(far1, base), w_rows, [1, 3], picks, gates, me_kv, rows, own_req)
+    parts1 = split_sum(keep1, swap_pg(give1, 1, n_pg), zs)
+    mixed, squares = close(base, [swap_pg(parts1[z], 4 * z + 2, n_pg) for z in range(zs)])
+    return last_norm(mixed, squares, swap_kv(squares), norm_gain_out)
+
+
 def solution(mesh):
+    fast = mesh.shape["kv"] == 2 and mesh.shape["pg"] == 16
+    local = fast_local if fast else general_local
     in_specs = (
         P("pg", "kv"),
         P("pg", "kv"),

time: 473 us -> 122 us (0.26)
  blocking collectives: 158 us -> 0 us
  waiting for transfers between devices: 136 us -> 42.7 us
  local copies, waits for them, and re-layouts: 89.1 us -> 18.3 us
  other arithmetic: 47 us -> 0.64 us
  starting transfers between devices: 5.88 us -> 36.6 us
  Pallas kernels: 0 us -> 22.4 us
  matrix products: 18.4 us -> 0 us
  between operations: 13.4 us -> 0.36 us
    all_gather x3 -> x0, waiting for transfers between devices: 106 us -> none  [the longest x1 57.9 us: local(): lax.all_gather(w_down, 'kv', axis=2, tiled=True)]
    all_to_all x3 -> x0, blocking collectives: 84.6 us -> none  [the longest x1 34.9 us: local(): lax.all_to_all(outgoing, 'pg', split_axis=0, concat_axis=0, tiled=True)]
    all_gather x3 -> x0, blocking collectives: 63.1 us -> none  [the longest x2 39.5 us: merged_2(): lax.all_gather(a.astype(kind), axis)]
    ppermute x0 -> x30, waiting for transfers between devices: none -> 38.2 us  [the longest x21 23.8 us: swap_pg(): return lax.ppermute(x, 'pg', [(i, i ^ mask) for i in range(n)])]
    add x34 -> x3, other arithmetic: 35.3 us -> 0.04 us  [the longest x1 0.03 us: fast_local(): where = (where * pages + page_table.T % pages).reshape(-1, 1)]
    ppermute x0 -> x30, starting transfers between devices: none -> 29.2 us  [the longest x21 20.3 us: swap_pg(): return lax.ppermute(x, 'pg', [(i, i ^ mask) for i in range(n)])]
    pallas_call x0 -> x26, Pallas kernels: none -> 22.4 us  [run(): pl.pallas_call(body, out_shape=[jax.ShapeDtypeStruct(s, d) for s, d in ou...]
    all_to_all x1, waiting for transfers between devices: 24.4 us -> 4.53 us  [fast_local(): sent = lax.all_to_all(packed, 'pg', split_axis=0, concat_axis=0, tiled=True)]
  transfers between devices with their start and end apart: 5 -> 31, of which waited for: 4 -> 15; matrix products, arithmetic and copies ran while one was open for 5% -> 1% of each run, Pallas kernels for 0% -> 15%
where the time goes in v2:
time: 122 us; the launch traced here: 121 us
  waiting for transfers between devices  42.7 us (35%)
  starting transfers between devices  36.6 us (30%)
  Pallas kernels  22.4 us (18%)
  local copies, waits for them, and re-layouts  18.3 us (15%)
    ppermute x21, waiting for transfers between devices, swap_pg(): return lax.ppermute(x, 'pg', [(i, i ^ mask) for i in range(n)])  23.8 us
    pallas_call x26, Pallas kernels, run(): pl.pallas_call(body, out_shape=[jax.ShapeDtypeStruct(s, d) for s, d in ou...  22.4 us
    ppermute x21, starting transfers between devices, swap_pg(): return lax.ppermute(x, 'pg', [(i, i ^ mask) for i in range(n)])  20.3 us
    unnamed x63, local copies, waits for them, and re-layouts  17.6 us
    ppermute x9, waiting for transfers between devices, swap_kv(): return lax.ppermute(x, 'kv', [(0, 1), (1, 0)])  14.4 us
    ppermute x9, starting transfers between devices, swap_kv(): return lax.ppermute(x, 'kv', [(0, 1), (1, 0)])  8.83 us
    all_to_all x1, starting transfers between devices, fast_local(): sent = lax.all_to_all(packed, 'pg', split_axis=0, concat_axis=0, tiled=True)  7.39 us
    all_to_all x1, waiting for transfers between devices, fast_local(): sent = lax.all_to_all(packed, 'pg', split_axis=0, concat_axis=0, tiled=True)  4.53 us
  transfers between devices with their start and end apart: 31, of which 15 were waited for; matrix products, arithmetic and copies ran while one was open for 1% of the time, Pallas kernels for 15%

profile of v2, /device:TPU:0, one launch (start us, length us, event | category | flops | bytes accessed | tf_op | source)
XLA Modules:
  0.0 121.0 jit_solution(1761514151279082326)
XLA Ops:
  3.8 7.4 %all-to-all-start = ((bf16[16,80,128]{2,1,0:T(8,128)(2,1)}), bf16[16,80,128]{2,1,0:T(8,128)(2,1)S(1)}, u32[]{:S(2)}, u32[]{:S(2)}) async-start(bf16[16,80,128]{2,1,0:T(8,128)(2,1)} %shard_map.136), calls=%async_computation | async-start | bytes 655360 | tf_op jit(solution)/shard_map/all_to_all | solution.py:812
  17.7 4.5 %all-to-all-done.sent_ref = bf16[16,80,128]{2,1,0:T(8,128)(2,1)S(1)} async-done(((bf16[16,80,128]{2,1,0:T(8,128)(2,1)}), bf16[16,80,128]{2,1,0:T(8,128)(2,1)S(1)}, u32[]{:S(2)}, u32[]{:S(2)}) %all-to-all-start) | async-done | bytes 327712 | tf_op jit(solution)/shard_map/all_to_all | solution.py:812
  25.0 2.3 %collective-permute-start.2 = (bf16[64,1024]{1,0:T(8,128)(2,1)S(1)}, bf16[64,1024]{1,0:T(8,128)(2,1)S(1)}, u32[]{:S(2)}, u32[]{:S(2)}) collective-permute-start(bf16[64,1024]{1,0:T(8,128)(2,1)S(1)} %get-tuple-element.68.refs_0_), channel_id=1, source_target_pairs={{0,8},{1,9},{2,10},{3,11},{4,12},{5,13},{6,14},{7,15},{8,0},{9,1},... | collective-permute-start | bytes 393224 | tf_op jit(solution)/shard_map/ppermute | solution.py:242
  27.3 1.8 %collective-permute-start.3 = (bf16[64,1024]{1,0:T(8,128)(2,1)S(1)}, bf16[64,1024]{1,0:T(8,128)(2,1)}, u32[]{:S(2)}, u32[]{:S(2)}) collective-permute-start(bf16[64,1024]{1,0:T(8,128)(2,1)S(1)} %get-tuple-element.68.refs_0_), channel_id=1, source_target_pairs={{0,12},{1,13},{2,14},{3,15},{4,8},{5,9},{6,10},{7,11},{8,4},{9,5},... | collective-permute-start | bytes 393224 | tf_op jit(solution)/shard_map/ppermute | solution.py:242
  31.8 1.7 %copy-done.6 = bf16[3,512,768]{2,1,0:T(8,128)(2,1)S(1)} copy-done((bf16[3,512,768]{2,1,0:T(8,128)(2,1)S(1)}, bf16[3,512,768]{2,1,0:T(8,128)(2,1)}, u32[]{:S(2)}) %copy-start.6) | copy-done | bytes 2359320
  33.5 2.4 %shard_map.141 = (bf16[3,768,1024]{2,1,0:T(8,128)(2,1)S(1)}, bf16[3,512,768]{2,1,0:T(8,128)(2,1)S(1)}) custom-call(bf16[3,768,1024]{2,1,0:T(8,128)(2,1)} %refs_0_, bf16[3,512,768]{2,1,0:T(8,128)(2,1)S(1)} %copy-done.6), custom_call_target="tpu_custom_call" | custom-call | flops 1 | bytes 1 | tf_op jit(solution)/shard_map/pallas_call | solution.py:202
  35.9 1.9 %collective-permute-done.2.refs_2_ = bf16[64,1024]{1,0:T(8,128)(2,1)S(1)} collective-permute-done((bf16[64,1024]{1,0:T(8,128)(2,1)S(1)}, bf16[64,1024]{1,0:T(8,128)(2,1)S(1)}, u32[]{:S(2)}, u32[]{:S(2)}) %collective-permute-start.2) | collective-permute-done | bytes 131104 | tf_op jit(solution)/shard_map/ppermute | solution.py:242
  39.4 1.7 %shard_map.142 = (bf16[128,768]{1,0:T(8,128)(2,1)}, bf16[128,768]{1,0:T(8,128)(2,1)}, bf16[64,1024]{1,0:T(8,128)(2,1)S(1)}) custom-call(bf16[64,1024]{1,0:T(8,128)(2,1)S(1)} %get-tuple-element.68.refs_0_, bf16[64,1024]{1,0:T(8,128)(2,1)S(1)} %collective-permute-done.1.refs_1_, bf16[64,1024]{1,0:T(8,128)(2,1)S(1)} %copy-done.17, ...), custom_call_target="tpu_custom_call" | custom-call | flops 1 | bytes 1 | tf_op jit(solution)/shard_map/pallas_call | solution.py:202
  43.0 2.5 %shard_map.143 = (bf16[3,128,768]{2,1,0:T(8,128)(2,1)S(1)}, bf16[3,128,512]{2,1,0:T(8,128)(2,1)}) custom-call(s32[1]{0:T(128)} %bitcast.1.me, s32[1]{0:T(128)} %bitcast.pg, bf16[3,768,1024]{2,1,0:T(8,128)(2,1)S(1)} %get-tuple-element.73.w_ref, bf16[4,192,256]{2,1,0:T(8,128)(2,1)S(1)} %get-tuple-element.70.picks_ref, ...), custom_call_target="tpu_custom_call" | custom-call | flops 1 | bytes 1 | tf_op jit(solution)/shard_map/pallas_call | solution.py:202
  51.5 1.7 %copy-done.3 = bf16[768,1536]{1,0:T(8,128)(2,1)S(1)} copy-done((bf16[768,1536]{1,0:T(8,128)(2,1)S(1)}, bf16[768,1536]{1,0:T(8,128)(2,1)}, u32[]{:S(2)}) %copy-start.3) | copy-done | bytes 2359320
  54.2 2.4 %shard_map.144 = (bf16[64,1536]{1,0:T(8,128)(2,1)S(1)}, f32[64,768]{1,0:T(8,128)S(1)}) custom-call(s32[1]{0:T(128)} %bitcast.1.me, s32[256,1]{1,0:T(8,128)S(1)} %reshape.49.where_ref, bf16[768,1536]{1,0:T(8,128)(2,1)S(1)} %copy-done.3, bf16[16,80,128]{2,1,0:T(8,128)(2,1)S(1)} %copy-done.5, bf16[64,1024]{1,0:T(8,128)(2,1)S(1)} %get-tuple-element.77.refs_0_, ...), custom_call_target="tpu_custom_call" | custom-call | flops 1 | bytes 1 | tf_op jit(solution)/shard_map/pallas_call | solution.py:202
  57.1 2.5 %collective-permute-done.12.refs_1_ = bf16[128,768]{1,0:T(8,128)(2,1)} collective-permute-done((bf16[128,768]{1,0:T(8,128)(2,1)}, bf16[128,768]{1,0:T(8,128)(2,1)}, u32[]{:S(2)}, u32[]{:S(2)}) %collective-permute-start.12) | collective-permute-done | bytes 196640 | tf_op jit(solution)/shard_map/ppermute | solution.py:242
  60.2 2.3 %copy-done.1 = bf16[3,768,1024]{2,1,0:T(8,128)(2,1)S(1)} copy-done((bf16[3,768,1024]{2,1,0:T(8,128)(2,1)S(1)}, bf16[3,768,1024]{2,1,0:T(8,128)(2,1)}, u32[]{:S(2)}) %copy-start.1) | copy-done | bytes 4718616
  67.4 2.1 %shard_map.150 = (bf16[3,128,768]{2,1,0:T(8,128)(2,1)S(1)}, bf16[3,128,512]{2,1,0:T(8,128)(2,1)S(1)}) custom-call(s32[1]{0:T(128)} %bitcast.1.me, s32[1]{0:T(128)} %bitcast.pg, bf16[3,768,1024]{2,1,0:T(8,128)(2,1)S(1)} %bitcast.23, bf16[4,192,256]{2,1,0:T(8,128)(2,1)S(1)} %get-tuple-element.70.picks_ref, bf16[128,768]{1,0:T(8,128)(2,1)} %collective-permute-done.11.refs_0_, ...), custom_call_target="tpu_custom_call" | custom-call | flops 1 | bytes 1 | tf_op jit(solution)/shard_map/pallas_call | solution.py:202
  70.6 3.8 %collective-permute-done.14.got_ref = bf16[3,32,512]{2,1,0:T(8,128)(2,1)S(1)} collective-permute-done((bf16[3,32,512]{2,1,0:T(8,128)(2,1)S(1)}, bf16[3,32,512]{2,1,0:T(8,128)(2,1)S(1)}, u32[]{:S(2)}, u32[]{:S(2)}) %collective-permute-start.14) | collective-permute-done | bytes 98336 | tf_op jit(solution)/shard_map/ppermute | solution.py:238
  75.1 7.9 %collective-permute-done.17.far_ref = bf16[3,32,256]{2,1,0:T(8,128)(2,1)S(1)} collective-permute-done((bf16[3,32,256]{2,1,0:T(8,128)(2,1)S(1)}, bf16[3,32,256]{2,1,0:T(8,128)(2,1)S(1)}, u32[]{:S(2)}, u32[]{:S(2)}) %collective-permute-start.17) | collective-permute-done | bytes 49184 | tf_op jit(solution)/shard_map/ppermute | solution.py:238
  86.2 2.5 %collective-permute-start.20 = (bf16[64,768]{1,0:T(8,128)(2,1)S(1)}, bf16[64,768]{1,0:T(8,128)(2,1)S(1)}, u32[]{:S(2)}, u32[]{:S(2)}) collective-permute-start(bf16[64,768]{1,0:T(8,128)(2,1)S(1)} %get-tuple-element.109), channel_id=1, source_target_pairs={{0,4},{1,5},{2,6},{3,7},{4,0},{5,1},{6,2},{7,3},{8,12},{9,13},{10,... | collective-permute-start | bytes 294920 | tf_op jit(solution)/shard_map/ppermute | solution.py:242
  89.2 1.9 %collective-permute-start.22 = (bf16[64,768]{1,0:T(8,128)(2,1)S(1)}, bf16[64,768]{1,0:T(8,128)(2,1)S(1)}, u32[]{:S(2)}, u32[]{:S(2)}) collective-permute-start(bf16[64,768]{1,0:T(8,128)(2,1)S(1)} %get-tuple-element.111), channel_id=1, source_target_pairs={{0,12},{1,13},{2,14},{3,15},{4,8},{5,9},{6,10},{7,11},{8,4},{9,5},... | collective-permute-start | bytes 294920 | tf_op jit(solution)/shard_map/ppermute | solution.py:242
  91.8 7.1 %collective-permute-done.21.refs_2_ = bf16[64,768]{1,0:T(8,128)(2,1)S(1)} collective-permute-done((bf16[64,768]{1,0:T(8,128)(2,1)S(1)}, bf16[64,768]{1,0:T(8,128)(2,1)S(1)}, u32[]{:S(2)}, u32[]{:S(2)}) %collective-permute-start.21) | collective-permute-done | bytes 98336 | tf_op jit(solution)/shard_map/ppermute | solution.py:242
  100.0 1.7 %collective-permute-done.24.b_ref = bf16[256,768]{1,0:T(8,128)(2,1)S(1)} collective-permute-done((bf16[256,768]{1,0:T(8,128)(2,1)S(1)}, bf16[256,768]{1,0:T(8,128)(2,1)S(1)}, u32[]{:S(2)}, u32[]{:S(2)}) %collective-permute-start.24) | collective-permute-done | bytes 393248 | tf_op jit(solution)/shard_map/ppermute | solution.py:242
  102.9 2.5 %collective-permute-start.26 = (bf16[64,768]{1,0:T(8,128)(2,1)S(1)}, bf16[64,768]{1,0:T(8,128)(2,1)S(1)}, u32[]{:S(2)}, u32[]{:S(2)}) collective-permute-start(bf16[64,768]{1,0:T(8,128)(2,1)S(1)} %get-tuple-element.116), channel_id=1, source_target_pairs={{0,6},{1,7},{2,4},{3,5},{4,2},{5,3},{6,0},{7,1},{8,14},{9,15},{10,... | collective-permute-start | bytes 294920 | tf_op jit(solution)/shard_map/ppermute | solution.py:242
  106.1 2.5 %collective-permute-start.28 = (bf16[64,768]{1,0:T(8,128)(2,1)S(1)}, bf16[64,768]{1,0:T(8,128)(2,1)S(1)}, u32[]{:S(2)}, u32[]{:S(2)}) collective-permute-start(bf16[64,768]{1,0:T(8,128)(2,1)S(1)} %get-tuple-element.118), channel_id=1, source_target_pairs={{0,14},{1,15},{2,12},{3,13},{4,10},{5,11},{6,8},{7,9},{8,6},{9,7},... | collective-permute-start | bytes 294920 | tf_op jit(solution)/shard_map/ppermute | solution.py:242
  108.8 7.3 %collective-permute-done.27.refs_2_ = bf16[64,768]{1,0:T(8,128)(2,1)S(1)} collective-permute-done((bf16[64,768]{1,0:T(8,128)(2,1)S(1)}, bf16[64,768]{1,0:T(8,128)(2,1)S(1)}, u32[]{:S(2)}, u32[]{:S(2)}) %collective-permute-start.27) | collective-permute-done | bytes 98336 | tf_op jit(solution)/shard_map/ppermute | solution.py:242
  117.5 2.8 %collective-permute-done.29.far_ref = f32[64,128]{1,0:T(8,128)S(1)} collective-permute-done((f32[64,128]{1,0:T(8,128)S(1)}, f32[64,128]{1,0:T(8,128)S(1)}, u32[]{:S(2)}, u32[]{:S(2)}) %collective-permute-start.29) | collective-permute-done | bytes 32800 | tf_op jit(solution)/shard_map/ppermute | solution.py:238
  (145 shorter events, 43.6 us)
Async XLA Ops:
  3.8 18.5 %all-to-all-start = ((bf16[16,80,128]{2,1,0:T(8,128)(2,1)}), bf16[16,80,128]{2,1,0:T(8,128)(2,1)S(1)}, u32[]{:S(2)}, u32[]{:S(2)}) async-start(bf16[16,80,128]{2,1,0:T(8,128)(2,1)} %shard_map.136), calls=%async_computation | async-start | bytes 655360 | tf_op jit(solution)/shard_map/all_to_all | solution.py:812
  15.2 8.7 %collective-permute-start = (bf16[64,1536]{1,0:T(8,128)(2,1)S(1)}, bf16[64,1536]{1,0:T(8,128)(2,1)S(1)}, u32[]{:S(2)}, u32[]{:S(2)}) collective-permute-start(bf16[64,1536]{1,0:T(8,128)(2,1)S(1)} %get-tuple-element.65.sent_ref), channel_id=1, source_target_pairs={{0,16},{16,0},{1,17},{17,1},{2,18},{18,2},{3,19},{19,3},{4,20},{20... | collective-permute-start | bytes 589832 | tf_op jit(solution)/shard_map/ppermute | solution.py:238
  24.7 11.2 %collective-permute-start.1 = (bf16[64,1024]{1,0:T(8,128)(2,1)S(1)}, bf16[64,1024]{1,0:T(8,128)(2,1)S(1)}, u32[]{:S(2)}, u32[]{:S(2)}) collective-permute-start(bf16[64,1024]{1,0:T(8,128)(2,1)S(1)} %get-tuple-element.68.refs_0_), channel_id=1, source_target_pairs={{0,4},{1,5},{2,6},{3,7},{4,0},{5,1},{6,2},{7,3},{8,12},{9,13},{10,... | collective-permute-start | bytes 393224 | tf_op jit(solution)/shard_map/ppermute | solution.py:242
  25.0 12.8 %collective-permute-start.2 = (bf16[64,1024]{1,0:T(8,128)(2,1)S(1)}, bf16[64,1024]{1,0:T(8,128)(2,1)S(1)}, u32[]{:S(2)}, u32[]{:S(2)}) collective-permute-start(bf16[64,1024]{1,0:T(8,128)(2,1)S(1)} %get-tuple-element.68.refs_0_), channel_id=1, source_target_pairs={{0,8},{1,9},{2,10},{3,11},{4,12},{5,13},{6,14},{7,15},{8,0},{9,1},... | collective-permute-start | bytes 393224 | tf_op jit(solution)/shard_map/ppermute | solution.py:242
  27.3 11.2 %collective-permute-start.3 = (bf16[64,1024]{1,0:T(8,128)(2,1)S(1)}, bf16[64,1024]{1,0:T(8,128)(2,1)}, u32[]{:S(2)}, u32[]{:S(2)}) collective-permute-start(bf16[64,1024]{1,0:T(8,128)(2,1)S(1)} %get-tuple-element.68.refs_0_), channel_id=1, source_target_pairs={{0,12},{1,13},{2,14},{3,15},{4,8},{5,9},{6,10},{7,11},{8,4},{9,5},... | collective-permute-start | bytes 393224 | tf_op jit(solution)/shard_map/ppermute | solution.py:242
  41.6 8.2 %collective-permute-start.4 = (bf16[64,1024]{1,0:T(8,128)(2,1)S(1)}, bf16[64,1024]{1,0:T(8,128)(2,1)}, u32[]{:S(2)}, u32[]{:S(2)}) collective-permute-start(bf16[64,1024]{1,0:T(8,128)(2,1)S(1)} %get-tuple-element.77.refs_0_), channel_id=1, source_target_pairs={{0,2},{1,3},{2,0},{3,1},{4,6},{5,7},{6,4},{7,5},{8,10},{9,11},{10,... | collective-permute-start | bytes 393224 | tf_op jit(solution)/shard_map/ppermute | solution.py:242
  46.3 16.7 %collective-permute-start.10 = (bf16[3,128,512]{2,1,0:T(8,128)(2,1)}, bf16[3,128,512]{2,1,0:T(8,128)(2,1)}, u32[]{:S(2)}, u32[]{:S(2)}) collective-permute-start(bf16[3,128,512]{2,1,0:T(8,128)(2,1)} %get-tuple-element.80), channel_id=1, source_target_pairs={{0,16},{16,0},{1,17},{17,1},{2,18},{18,2},{3,19},{19,3},{4,20},{20... | collective-permute-start | bytes 1179656 | tf_op jit(solution)/shard_map/ppermute | solution.py:238
  47.8 9.3 %collective-permute-start.11 = (bf16[128,768]{1,0:T(8,128)(2,1)}, bf16[128,768]{1,0:T(8,128)(2,1)}, u32[]{:S(2)}, u32[]{:S(2)}) collective-permute-start(bf16[128,768]{1,0:T(8,128)(2,1)} %get-tuple-element.78.refs_0_), channel_id=1, source_target_pairs={{0,2},{1,3},{2,0},{3,1},{4,6},{5,7},{6,4},{7,5},{8,10},{9,11},{10,... | collective-permute-start | bytes 589832 | tf_op jit(solution)/shard_map/ppermute | solution.py:242
  48.9 10.8 %collective-permute-start.12 = (bf16[128,768]{1,0:T(8,128)(2,1)}, bf16[128,768]{1,0:T(8,128)(2,1)}, u32[]{:S(2)}, u32[]{:S(2)}) collective-permute-start(bf16[128,768]{1,0:T(8,128)(2,1)} %get-tuple-element.79.refs_1_), channel_id=1, source_target_pairs={{0,2},{1,3},{2,0},{3,1},{4,6},{5,7},{6,4},{7,5},{8,10},{9,11},{10,... | collective-permute-start | bytes 589832 | tf_op jit(solution)/shard_map/ppermute | solution.py:242
  56.5 8.6 %collective-permute-start.9 = (bf16[64,1536]{1,0:T(8,128)(2,1)S(1)}, bf16[64,1536]{1,0:T(8,128)(2,1)S(1)}, u32[]{:S(2)}, u32[]{:S(2)}) collective-permute-start(bf16[64,1536]{1,0:T(8,128)(2,1)S(1)} %get-tuple-element.83.sent_ref), channel_id=1, source_target_pairs={{0,16},{16,0},{1,17},{17,1},{2,18},{18,2},{3,19},{19,3},{4,20},{20... | collective-permute-start | bytes 589832 | tf_op jit(solution)/shard_map/ppermute | solution.py:238
  59.7 7.7 %collective-permute-start.15 = (bf16[128,768]{1,0:T(8,128)(2,1)}, bf16[128,768]{1,0:T(8,128)(2,1)S(1)}, u32[]{:S(2)}, u32[]{:S(2)}) collective-permute-start(bf16[128,768]{1,0:T(8,128)(2,1)} %collective-permute-done.11.refs_0_), channel_id=1, source_target_pairs={{0,1},{1,0},{2,3},{3,2},{4,5},{5,4},{6,7},{7,6},{8,9},{9,8},{10,11... | collective-permute-start | bytes 589832 | tf_op jit(solution)/shard_map/ppermute | solution.py:242
  59.7 7.7 %collective-permute-start.16 = (bf16[128,768]{1,0:T(8,128)(2,1)}, bf16[128,768]{1,0:T(8,128)(2,1)S(1)}, u32[]{:S(2)}, u32[]{:S(2)}) collective-permute-start(bf16[128,768]{1,0:T(8,128)(2,1)} %collective-permute-done.12.refs_1_), channel_id=1, source_target_pairs={{0,1},{1,0},{2,3},{3,2},{4,5},{5,4},{6,7},{7,6},{8,9},{9,8},{10,11... | collective-permute-start | bytes 589832 | tf_op jit(solution)/shard_map/ppermute | solution.py:242
  64.5 18.5 %collective-permute-start.13 = (bf16[3,128,256]{2,1,0:T(8,128)(2,1)S(1)}, bf16[3,128,256]{2,1,0:T(8,128)(2,1)S(1)}, u32[]{:S(2)}, u32[]{:S(2)}) collective-permute-start(bf16[3,128,256]{2,1,0:T(8,128)(2,1)S(1)} %shard_map.146.near_ref), channel_id=1, source_target_pairs={{0,16},{16,0},{1,17},{17,1},{2,18},{18,2},{3,19},{19,3},{4,20},{20... | collective-permute-start | bytes 589832 | tf_op jit(solution)/shard_map/ppermute | solution.py:238
  65.9 8.5 %collective-permute-start.14 = (bf16[3,32,512]{2,1,0:T(8,128)(2,1)S(1)}, bf16[3,32,512]{2,1,0:T(8,128)(2,1)S(1)}, u32[]{:S(2)}, u32[]{:S(2)}) collective-permute-start(bf16[3,32,512]{2,1,0:T(8,128)(2,1)S(1)} %get-tuple-element.94), channel_id=1, source_target_pairs={{0,16},{16,0},{1,17},{17,1},{2,18},{18,2},{3,19},{19,3},{4,20},{20... | collective-permute-start | bytes 294920 | tf_op jit(solution)/shard_map/ppermute | solution.py:238
  69.5 15.5 %collective-permute-start.19 = (bf16[3,128,512]{2,1,0:T(8,128)(2,1)S(1)}, bf16[3,128,512]{2,1,0:T(8,128)(2,1)S(1)}, u32[]{:S(2)}, u32[]{:S(2)}) collective-permute-start(bf16[3,128,512]{2,1,0:T(8,128)(2,1)S(1)} %get-tuple-element.99), channel_id=1, source_target_pairs={{0,16},{16,0},{1,17},{17,1},{2,18},{18,2},{3,19},{19,3},{4,20},{20... | collective-permute-start | bytes 1179656 | tf_op jit(solution)/shard_map/ppermute | solution.py:238
  74.5 8.5 %collective-permute-start.17 = (bf16[3,32,256]{2,1,0:T(8,128)(2,1)S(1)}, bf16[3,32,256]{2,1,0:T(8,128)(2,1)S(1)}, u32[]{:S(2)}, u32[]{:S(2)}) collective-permute-start(bf16[3,32,256]{2,1,0:T(8,128)(2,1)S(1)} %shard_map.151.near_ref), channel_id=1, source_target_pairs={{0,16},{16,0},{1,17},{17,1},{2,18},{18,2},{3,19},{19,3},{4,20},{20... | collective-permute-start | bytes 147464 | tf_op jit(solution)/shard_map/ppermute | solution.py:238
  85.1 14.0 %collective-permute-start.23 = (bf16[3,128,256]{2,1,0:T(8,128)(2,1)S(1)}, bf16[3,128,256]{2,1,0:T(8,128)(2,1)S(1)}, u32[]{:S(2)}, u32[]{:S(2)}) collective-permute-start(bf16[3,128,256]{2,1,0:T(8,128)(2,1)S(1)} %shard_map.155.near_ref), channel_id=1, source_target_pairs={{0,16},{16,0},{1,17},{17,1},{2,18},{18,2},{3,19},{19,3},{4,20},{20... | collective-permute-start | bytes 589832 | tf_op jit(solution)/shard_map/ppermute | solution.py:238
  86.2 5.6 %collective-permute-start.20 = (bf16[64,768]{1,0:T(8,128)(2,1)S(1)}, bf16[64,768]{1,0:T(8,128)(2,1)S(1)}, u32[]{:S(2)}, u32[]{:S(2)}) collective-permute-start(bf16[64,768]{1,0:T(8,128)(2,1)S(1)} %get-tuple-element.109), channel_id=1, source_target_pairs={{0,4},{1,5},{2,6},{3,7},{4,0},{5,1},{6,2},{7,3},{8,12},{9,13},{10,... | collective-permute-start | bytes 294920 | tf_op jit(solution)/shard_map/ppermute | solution.py:242
  88.7 10.3 %collective-permute-start.21 = (bf16[64,768]{1,0:T(8,128)(2,1)S(1)}, bf16[64,768]{1,0:T(8,128)(2,1)S(1)}, u32[]{:S(2)}, u32[]{:S(2)}) collective-permute-start(bf16[64,768]{1,0:T(8,128)(2,1)S(1)} %get-tuple-element.110), channel_id=1, source_target_pairs={{0,8},{1,9},{2,10},{3,11},{4,12},{5,13},{6,14},{7,15},{8,0},{9,1},... | collective-permute-start | bytes 294920 | tf_op jit(solution)/shard_map/ppermute | solution.py:242
  89.2 9.7 %collective-permute-start.22 = (bf16[64,768]{1,0:T(8,128)(2,1)S(1)}, bf16[64,768]{1,0:T(8,128)(2,1)S(1)}, u32[]{:S(2)}, u32[]{:S(2)}) collective-permute-start(bf16[64,768]{1,0:T(8,128)(2,1)S(1)} %get-tuple-element.111), channel_id=1, source_target_pairs={{0,12},{1,13},{2,14},{3,15},{4,8},{5,9},{6,10},{7,11},{8,4},{9,5},... | collective-permute-start | bytes 294920 | tf_op jit(solution)/shard_map/ppermute | solution.py:242
  101.8 7.0 %collective-permute-start.25 = (bf16[64,768]{1,0:T(8,128)(2,1)S(1)}, bf16[64,768]{1,0:T(8,128)(2,1)S(1)}, u32[]{:S(2)}, u32[]{:S(2)}) collective-permute-start(bf16[64,768]{1,0:T(8,128)(2,1)S(1)} %get-tuple-element.115), channel_id=1, source_target_pairs={{0,2},{1,3},{2,0},{3,1},{4,6},{5,7},{6,4},{7,5},{8,10},{9,11},{10,... | collective-permute-start | bytes 294920 | tf_op jit(solution)/shard_map/ppermute | solution.py:242
  102.9 5.9 %collective-permute-start.26 = (bf16[64,768]{1,0:T(8,128)(2,1)S(1)}, bf16[64,768]{1,0:T(8,128)(2,1)S(1)}, u32[]{:S(2)}, u32[]{:S(2)}) collective-permute-start(bf16[64,768]{1,0:T(8,128)(2,1)S(1)} %get-tuple-element.116), channel_id=1, source_target_pairs={{0,6},{1,7},{2,4},{3,5},{4,2},{5,3},{6,0},{7,1},{8,14},{9,15},{10,... | collective-permute-start | bytes 294920 | tf_op jit(solution)/shard_map/ppermute | solution.py:242
  105.4 10.7 %collective-permute-start.27 = (bf16[64,768]{1,0:T(8,128)(2,1)S(1)}, bf16[64,768]{1,0:T(8,128)(2,1)S(1)}, u32[]{:S(2)}, u32[]{:S(2)}) collective-permute-start(bf16[64,768]{1,0:T(8,128)(2,1)S(1)} %get-tuple-element.117), channel_id=1, source_target_pairs={{0,10},{1,11},{2,8},{3,9},{4,14},{5,15},{6,12},{7,13},{8,2},{9,3},... | collective-permute-start | bytes 294920 | tf_op jit(solution)/shard_map/ppermute | solution.py:242
  106.1 10.0 %collective-permute-start.28 = (bf16[64,768]{1,0:T(8,128)(2,1)S(1)}, bf16[64,768]{1,0:T(8,128)(2,1)S(1)}, u32[]{:S(2)}, u32[]{:S(2)}) collective-permute-start(bf16[64,768]{1,0:T(8,128)(2,1)S(1)} %get-tuple-element.118), channel_id=1, source_target_pairs={{0,14},{1,15},{2,12},{3,13},{4,10},{5,11},{6,8},{7,9},{8,6},{9,7},... | collective-permute-start | bytes 294920 | tf_op jit(solution)/shard_map/ppermute | solution.py:242
  (38 other events, 208.7 us)

commit v3 on v2

--- a/solution.py
+++ b/solution.py
@@ -193,7 +193,7 @@
 HIGH = lax.Precision.HIGHEST
 
 
-def call(body, outs, scratch=(), smem=(), hbm=(), vmem=16):
+def call(body, outs, scratch=(), smem=(), hbm=(), vmem=16, flops=10**9):
     def run(*operands):
         kinds = [
             pltpu.SMEM if n in smem else pltpu.HBM if n in hbm else pltpu.VMEM
@@ -208,7 +208,7 @@
             compiler_params=pltpu.CompilerParams(
                 vmem_limit_bytes=vmem * 2**20
             ),
-            cost_estimate=pl.CostEstimate(flops=1, bytes_accessed=1, transcendentals=0),
+            cost_estimate=pl.CostEstimate(flops=flops, bytes_accessed=1, transcendentals=0),
         )(*operands)
 
     return run
@@ -247,25 +247,43 @@
     rows, top = expert_ids.shape
     tiles = cols // 128
     high = 2 * own_req * tiles
-    total = -(-(high + 3 * top) // 16) * 16
-
-    def body(q_ref, res_ref, ids_ref, gates_ref, out_ref, scr):
-        scr[...] = jnp.zeros((total, 128), F32)
+    total = high + top
+
+    def body(q_hbm, res_hbm, ids_hbm, gates_hbm, out_ref, scr, q_ref, res_ref, ids, gates, sems):
+        copies = [
+            pltpu.make_async_copy(q_hbm, q_ref, sems.at[0]),
+            pltpu.make_async_copy(res_hbm.at[0:16, :], res_ref, sems.at[1]),
+            pltpu.make_async_copy(ids_hbm, ids, sems.at[2]),
+            pltpu.make_async_copy(gates_hbm, gates, sems.at[3]),
+        ]
+        for copy in copies:
+            copy.start()
+        for copy in copies:
+            copy.wait()
         for n, ref in enumerate((q_ref, res_ref)):
             for i in range(tiles):
                 low = (n * tiles + i) * own_req
                 scr[low : low + own_req, :] = ref[0:own_req, 128 * i : 128 * (i + 1)].astype(F32)
-        gates = gates_ref[...]
-        gates_high = gates.astype(BF16).astype(F32)
-        for n, x in enumerate((ids_ref[...].astype(F32), gates_high, gates - gates_high)):
-            scr[high + n * top : high + (n + 1) * top, 0:rows] = x
+        scr[high:, 0:rows] = ids[...].astype(F32)
+        scr[high:, 64 : 64 + rows] = gates[...]
         packed = scr[...].astype(BF16)
         for g in range(n_pg):
             out_ref[g] = packed
 
-    return call(body, [((n_pg, total, 128), BF16)], [pltpu.VMEM((total, 128), F32)])(
-        queries, residual, expert_ids.T, route_weight.T
-    )[0]
+    return call(
+        body,
+        [((n_pg, total, 128), BF16)],
+        [
+            pltpu.VMEM((total, 128), F32),
+            pltpu.VMEM((own_req, cols), BF16),
+            pltpu.VMEM((16, cols), BF16),
+            pltpu.VMEM((top, rows), expert_ids.dtype),
+            pltpu.VMEM((top, rows), F32),
+            pltpu.SemaphoreType.DMA((4,)),
+        ],
+        hbm=(0, 1, 2, 3),
+        vmem=62,
+    )(queries, residual, expert_ids.T, route_weight.T)[0]
 
 
 def unpack(sent_ref, out, which, own_req):
@@ -279,11 +297,10 @@
 
 
 def routing(sent_ref, me, masks, first, top, count):
-    got = jnp.concatenate(
-        [sent_ref[me ^ mask, first : first + 3 * top, 0:count].astype(F32) for mask in masks],
-        axis=1,
-    )
-    return jnp.concatenate([got[0:top], got[top : 2 * top] + got[2 * top :]], axis=0)
+    got = [sent_ref[me ^ mask, first : first + top, :].astype(F32) for mask in masks]
+    ids = jnp.concatenate([x[:, 0:count] for x in got], axis=1)
+    gates = jnp.concatenate([x[:, 64 : 64 + count] for x in got], axis=1)
+    return jnp.concatenate([ids, gates], axis=0)
 
 
 def group_masks(g, zs):
@@ -345,47 +362,53 @@
     )(jnp.repeat(owner, rows)[:, None], jnp.repeat(live, rows)[:, None], sent, kv_cache)[0]
 
 
-def half_products(left, w_ref, res, me, cols, send, base):
+def half_products(left, w_ref, res, me, cols, far, near, base):
     mine = pl.multiple_of(me[0] * cols, 128)
     other = pl.multiple_of((1 - me[0]) * cols, 128)
-    send[:, 0:cols] = dot(left, w_ref[:, pl.ds(other, cols)]).astype(BF16)
+    far[...] = dot(left, w_ref[:, pl.ds(other, cols)]).astype(BF16)
     own = dot(left, w_ref[:, pl.ds(mine, cols)]).astype(BF16).astype(F32) + res
     base[...] = own
-    send[:, cols:] = own.astype(BF16)
+    near[...] = own.astype(BF16)
 
 
 def project_prefill(prefill, weight, residual, me_kv):
     rows, cols = residual.shape
     skip = rows - prefill.shape[0]
 
-    def body(me, pre, w_ref, res, send, base, rows_scr):
+    def body(me, pre, w_ref, res, far, near, base, rows_scr):
         rows_scr[0:skip, :] = jnp.zeros((skip, cols), F32)
         rows_scr[skip:, :] = pre[...].astype(F32)
         left = rows_scr[...].astype(BF16)
-        half_products(left, w_ref, res[...].astype(F32), me, cols, send, base)
+        half_products(left, w_ref, res[...].astype(F32), me, cols, far, near, base)
 
     return call(
         body,
-        [((rows, 2 * cols), BF16), ((rows, cols), F32)],
+        [((rows, cols), BF16)] * 2 + [((rows, cols), F32)],
         [pltpu.VMEM((rows, cols), F32)],
         smem=(0,),
     )(me_kv, prefill, weight, residual)
 
 
-def project_decode(pieces, where, sent, weight, me_kv, own_req, head_dim):
+def project_decode(pieces, page_table, pages, sent, weight, me_kv, me_pg, own_req, head_dim):
     groups = sent.shape[0]
     cols = weight.shape[0]
     requests = groups * own_req
-    entries = where.shape[0]
+    entries = page_table.size
     count = len(pieces)
-    total = count * pieces[0].shape[0]
-
-    def body(me, where_ref, w_ref, sent_ref, *refs):
-        send, base, res = refs[count:]
+    high = pieces[0].shape[0]
+    total = count * high
+
+    def body(me, pg, table_ref, w_ref, sent_ref, *refs):
+        far, near, base, res = refs[count:]
         unpack(sent_ref, res, 1, own_req)
         table = jnp.concatenate([ref[...] for ref in refs[:count]], axis=0)
-        pick = (where_ref[...] == iota((entries, total), 1)).astype(BF16)
-        got = dot(pick, table)
+        page = jnp.concatenate(
+            [table_ref[j : j + 1, :] for j in range(entries // requests)], axis=1
+        )
+        away = (page // pages) ^ pg[0]
+        where = ((away % 2) * 2 + away // 2 % 2) * high + away // 4 * pages + page % pages
+        pick = (iota((total, entries), 0) == where).astype(BF16)
+        got = t_dot(pick, table)
         parts = [got[n : n + requests] for n in range(0, entries, requests)]
         sums = [part[:, cols + 128 :] for part in parts]
         tops = [
@@ -404,24 +427,24 @@
         merged = jnp.zeros((requests, cols), F32)
         for n, part in enumerate(parts):
             merged += wide[n * requests : (n + 1) * requests] * part[:, 0:cols]
-        half_products(merged.astype(BF16), w_ref, res[...], me, cols, send, base)
+        half_products(merged.astype(BF16), w_ref, res[...], me, cols, far, near, base)
 
     return call(
         body,
-        [((requests, 2 * cols), BF16), ((requests, cols), F32)],
+        [((requests, cols), BF16)] * 2 + [((requests, cols), F32)],
         [pltpu.VMEM((requests, cols), F32)],
-        smem=(0,),
-    )(me_kv, where, weight, sent, *pieces)
-
-
-def norm_and_pages(base, sent, got, gain, pages):
+        smem=(0, 1),
+    )(me_kv, me_pg, page_table.T, weight, sent, *pieces)
+
+
+def norm_and_pages(base, sent, got_own, got_far, gain, pages):
     rows, cols = base.shape
     count, wide = pages.shape
     lanes = wide * count // rows
 
-    def body(base_ref, sent_ref, got_ref, gain_ref, pages_ref, middle, out):
-        mid = base_ref[...] + got_ref[:, 0:cols].astype(F32)
-        far = got_ref[:, cols:].astype(F32) + sent_ref[:, 0:cols].astype(F32)
+    def body(base_ref, sent_ref, got_ref, far_ref, gain_ref, pages_ref, middle, out):
+        mid = base_ref[...] + got_ref[...].astype(F32)
+        far = far_ref[...].astype(F32) + sent_ref[...].astype(F32)
         squares = jnp.sum(mid * mid + far * far, axis=1, keepdims=True)
         middle[...] = mid
         out[:, 0:cols] = (
@@ -431,7 +454,7 @@
             out[n * count : (n + 1) * count, cols:] = pages_ref[:, n * lanes : (n + 1) * lanes]
 
     return call(body, [((rows, cols), F32), ((rows, cols + lanes), BF16)])(
-        base, sent, got, gain.reshape(1, -1), pages
+        base, sent, got_own, got_far, gain.reshape(1, -1), pages
     )
 
 
@@ -457,12 +480,12 @@
     )(*parts)
 
 
-def first_norm(base, sent, got, gain):
+def first_norm(base, sent, got_own, got_far, gain):
     rows, cols = base.shape
 
-    def body(base_ref, sent_ref, got_ref, gain_ref, middle, normed):
-        mid = base_ref[...] + got_ref[:, 0:cols].astype(F32)
-        far = got_ref[:, cols:].astype(F32) + sent_ref[:, 0:cols].astype(F32)
+    def body(base_ref, sent_ref, got_ref, far_ref, gain_ref, middle, normed):
+        mid = base_ref[...] + got_ref[...].astype(F32)
+        far = far_ref[...].astype(F32) + sent_ref[...].astype(F32)
         squares = jnp.sum(mid * mid + far * far, axis=1, keepdims=True)
         middle[...] = mid
         normed[...] = (
@@ -470,7 +493,7 @@
         ).astype(BF16)
 
     return call(body, [((rows, cols), F32), ((rows, cols), BF16)])(
-        base, sent, got, gain.reshape(1, -1)
+        base, sent, got_own, got_far, gain.reshape(1, -1)
     )
 
 
@@ -564,18 +587,19 @@
     )(*arrays)
 
 
-def products(xs, w_ref, side, out):
-    half = out.shape[2] // 2
-    for s in range(out.shape[0]):
+def products(xs, w_ref, side, *outs):
+    half = outs[0].shape[2] // 2
+    places = [(out, n) for out in outs for n in range(out.shape[0])]
+    for s, (out, n) in enumerate(places):
         x = xs[s] if len(xs.shape) == 3 else xs[...]
         for k in range(2):
             low = pl.multiple_of(k * 2 * half + side * half, 128)
-            out[s, :, k * half : (k + 1) * half] = dot(x, w_ref[s, :, pl.ds(low, half)]).astype(
+            out[n, :, k * half : (k + 1) * half] = dot(x, w_ref[s, :, pl.ds(low, half)]).astype(
                 out.dtype
             )
 
 
-def gather(groups, which, picks, w, me_kv, me_pg, rows, skip, decode=None):
+def gather(groups, which, picks, w, me_kv, me_pg, rows, skip, parts, decode=None):
     count, slots = len(groups), w.shape[0]
     pieces = len(groups[0])
     cols = w.shape[1]
@@ -585,7 +609,7 @@
     ff = w.shape[2] // 2
 
     def body(me, pg, w_ref, picks_ref, *refs):
-        xs, send = refs[-2:]
+        xs, sends = refs[-1 - len(parts)], refs[-len(parts) :]
         for n, g in enumerate(which):
             x = jnp.concatenate(
                 [ref[...] for ref in refs[n * pieces : (n + 1) * pieces]], axis=0
@@ -607,41 +631,45 @@
             got = dot(picks_ref[g], x).astype(BF16)
             for s in range(slots):
                 xs[s, n * part : (n + 1) * part, :] = got[s * part : (s + 1) * part]
-        products(xs, w_ref, 1 - me[0], send)
+        products(xs, w_ref, 1 - me[0], *sends)
 
     more = [] if decode is None else [decode]
+    high = count * part
     return call(
         body,
-        [((slots, count * part, cols), BF16), ((slots, count * part, ff), BF16)],
+        [((slots, high, cols), BF16)] + [((n, high, ff), BF16) for n in parts],
         smem=(0, 1),
     )(me_kv, me_pg, w, picks, *[x for group in groups for x in group], *more)
 
 
-def pick_decode(normed, w, me_kv, me_pg, skip, zs):
-    slots = w.shape[0]
+def pick_decode(normed, w, me_pg, skip, zs):
+    slots, _, wide = w.shape
     total, cols = normed.shape
     masks = group_masks(0, zs) + group_masks(2, zs)
     rows = len(masks) * skip
 
-    def body(me, pg, w_ref, x_ref, xs, send):
+    def body(pg, w_ref, x_ref, own, send):
         row = iota((rows, total), 0)
         source = jnp.zeros((rows, total), jnp.int32)
         for n, mask in enumerate(masks):
             source = jnp.where(row // skip == n, (pg[0] ^ mask) * skip, source)
         put = iota((rows, total), 1) == source + row % skip
-        xs[...] = dot(put.astype(BF16), x_ref[...]).astype(BF16)
-        products(xs, w_ref, 1 - me[0], send)
-
-    return call(
-        body, [((rows, cols), BF16), ((slots, rows, w.shape[2] // 2), BF16)], smem=(0, 1)
-    )(me_kv, me_pg, w, normed)
-
-
-def own_products(xs, w, me_kv):
+        x = dot(put.astype(BF16), x_ref[...]).astype(BF16)
+        for s in range(slots):
+            made = dot(x, w_ref[s])
+            own[s] = made
+            send[s] = made.astype(BF16)
+
+    return call(body, [((slots, rows, wide), F32), ((slots, rows, wide), BF16)], smem=(0,))(
+        me_pg, w, normed
+    )
+
+
+def own_products(xs, w, me_kv, flops=1):
     def body(me, w_ref, x_ref, out):
         products(x_ref, w_ref, me[0], out)
 
-    return call(body, [((w.shape[0], xs.shape[-2], w.shape[2] // 2), F32)], smem=(0,))(
+    return call(body, [((w.shape[0], xs.shape[-2], w.shape[2] // 2), F32)], smem=(0,), flops=flops)(
         me_kv, w, xs
     )[0]
 
@@ -650,12 +678,14 @@
     slots, rows, ff = own.shape
     half = ff // 2
 
-    def body(own_ref, got_ref, out):
-        gate = own_ref[:, :, 0:half] + got_ref[:, :, 0:half].astype(F32)
-        up = own_ref[:, :, half:] + got_ref[:, :, half:].astype(F32)
-        out[...] = (gate / (1.0 + jnp.exp(-gate)) * up).astype(BF16)
-
-    return call(body, [((slots, rows, half), BF16)])(own, got)[0]
+    def body(own_ref, *refs):
+        places = [(ref, n) for ref in refs[:-1] for n in range(ref.shape[0])]
+        for s, (ref, n) in enumerate(places):
+            gate = own_ref[s, :, 0:half] + ref[n, :, 0:half].astype(F32)
+            up = own_ref[s, :, half:] + ref[n, :, half:].astype(F32)
+            refs[-1][s] = (gate / (1.0 + jnp.exp(-gate)) * up).astype(BF16)
+
+    return call(body, [((slots, rows, half), BF16)], flops=1)(own, *got)[0]
 
 
 def outputs(near_ref, far_ref, w_ref, me, s):
@@ -664,19 +694,22 @@
     return made + dot(far_ref[s], w_ref[s, pl.ds(pl.multiple_of((1 - me) * half, 128), half), :])
 
 
-def down_decode(near, far, w_down, gates, me_kv):
-    slots, rows, _ = near.shape
+def decode_experts(own, got, w_down, gates):
+    slots, rows, wide = own.shape
     cols = w_down.shape[2]
-
-    def body(me, w_ref, near_ref, far_ref, gates_ref, out):
+    half = wide // 2
+
+    def body(w_ref, own_ref, got_ref, gates_ref, out):
         total = jnp.zeros((rows, cols), F32)
         for s in range(slots):
-            made = outputs(near_ref, far_ref, w_ref, me[0], s)
-            gate = gates_ref[s * rows : (s + 1) * rows, 0:1]
-            total = total + made.astype(BF16).astype(F32) * gate
+            units = own_ref[s] + got_ref[s].astype(F32)
+            gate, up = units[:, 0:half], units[:, half:]
+            hidden = (gate / (1.0 + jnp.exp(-gate)) * up).astype(BF16)
+            made = dot(hidden, w_ref[s]).astype(BF16).astype(F32)
+            total = total + made * gates_ref[s * rows : (s + 1) * rows, 0:1]
         out[...] = total
 
-    return call(body, [((rows, cols), F32)], smem=(0,))(me_kv, w_down, near, far, gates)[0]
+    return call(body, [((rows, cols), F32)], flops=1)(w_down, own, got, gates)[0]
 
 
 def down(near, far, w_down, which, picks, gates, me_kv, rows, skip, decode=None):
@@ -687,7 +720,7 @@
     blocks = part // CAP
 
     def body(me, w_ref, near_ref, far_ref, picks_ref, gates_ref, *refs):
-        outs = refs[-count:]
+        outs = refs[-3:]
         made = [outputs(near_ref, far_ref, w_ref, me[0], s) for s in range(slots)]
         for n, g in enumerate(which):
             parts = jnp.concatenate(
@@ -695,33 +728,39 @@
             )
             parts = (parts * gates_ref[g, :, 0:1]).astype(BF16)
             total = t_dot(picks_ref[g], parts)
-            outs[n][...] = total.astype(BF16)
-            if decode is None:
-                continue
             for b in range(blocks):
+                out, low = outs[n + b * 2 // blocks if n else 0], b * rows
+                low = low % out.shape[0]
+                block = total[b * rows : (b + 1) * rows]
+                out[low : low + rows, :] = block.astype(BF16)
+                if decode is None:
+                    continue
                 late = (n * blocks + b) * skip
-                late = jnp.concatenate(
-                    [refs[0][late : late + skip, :], total[b * rows + skip : b * rows + 16]], axis=0
-                )
-                outs[n][b * rows : b * rows + 16, :] = late.astype(BF16)
+                late = jnp.concatenate([refs[0][late : late + skip, :], block[skip:16]], axis=0)
+                out[low : low + 16, :] = late.astype(BF16)
 
     more = [] if decode is None else [decode]
-    return call(body, [((blocks * rows, cols), BF16)] * count, smem=(0,))(
+    shapes = [((blocks * rows, cols), BF16)] + [((blocks // 2 * rows, cols), BF16)] * 2
+    return call(body, shapes, smem=(0,), flops=1)(
         me_kv, w_down, near, far, picks, gates, *more
     )
 
 
-def split_sum(a, b, blocks, first=BF16):
-    tokens, cols = a.shape
-    high = tokens // blocks
-
-    def body(a_ref, b_ref, *outs):
-        for n in range(blocks):
-            part = slice(n * high, (n + 1) * high)
-            total = a_ref[part, :].astype(F32) + b_ref[part, :].astype(F32)
-            outs[n][...] = total.astype(outs[n].dtype)
-
-    return call(body, [((high, cols), first)] + [((high, cols), BF16)] * (blocks - 1))(a, b)
+def split_sum(kept, halves, rows, first=BF16):
+    cols = kept.shape[1]
+    high = halves[0].shape[0]
+    count = kept.shape[0] // rows
+
+    def body(kept_ref, *refs):
+        for n in range(count):
+            low = n * rows
+            more = refs[low // high][low % high : low % high + rows, :]
+            total = kept_ref[low : low + rows, :].astype(F32) + more.astype(F32)
+            refs[2 + n][...] = total.astype(refs[2 + n].dtype)
+
+    return call(
+        body, [((rows, cols), first)] + [((rows, cols), BF16)] * (count - 1), flops=1
+    )(kept, *halves)
 
 
 def line_base(middle, decode_middle, own, parts, me_pg, skip):
@@ -810,7 +849,9 @@
 
     packed = pack(queries, residual_in, expert_ids, route_weight, n_pg)
     sent = lax.all_to_all(packed, "pg", split_axis=0, concat_axis=0, tiled=True)
-    send, base = project_prefill(after(prefill_attn, packed), out_weight, residual_in, me_kv)
+    send, near, base = project_prefill(
+        after(prefill_attn, packed), out_weight, residual_in, me_kv
+    )
 
     mine = me * slots + jnp.arange(slots, dtype=jnp.int32)
     expert = jnp.arange(slot_table.shape[0], dtype=jnp.int32)
@@ -834,61 +875,60 @@
     )
     live = owner_len - found % max_pages * page_len
     partial = page_attention(sent, kv_cache, owner, live, own_req, cols)
-    middle, payload = norm_and_pages(
-        base, send, after(swap_kv(send), partial), norm_gain_in, partial
-    )
+    got, far = after([swap_kv(send), swap_kv(near)], partial)
+    middle, payload = norm_and_pages(base, send, got, far, norm_gain_in, partial)
     line = [swap_pg(payload, 4 * z, n_pg) for z in range(1, zs)]
     picks, gates, dec_gates = plan(
         after(sent, payload), first, top, experts, me_pg, slots, rows, own_req, zs
     )
     w_units, w_rows = load(after([w_gate_up, w_down], picks))
+
+    def swap_each(arrays, mask):
+        return [swap_pg(x, mask, n_pg) for x in arrays]
+
+    def swap_units(arrays):
+        return [swap_kv(x) for x in arrays]
+
+    def gathered(which, groups, parts, decode=None):
+        return gather(groups, which, picks, w_units, me_kv, me_pg, rows, own_req, parts, decode)
+
     *near, near_pages = join([payload] + after(line, w_units), cols, pages)
     across_pages = swap_pg(near_pages, 2, n_pg)
+    across = swap_each(near, 2)
     near_pages_core = swap_pg(near_pages, 1, n_pg)
-
-    def swap_halves(halves, mask):
-        return [swap_pg(x, mask, n_pg) for x in halves]
-
-    def gathered(which, groups, decode=None):
-        return gather(groups, which, picks, w_units, me_kv, me_pg, rows, own_req, decode)
-
-    xs0, out0 = gathered([0, 2], [near, swap_halves(near, 1)])
-    got0 = swap_kv(out0)
-    across = swap_halves(near, 2)
-    across_pages = after(across_pages, out0)
+    xs0, *out0 = gathered([0, 2], [near, swap_each(near, 1)], (slots,))
+    got0 = swap_units(out0)
+    own0 = own_products(xs0, w_units, me_kv)
+    across_pages = after(across_pages, own0)
     pieces = [near_pages, across_pages, near_pages_core, swap_pg(across_pages, 1, n_pg)]
-    away = (page_table.T // pages) ^ me
-    where = ((away % 2) * 2 + away // 2 % 2) * zs + away // 4
-    where = (where * pages + page_table.T % pages).reshape(-1, 1)
-    dec_send, dec_base = project_decode(
-        pieces, where, sent, out_weight, me_kv, own_req, head_dim
-    )
-    dec_got = swap_kv(dec_send)
-    across = after(across, dec_send)
-    across_core = swap_halves(across, 1)
-    near0 = activate(own_products(xs0, w_units, me_kv), after(got0, across))
+    dec_send, dec_near, dec_base = project_decode(
+        pieces, page_table, pages, sent, out_weight, me_kv, me_pg, own_req, head_dim
+    )
+    dec_got, dec_far = swap_kv(dec_send), swap_kv(dec_near)
+    near0 = activate(own0, after(got0, dec_send))
     far0 = swap_kv(near0)
-    dec_middle, dec_normed = first_norm(dec_base, dec_send, after(dec_got, near0), norm_gain_in)
-    xs2, out2 = pick_decode(dec_normed, w_units, me_kv, me_pg, own_req, zs)
-    got2 = swap_kv(out2)
-    xs1, out1 = gathered([1, 3], after([across, across_core], out2), dec_normed)
-    got1 = swap_kv(out1)
+    across = after(across, near0)
+    across_core = swap_each(across, 1)
+    dec_got, dec_far = after([dec_got, dec_far], across)
+    dec_middle, dec_normed = first_norm(dec_base, dec_send, dec_got, dec_far, norm_gain_in)
+    dec_own, dec_units = pick_decode(dec_normed, w_units, me_pg, own_req, zs)
+    dec_got = swap_kv(dec_units)
+    xs1, *out1 = gathered([1, 3], after([across, across_core], [dec_units, far0]), (slots - 1, 1), dec_normed)
+    got1 = swap_units(out1)
     own1 = own_products(xs1, w_units, me_kv)
-    own2 = own_products(xs2, w_units, me_kv)
-    near2 = activate(own2, after(got2, out1))
-    far2 = swap_kv(near2)
-    decode = down_decode(near2, after(far2, far0), w_rows, dec_gates, me_kv)
-    keep0, give0 = down(
-        near0, far0, w_rows, [0, 2], picks, gates, me_kv, rows, own_req, decode
-    )
-    back0 = swap_pg(give0, 1, n_pg)
-    near1 = activate(own1, after(got1, give0))
+    decode = decode_experts(dec_own, after(dec_got, out1), w_rows, dec_gates)
+    keep0, *give0 = down(
+        near0, after(far0, decode), w_rows, [0, 2], picks, gates, me_kv, rows, own_req, decode
+    )
+    parts0 = split_sum(keep0, swap_each(give0, 1), rows, F32)
+    lines0 = [swap_pg(parts0[z], 4 * z, n_pg) for z in range(1, zs)]
+    near1 = activate(own1, after(got1, parts0))
     far1 = swap_kv(near1)
-    parts0 = split_sum(keep0, after(back0, near1), zs, F32)
-    lines0 = [swap_pg(parts0[z], 4 * z, n_pg) for z in range(1, zs)]
-    base = line_base(middle, dec_middle, parts0[0], lines0, me_pg, own_req)
-    keep1, give1 = down(near1, after(far1, base), w_rows, [1, 3], picks, gates, me_kv, rows, own_req)
-    parts1 = split_sum(keep1, swap_pg(give1, 1, n_pg), zs)
+    base = line_base(middle, dec_middle, parts0[0], after(lines0, near1), me_pg, own_req)
+    keep1, *give1 = down(
+        near1, after(far1, base), w_rows, [1, 3], picks, gates, me_kv, rows, own_req
+    )
+    parts1 = split_sum(keep1, swap_each(give1, 1), rows)
     mixed, squares = close(base, [swap_pg(parts1[z], 4 * z + 2, n_pg) for z in range(zs)])
     return last_norm(mixed, squares, swap_kv(squares), norm_gain_out)
 

time: 122 us -> 104 us (0.85)
  local copies, waits for them, and re-layouts: 18.3 us -> 2.36 us
  starting transfers between devices: 36.6 us -> 43 us
  Pallas kernels: 22.4 us -> 16.3 us
    unnamed x63 -> x23, local copies, waits for them, and re-layouts: 17.6 us -> 1.81 us
    pallas_call x26 -> x24, Pallas kernels: 22.4 us -> 16.3 us  [run(): pl.pallas_call(body, out_shape=[jax.ShapeDtypeStruct(s, d) for s, d in ou...]
    ppermute x9 -> x11, starting transfers between devices: 8.83 us -> 14.1 us  [swap_kv(): return lax.ppermute(x, 'kv', [(0, 1), (1, 0)])]
    ppermute x21 -> x23, starting transfers between devices: 20.3 us -> 21.4 us  [swap_pg(): return lax.ppermute(x, 'pg', [(i, i ^ mask) for i in range(n)])]
    ppermute x9 -> x11, waiting for transfers between devices: 14.4 us -> 13.7 us  [swap_kv(): return lax.ppermute(x, 'kv', [(0, 1), (1, 0)])]
    ppermute x21 -> x23, waiting for transfers between devices: 23.8 us -> 23.9 us  [swap_pg(): return lax.ppermute(x, 'pg', [(i, i ^ mask) for i in range(n)])]
  transfers between devices with their start and end apart: 31 -> 35, of which waited for: 15 -> 18; matrix products, arithmetic and copies ran while one was open for 1% -> 1% of each run, Pallas kernels for 15% -> 12%
where the time goes in v3:
time: 104 us
  starting transfers between devices  43 us (41%)
  waiting for transfers between devices  41.5 us (40%)
  Pallas kernels  16.3 us (16%)
  local copies, waits for them, and re-layouts  2.36 us (2%)
    ppermute x23, waiting for transfers between devices, swap_pg(): return lax.ppermute(x, 'pg', [(i, i ^ mask) for i in range(n)])  23.9 us
    ppermute x23, starting transfers between devices, swap_pg(): return lax.ppermute(x, 'pg', [(i, i ^ mask) for i in range(n)])  21.4 us
    pallas_call x24, Pallas kernels, run(): pl.pallas_call(body, out_shape=[jax.ShapeDtypeStruct(s, d) for s, d in ou...  16.3 us
    ppermute x11, starting transfers between devices, swap_kv(): return lax.ppermute(x, 'kv', [(0, 1), (1, 0)])  14.1 us
    ppermute x11, waiting for transfers between devices, swap_kv(): return lax.ppermute(x, 'kv', [(0, 1), (1, 0)])  13.7 us
    all_to_all x1, starting transfers between devices, fast_local(): sent = lax.all_to_all(packed, 'pg', split_axis=0, concat_axis=0, tiled=True)  7.53 us
    all_to_all x1, waiting for transfers between devices, fast_local(): sent = lax.all_to_all(packed, 'pg', split_axis=0, concat_axis=0, tiled=True)  3.86 us
  transfers between devices with their start and end apart: 35, of which 18 were waited for; matrix products, arithmetic and copies ran while one was open for 1% of the time, Pallas kernels for 12%

profile of v3, /device:TPU:0, one launch (start us, length us, event | category | flops | bytes accessed | tf_op | source)
XLA Modules:
  0.0 104.1 jit_solution(17765099134137266126)
XLA Ops:
  0.0 1.6 %shard_map.136 = bf16[16,56,128]{2,1,0:T(8,128)(2,1)} custom-call(bf16[4,768]{1,0:T(4,128)(2,1)} %q_hbm.1, bf16[64,768]{1,0:T(8,128)(2,1)} %res.1, s32[8,64]{1,0:T(8,128)} %bitcast.6, f32[8,64]{1,0:T(8,128)} %bitcast.7), custom_call_target="tpu_custom_call" | custom-call | flops 1000000000 | bytes 1 | tf_op jit(solution)/shard_map/pallas_call | solution.py:202
  1.7 7.5 %all-to-all-start = ((bf16[16,56,128]{2,1,0:T(8,128)(2,1)}), bf16[16,56,128]{2,1,0:T(8,128)(2,1)S(1)}, u32[]{:S(2)}, u32[]{:S(2)}) async-start(bf16[16,56,128]{2,1,0:T(8,128)(2,1)} %shard_map.136), calls=%async_computation | async-start | bytes 458752 | tf_op jit(solution)/shard_map/all_to_all | solution.py:851
  9.2 1.7 %copy-done.2 = bf16[768,1536]{1,0:T(8,128)(2,1)S(1)} copy-done((bf16[768,1536]{1,0:T(8,128)(2,1)S(1)}, bf16[768,1536]{1,0:T(8,128)(2,1)}, u32[]{:S(2)}) %copy-start.2) | copy-done | bytes 2359320
  14.9 3.9 %all-to-all-done.sent_ref = bf16[16,56,128]{2,1,0:T(8,128)(2,1)S(1)} async-done(((bf16[16,56,128]{2,1,0:T(8,128)(2,1)}), bf16[16,56,128]{2,1,0:T(8,128)(2,1)S(1)}, u32[]{:S(2)}, u32[]{:S(2)}) %all-to-all-start) | async-done | bytes 229408 | tf_op jit(solution)/shard_map/all_to_all | solution.py:851
  18.7 1.7 %shard_map.138.pages_ref = bf16[16,1024]{1,0:T(8,128)(2,1)S(1)} custom-call(s32[256,1]{1,0:T(8,128)S(1)} %broadcast_in_dim_reshape.9.owner_col, s32[256,1]{1,0:T(8,128)S(1)} %broadcast_in_dim_reshape.10.live_col, bf16[16,56,128]{2,1,0:T(8,128)(2,1)S(1)} %all-to-all-done.sent_ref, bf16[16,4,128,128]{3,2,1,0:T(8,128)(2,1)S(1)} %copy-done.4), custom_call_target="tpu_custom_call" | custom-call | flops 1000000000 | bytes 1 | tf_op jit(solution)/shard_map/pallas_call | solution.py:202
  20.6 2.3 %collective-permute-start.3 = (bf16[64,1024]{1,0:T(8,128)(2,1)S(1)}, bf16[64,1024]{1,0:T(8,128)(2,1)S(1)}, u32[]{:S(2)}, u32[]{:S(2)}) collective-permute-start(bf16[64,1024]{1,0:T(8,128)(2,1)S(1)} %get-tuple-element.80.refs_0_), channel_id=1, source_target_pairs={{0,8},{1,9},{2,10},{3,11},{4,12},{5,13},{6,14},{7,15},{8,0},{9,1},... | collective-permute-start | bytes 393224 | tf_op jit(solution)/shard_map/ppermute | solution.py:242
  23.0 2.0 %collective-permute-start.4 = (bf16[64,1024]{1,0:T(8,128)(2,1)S(1)}, bf16[64,1024]{1,0:T(8,128)(2,1)S(1)}, u32[]{:S(2)}, u32[]{:S(2)}) collective-permute-start(bf16[64,1024]{1,0:T(8,128)(2,1)S(1)} %get-tuple-element.80.refs_0_), channel_id=1, source_target_pairs={{0,12},{1,13},{2,14},{3,15},{4,8},{5,9},{6,10},{7,11},{8,4},{9,5},... | collective-permute-start | bytes 393224 | tf_op jit(solution)/shard_map/ppermute | solution.py:242
  26.0 2.4 %shard_map.141 = (bf16[3,768,1024]{2,1,0:T(8,128)(2,1)S(1)}, bf16[3,512,768]{2,1,0:T(8,128)(2,1)S(1)}) custom-call(bf16[3,768,1024]{2,1,0:T(8,128)(2,1)} %refs_0_, bf16[3,512,768]{2,1,0:T(8,128)(2,1)S(1)} %copy-done), custom_call_target="tpu_custom_call" | custom-call | flops 1000000000 | bytes 1 | tf_op jit(solution)/shard_map/pallas_call | solution.py:202
  28.4 5.1 %collective-permute-done.3.refs_2_ = bf16[64,1024]{1,0:T(8,128)(2,1)S(1)} collective-permute-done((bf16[64,1024]{1,0:T(8,128)(2,1)S(1)}, bf16[64,1024]{1,0:T(8,128)(2,1)S(1)}, u32[]{:S(2)}, u32[]{:S(2)}) %collective-permute-start.3) | collective-permute-done | bytes 131104 | tf_op jit(solution)/shard_map/ppermute | solution.py:242
  36.1 1.6 %collective-permute-start.14 = (bf16[3,128,512]{2,1,0:T(8,128)(2,1)S(1)}, bf16[3,128,512]{2,1,0:T(8,128)(2,1)S(1)}, u32[]{:S(2)}, u32[]{:S(2)}) collective-permute-start(bf16[3,128,512]{2,1,0:T(8,128)(2,1)S(1)} %get-tuple-element.97), channel_id=1, source_target_pairs={{0,16},{16,0},{1,17},{17,1},{2,18},{18,2},{3,19},{19,3},{4,20},{20... | collective-permute-start | bytes 1179656 | tf_op jit(solution)/shard_map/ppermute | solution.py:238
  43.1 1.6 %collective-permute-start.10 = (bf16[64,768]{1,0:T(8,128)(2,1)S(1)}, bf16[64,768]{1,0:T(8,128)(2,1)S(1)}, u32[]{:S(2)}, u32[]{:S(2)}) collective-permute-start(bf16[64,768]{1,0:T(8,128)(2,1)S(1)} %get-tuple-element.95.sent_ref), channel_id=1, source_target_pairs={{0,16},{16,0},{1,17},{17,1},{2,18},{18,2},{3,19},{19,3},{4,20},{20... | collective-permute-start | bytes 294920 | tf_op jit(solution)/shard_map/ppermute | solution.py:238
  45.2 2.9 %collective-permute-done.14.refs_0_ = bf16[3,128,512]{2,1,0:T(8,128)(2,1)S(1)} collective-permute-done((bf16[3,128,512]{2,1,0:T(8,128)(2,1)S(1)}, bf16[3,128,512]{2,1,0:T(8,128)(2,1)S(1)}, u32[]{:S(2)}, u32[]{:S(2)}) %collective-permute-start.14) | collective-permute-done | bytes 393248 | tf_op jit(solution)/shard_map/ppermute | solution.py:238
  48.3 1.6 %collective-permute-start.15 = (bf16[3,128,256]{2,1,0:T(8,128)(2,1)S(1)}, bf16[3,128,256]{2,1,0:T(8,128)(2,1)S(1)}, u32[]{:S(2)}, u32[]{:S(2)}) collective-permute-start(bf16[3,128,256]{2,1,0:T(8,128)(2,1)S(1)} %shard_map.146.near_ref), channel_id=1, source_target_pairs={{0,16},{16,0},{1,17},{17,1},{2,18},{18,2},{3,19},{19,3},{4,20},{20... | collective-permute-start | bytes 589832 | tf_op jit(solution)/shard_map/ppermute | solution.py:238
  57.1 1.6 %collective-permute-start.24 = (bf16[2,128,512]{2,1,0:T(8,128)(2,1)S(1)}, bf16[2,128,512]{2,1,0:T(8,128)(2,1)S(1)}, u32[]{:S(2)}, u32[]{:S(2)}) collective-permute-start(bf16[2,128,512]{2,1,0:T(8,128)(2,1)S(1)} %get-tuple-element.112), channel_id=1, source_target_pairs={{0,16},{16,0},{1,17},{17,1},{2,18},{18,2},{3,19},{19,3},{4,20},{20... | collective-permute-start | bytes 786440 | tf_op jit(solution)/shard_map/ppermute | solution.py:238
  58.7 2.4 %collective-permute-done.16.got_ref = bf16[3,32,1024]{2,1,0:T(8,128)(2,1)S(1)} collective-permute-done((bf16[3,32,1024]{2,1,0:T(8,128)(2,1)S(1)}, bf16[3,32,1024]{2,1,0:T(8,128)(2,1)S(1)}, u32[]{:S(2)}, u32[]{:S(2)}) %collective-permute-start.16) | collective-permute-done | bytes 196640 | tf_op jit(solution)/shard_map/ppermute | solution.py:238
  65.1 3.4 %collective-permute-done.25.refs_1_ = bf16[1,128,512]{2,1,0:T(8,128)(2,1)S(1)} collective-permute-done((bf16[1,128,512]{2,1,0:T(8,128)(2,1)S(1)}, bf16[1,128,512]{2,1,0:T(8,128)(2,1)S(1)}, u32[]{:S(2)}, u32[]{:S(2)}) %collective-permute-start.25) | collective-permute-done | bytes 131104 | tf_op jit(solution)/shard_map/ppermute | solution.py:238
  68.6 1.6 %collective-permute-start.26 = (bf16[3,128,256]{2,1,0:T(8,128)(2,1)S(1)}, bf16[3,128,256]{2,1,0:T(8,128)(2,1)S(1)}, u32[]{:S(2)}, u32[]{:S(2)}) collective-permute-start(bf16[3,128,256]{2,1,0:T(8,128)(2,1)S(1)} %shard_map.154.near_ref), channel_id=1, source_target_pairs={{0,16},{16,0},{1,17},{17,1},{2,18},{18,2},{3,19},{19,3},{4,20},{20... | collective-permute-start | bytes 589832 | tf_op jit(solution)/shard_map/ppermute | solution.py:238
  70.2 2.6 %collective-permute-start.21 = (bf16[64,768]{1,0:T(8,128)(2,1)S(1)}, bf16[64,768]{1,0:T(8,128)(2,1)S(1)}, u32[]{:S(2)}, u32[]{:S(2)}) collective-permute-start(bf16[64,768]{1,0:T(8,128)(2,1)S(1)} %get-tuple-element.122), channel_id=1, source_target_pairs={{0,4},{1,5},{2,6},{3,7},{4,0},{5,1},{6,2},{7,3},{8,12},{9,13},{10,... | collective-permute-start | bytes 294920 | tf_op jit(solution)/shard_map/ppermute | solution.py:242
  72.8 2.4 %collective-permute-start.23 = (bf16[64,768]{1,0:T(8,128)(2,1)S(1)}, bf16[64,768]{1,0:T(8,128)(2,1)S(1)}, u32[]{:S(2)}, u32[]{:S(2)}) collective-permute-start(bf16[64,768]{1,0:T(8,128)(2,1)S(1)} %get-tuple-element.124), channel_id=1, source_target_pairs={{0,12},{1,13},{2,14},{3,15},{4,8},{5,9},{6,10},{7,11},{8,4},{9,5},... | collective-permute-start | bytes 294920 | tf_op jit(solution)/shard_map/ppermute | solution.py:242
  76.1 5.8 %collective-permute-done.22.refs_2_ = bf16[64,768]{1,0:T(8,128)(2,1)S(1)} collective-permute-done((bf16[64,768]{1,0:T(8,128)(2,1)S(1)}, bf16[64,768]{1,0:T(8,128)(2,1)S(1)}, u32[]{:S(2)}, u32[]{:S(2)}) %collective-permute-start.22) | collective-permute-done | bytes 98336 | tf_op jit(solution)/shard_map/ppermute | solution.py:242
  86.0 2.3 %collective-permute-start.30 = (bf16[64,768]{1,0:T(8,128)(2,1)S(1)}, bf16[64,768]{1,0:T(8,128)(2,1)S(1)}, u32[]{:S(2)}, u32[]{:S(2)}) collective-permute-start(bf16[64,768]{1,0:T(8,128)(2,1)S(1)} %get-tuple-element.136), channel_id=1, source_target_pairs={{0,6},{1,7},{2,4},{3,5},{4,2},{5,3},{6,0},{7,1},{8,14},{9,15},{10,... | collective-permute-start | bytes 294920 | tf_op jit(solution)/shard_map/ppermute | solution.py:242
  89.4 2.3 %collective-permute-start.32 = (bf16[64,768]{1,0:T(8,128)(2,1)S(1)}, bf16[64,768]{1,0:T(8,128)(2,1)S(1)}, u32[]{:S(2)}, u32[]{:S(2)}) collective-permute-start(bf16[64,768]{1,0:T(8,128)(2,1)S(1)} %get-tuple-element.138), channel_id=1, source_target_pairs={{0,14},{1,15},{2,12},{3,13},{4,10},{5,11},{6,8},{7,9},{8,6},{9,7},... | collective-permute-start | bytes 294920 | tf_op jit(solution)/shard_map/ppermute | solution.py:242
  92.0 7.3 %collective-permute-done.31.refs_2_ = bf16[64,768]{1,0:T(8,128)(2,1)S(1)} collective-permute-done((bf16[64,768]{1,0:T(8,128)(2,1)S(1)}, bf16[64,768]{1,0:T(8,128)(2,1)S(1)}, u32[]{:S(2)}, u32[]{:S(2)}) %collective-permute-start.31) | collective-permute-done | bytes 98336 | tf_op jit(solution)/shard_map/ppermute | solution.py:242
  100.0 3.4 %collective-permute-done.33.far_ref = f32[64,128]{1,0:T(8,128)S(1)} collective-permute-done((f32[64,128]{1,0:T(8,128)S(1)}, f32[64,128]{1,0:T(8,128)S(1)}, u32[]{:S(2)}, u32[]{:S(2)}) %collective-permute-start.33) | collective-permute-done | bytes 32800 | tf_op jit(solution)/shard_map/ppermute | solution.py:238
  (108 shorter events, 33.0 us)
Async XLA Ops:
  1.7 17.1 %all-to-all-start = ((bf16[16,56,128]{2,1,0:T(8,128)(2,1)}), bf16[16,56,128]{2,1,0:T(8,128)(2,1)S(1)}, u32[]{:S(2)}, u32[]{:S(2)}) async-start(bf16[16,56,128]{2,1,0:T(8,128)(2,1)} %shard_map.136), calls=%async_computation | async-start | bytes 458752 | tf_op jit(solution)/shard_map/all_to_all | solution.py:851
  11.4 8.9 %collective-permute-start = (bf16[64,768]{1,0:T(8,128)(2,1)S(1)}, bf16[64,768]{1,0:T(8,128)(2,1)S(1)}, u32[]{:S(2)}, u32[]{:S(2)}) collective-permute-start(bf16[64,768]{1,0:T(8,128)(2,1)S(1)} %get-tuple-element.75.sent_ref), channel_id=1, source_target_pairs={{0,16},{16,0},{1,17},{17,1},{2,18},{18,2},{3,19},{19,3},{4,20},{20... | collective-permute-start | bytes 294920 | tf_op jit(solution)/shard_map/ppermute | solution.py:238
  13.0 7.4 %collective-permute-start.1 = (bf16[64,768]{1,0:T(8,128)(2,1)S(1)}, bf16[64,768]{1,0:T(8,128)(2,1)S(1)}, u32[]{:S(2)}, u32[]{:S(2)}) collective-permute-start(bf16[64,768]{1,0:T(8,128)(2,1)S(1)} %get-tuple-element.76), channel_id=1, source_target_pairs={{0,16},{16,0},{1,17},{17,1},{2,18},{18,2},{3,19},{19,3},{4,20},{20... | collective-permute-start | bytes 294920 | tf_op jit(solution)/shard_map/ppermute | solution.py:238
  20.6 7.9 %collective-permute-start.2 = (bf16[64,1024]{1,0:T(8,128)(2,1)S(1)}, bf16[64,1024]{1,0:T(8,128)(2,1)S(1)}, u32[]{:S(2)}, u32[]{:S(2)}) collective-permute-start(bf16[64,1024]{1,0:T(8,128)(2,1)S(1)} %get-tuple-element.80.refs_0_), channel_id=1, source_target_pairs={{0,4},{1,5},{2,6},{3,7},{4,0},{5,1},{6,2},{7,3},{8,12},{9,13},{10,... | collective-permute-start | bytes 393224 | tf_op jit(solution)/shard_map/ppermute | solution.py:242
  20.6 12.9 %collective-permute-start.3 = (bf16[64,1024]{1,0:T(8,128)(2,1)S(1)}, bf16[64,1024]{1,0:T(8,128)(2,1)S(1)}, u32[]{:S(2)}, u32[]{:S(2)}) collective-permute-start(bf16[64,1024]{1,0:T(8,128)(2,1)S(1)} %get-tuple-element.80.refs_0_), channel_id=1, source_target_pairs={{0,8},{1,9},{2,10},{3,11},{4,12},{5,13},{6,14},{7,15},{8,0},{9,1},... | collective-permute-start | bytes 393224 | tf_op jit(solution)/shard_map/ppermute | solution.py:242
  23.0 10.6 %collective-permute-start.4 = (bf16[64,1024]{1,0:T(8,128)(2,1)S(1)}, bf16[64,1024]{1,0:T(8,128)(2,1)S(1)}, u32[]{:S(2)}, u32[]{:S(2)}) collective-permute-start(bf16[64,1024]{1,0:T(8,128)(2,1)S(1)} %get-tuple-element.80.refs_0_), channel_id=1, source_target_pairs={{0,12},{1,13},{2,14},{3,15},{4,8},{5,9},{6,10},{7,11},{8,4},{9,5},... | collective-permute-start | bytes 393224 | tf_op jit(solution)/shard_map/ppermute | solution.py:242
  34.2 5.5 %collective-permute-start.5 = (bf16[64,1024]{1,0:T(8,128)(2,1)S(1)}, bf16[64,1024]{1,0:T(8,128)(2,1)S(1)}, u32[]{:S(2)}, u32[]{:S(2)}) collective-permute-start(bf16[64,1024]{1,0:T(8,128)(2,1)S(1)} %get-tuple-element.89.refs_0_), channel_id=1, source_target_pairs={{0,2},{1,3},{2,0},{3,1},{4,6},{5,7},{6,4},{7,5},{8,10},{9,11},{10,... | collective-permute-start | bytes 393224 | tf_op jit(solution)/shard_map/ppermute | solution.py:242
  36.1 12.0 %collective-permute-start.14 = (bf16[3,128,512]{2,1,0:T(8,128)(2,1)S(1)}, bf16[3,128,512]{2,1,0:T(8,128)(2,1)S(1)}, u32[]{:S(2)}, u32[]{:S(2)}) collective-permute-start(bf16[3,128,512]{2,1,0:T(8,128)(2,1)S(1)} %get-tuple-element.97), channel_id=1, source_target_pairs={{0,16},{16,0},{1,17},{17,1},{2,18},{18,2},{3,19},{19,3},{4,20},{20... | collective-permute-start | bytes 1179656 | tf_op jit(solution)/shard_map/ppermute | solution.py:238
  39.7 10.2 %collective-permute-start.12 = (bf16[128,768]{1,0:T(8,128)(2,1)S(1)}, bf16[128,768]{1,0:T(8,128)(2,1)S(1)}, u32[]{:S(2)}, u32[]{:S(2)}) collective-permute-start(bf16[128,768]{1,0:T(8,128)(2,1)S(1)} %get-tuple-element.90.refs_0_), channel_id=1, source_target_pairs={{0,2},{1,3},{2,0},{3,1},{4,6},{5,7},{6,4},{7,5},{8,10},{9,11},{10,... | collective-permute-start | bytes 589832 | tf_op jit(solution)/shard_map/ppermute | solution.py:242
  40.5 10.7 %collective-permute-start.13 = (bf16[128,768]{1,0:T(8,128)(2,1)S(1)}, bf16[128,768]{1,0:T(8,128)(2,1)S(1)}, u32[]{:S(2)}, u32[]{:S(2)}) collective-permute-start(bf16[128,768]{1,0:T(8,128)(2,1)S(1)} %get-tuple-element.91.refs_1_), channel_id=1, source_target_pairs={{0,2},{1,3},{2,0},{3,1},{4,6},{5,7},{6,4},{7,5},{8,10},{9,11},{10,... | collective-permute-start | bytes 589832 | tf_op jit(solution)/shard_map/ppermute | solution.py:242
  43.1 8.6 %collective-permute-start.10 = (bf16[64,768]{1,0:T(8,128)(2,1)S(1)}, bf16[64,768]{1,0:T(8,128)(2,1)S(1)}, u32[]{:S(2)}, u32[]{:S(2)}) collective-permute-start(bf16[64,768]{1,0:T(8,128)(2,1)S(1)} %get-tuple-element.95.sent_ref), channel_id=1, source_target_pairs={{0,16},{16,0},{1,17},{17,1},{2,18},{18,2},{3,19},{19,3},{4,20},{20... | collective-permute-start | bytes 294920 | tf_op jit(solution)/shard_map/ppermute | solution.py:238
  44.6 7.7 %collective-permute-start.11 = (bf16[64,768]{1,0:T(8,128)(2,1)S(1)}, bf16[64,768]{1,0:T(8,128)(2,1)S(1)}, u32[]{:S(2)}, u32[]{:S(2)}) collective-permute-start(bf16[64,768]{1,0:T(8,128)(2,1)S(1)} %get-tuple-element.96), channel_id=1, source_target_pairs={{0,16},{16,0},{1,17},{17,1},{2,18},{18,2},{3,19},{19,3},{4,20},{20... | collective-permute-start | bytes 294920 | tf_op jit(solution)/shard_map/ppermute | solution.py:238
  48.3 7.8 %collective-permute-start.15 = (bf16[3,128,256]{2,1,0:T(8,128)(2,1)S(1)}, bf16[3,128,256]{2,1,0:T(8,128)(2,1)S(1)}, u32[]{:S(2)}, u32[]{:S(2)}) collective-permute-start(bf16[3,128,256]{2,1,0:T(8,128)(2,1)S(1)} %shard_map.146.near_ref), channel_id=1, source_target_pairs={{0,16},{16,0},{1,17},{17,1},{2,18},{18,2},{3,19},{19,3},{4,20},{20... | collective-permute-start | bytes 589832 | tf_op jit(solution)/shard_map/ppermute | solution.py:238
  53.5 7.6 %collective-permute-start.16 = (bf16[3,32,1024]{2,1,0:T(8,128)(2,1)S(1)}, bf16[3,32,1024]{2,1,0:T(8,128)(2,1)S(1)}, u32[]{:S(2)}, u32[]{:S(2)}) collective-permute-start(bf16[3,32,1024]{2,1,0:T(8,128)(2,1)S(1)} %get-tuple-element.107), channel_id=1, source_target_pairs={{0,16},{16,0},{1,17},{17,1},{2,18},{18,2},{3,19},{19,3},{4,20},{20... | collective-permute-start | bytes 589832 | tf_op jit(solution)/shard_map/ppermute | solution.py:238
  57.1 11.3 %collective-permute-start.24 = (bf16[2,128,512]{2,1,0:T(8,128)(2,1)S(1)}, bf16[2,128,512]{2,1,0:T(8,128)(2,1)S(1)}, u32[]{:S(2)}, u32[]{:S(2)}) collective-permute-start(bf16[2,128,512]{2,1,0:T(8,128)(2,1)S(1)} %get-tuple-element.112), channel_id=1, source_target_pairs={{0,16},{16,0},{1,17},{17,1},{2,18},{18,2},{3,19},{19,3},{4,20},{20... | collective-permute-start | bytes 786440 | tf_op jit(solution)/shard_map/ppermute | solution.py:238
  62.9 5.5 %collective-permute-start.25 = (bf16[1,128,512]{2,1,0:T(8,128)(2,1)S(1)}, bf16[1,128,512]{2,1,0:T(8,128)(2,1)S(1)}, u32[]{:S(2)}, u32[]{:S(2)}) collective-permute-start(bf16[1,128,512]{2,1,0:T(8,128)(2,1)S(1)} %get-tuple-element.113), channel_id=1, source_target_pairs={{0,16},{16,0},{1,17},{17,1},{2,18},{18,2},{3,19},{19,3},{4,20},{20... | collective-permute-start | bytes 393224 | tf_op jit(solution)/shard_map/ppermute | solution.py:238
  68.6 13.5 %collective-permute-start.26 = (bf16[3,128,256]{2,1,0:T(8,128)(2,1)S(1)}, bf16[3,128,256]{2,1,0:T(8,128)(2,1)S(1)}, u32[]{:S(2)}, u32[]{:S(2)}) collective-permute-start(bf16[3,128,256]{2,1,0:T(8,128)(2,1)S(1)} %shard_map.154.near_ref), channel_id=1, source_target_pairs={{0,16},{16,0},{1,17},{17,1},{2,18},{18,2},{3,19},{19,3},{4,20},{20... | collective-permute-start | bytes 589832 | tf_op jit(solution)/shard_map/ppermute | solution.py:238
  70.2 5.9 %collective-permute-start.21 = (bf16[64,768]{1,0:T(8,128)(2,1)S(1)}, bf16[64,768]{1,0:T(8,128)(2,1)S(1)}, u32[]{:S(2)}, u32[]{:S(2)}) collective-permute-start(bf16[64,768]{1,0:T(8,128)(2,1)S(1)} %get-tuple-element.122), channel_id=1, source_target_pairs={{0,4},{1,5},{2,6},{3,7},{4,0},{5,1},{6,2},{7,3},{8,12},{9,13},{10,... | collective-permute-start | bytes 294920 | tf_op jit(solution)/shard_map/ppermute | solution.py:242
  72.8 9.1 %collective-permute-start.22 = (bf16[64,768]{1,0:T(8,128)(2,1)S(1)}, bf16[64,768]{1,0:T(8,128)(2,1)S(1)}, u32[]{:S(2)}, u32[]{:S(2)}) collective-permute-start(bf16[64,768]{1,0:T(8,128)(2,1)S(1)} %get-tuple-element.123), channel_id=1, source_target_pairs={{0,8},{1,9},{2,10},{3,11},{4,12},{5,13},{6,14},{7,15},{8,0},{9,1},... | collective-permute-start | bytes 294920 | tf_op jit(solution)/shard_map/ppermute | solution.py:242
  72.8 9.1 %collective-permute-start.23 = (bf16[64,768]{1,0:T(8,128)(2,1)S(1)}, bf16[64,768]{1,0:T(8,128)(2,1)S(1)}, u32[]{:S(2)}, u32[]{:S(2)}) collective-permute-start(bf16[64,768]{1,0:T(8,128)(2,1)S(1)} %get-tuple-element.124), channel_id=1, source_target_pairs={{0,12},{1,13},{2,14},{3,15},{4,8},{5,9},{6,10},{7,11},{8,4},{9,5},... | collective-permute-start | bytes 294920 | tf_op jit(solution)/shard_map/ppermute | solution.py:242
  84.9 7.1 %collective-permute-start.29 = (bf16[64,768]{1,0:T(8,128)(2,1)S(1)}, bf16[64,768]{1,0:T(8,128)(2,1)S(1)}, u32[]{:S(2)}, u32[]{:S(2)}) collective-permute-start(bf16[64,768]{1,0:T(8,128)(2,1)S(1)} %get-tuple-element.135), channel_id=1, source_target_pairs={{0,2},{1,3},{2,0},{3,1},{4,6},{5,7},{6,4},{7,5},{8,10},{9,11},{10,... | collective-permute-start | bytes 294920 | tf_op jit(solution)/shard_map/ppermute | solution.py:242
  86.0 6.0 %collective-permute-start.30 = (bf16[64,768]{1,0:T(8,128)(2,1)S(1)}, bf16[64,768]{1,0:T(8,128)(2,1)S(1)}, u32[]{:S(2)}, u32[]{:S(2)}) collective-permute-start(bf16[64,768]{1,0:T(8,128)(2,1)S(1)} %get-tuple-element.136), channel_id=1, source_target_pairs={{0,6},{1,7},{2,4},{3,5},{4,2},{5,3},{6,0},{7,1},{8,14},{9,15},{10,... | collective-permute-start | bytes 294920 | tf_op jit(solution)/shard_map/ppermute | solution.py:242
  88.3 11.0 %collective-permute-start.31 = (bf16[64,768]{1,0:T(8,128)(2,1)S(1)}, bf16[64,768]{1,0:T(8,128)(2,1)S(1)}, u32[]{:S(2)}, u32[]{:S(2)}) collective-permute-start(bf16[64,768]{1,0:T(8,128)(2,1)S(1)} %get-tuple-element.137), channel_id=1, source_target_pairs={{0,10},{1,11},{2,8},{3,9},{4,14},{5,15},{6,12},{7,13},{8,2},{9,3},... | collective-permute-start | bytes 294920 | tf_op jit(solution)/shard_map/ppermute | solution.py:242
  89.4 9.8 %collective-permute-start.32 = (bf16[64,768]{1,0:T(8,128)(2,1)S(1)}, bf16[64,768]{1,0:T(8,128)(2,1)S(1)}, u32[]{:S(2)}, u32[]{:S(2)}) collective-permute-start(bf16[64,768]{1,0:T(8,128)(2,1)S(1)} %get-tuple-element.138), channel_id=1, source_target_pairs={{0,14},{1,15},{2,12},{3,13},{4,10},{5,11},{6,8},{7,9},{8,6},{9,7},... | collective-permute-start | bytes 294920 | tf_op jit(solution)/shard_map/ppermute | solution.py:242
  (22 other events, 135.7 us)

commit v4 on v3

--- a/solution.py
+++ b/solution.py
@@ -674,24 +674,33 @@
     )[0]
 
 
-def activate(own, got):
+def activate(own, got, parts=1):
     slots, rows, ff = own.shape
     half = ff // 2
+    high = rows // parts
 
     def body(own_ref, *refs):
-        places = [(ref, n) for ref in refs[:-1] for n in range(ref.shape[0])]
+        places = [(ref, n) for ref in refs[:-parts] for n in range(ref.shape[0])]
         for s, (ref, n) in enumerate(places):
             gate = own_ref[s, :, 0:half] + ref[n, :, 0:half].astype(F32)
             up = own_ref[s, :, half:] + ref[n, :, half:].astype(F32)
-            refs[-1][s] = (gate / (1.0 + jnp.exp(-gate)) * up).astype(BF16)
-
-    return call(body, [((slots, rows, half), BF16)], flops=1)(own, *got)[0]
-
-
-def outputs(near_ref, far_ref, w_ref, me, s):
-    half = near_ref.shape[2]
-    made = dot(near_ref[s], w_ref[s, pl.ds(pl.multiple_of(me * half, 128), half), :])
-    return made + dot(far_ref[s], w_ref[s, pl.ds(pl.multiple_of((1 - me) * half, 128), half), :])
+            hidden = (gate / (1.0 + jnp.exp(-gate)) * up).astype(BF16)
+            for k in range(parts):
+                refs[k - parts][s] = hidden[k * high : (k + 1) * high]
+
+    return call(body, [((slots, high, half), BF16)] * parts, flops=1)(own, *got)
+
+
+def outputs(near, far, w_ref, me, s):
+    half = near[0].shape[2]
+    made = dot(
+        jnp.concatenate([ref[s] for ref in near], axis=0),
+        w_ref[s, pl.ds(pl.multiple_of(me * half, 128), half), :],
+    )
+    return made + dot(
+        jnp.concatenate([ref[s] for ref in far], axis=0),
+        w_ref[s, pl.ds(pl.multiple_of((1 - me) * half, 128), half), :],
+    )
 
 
 def decode_experts(own, got, w_down, gates):
@@ -713,15 +722,18 @@
 
 
 def down(near, far, w_down, which, picks, gates, me_kv, rows, skip, decode=None):
-    slots, total_rows, _ = near.shape
+    pieces = len(near)
+    slots, total_rows, _ = near[0].shape
+    total_rows = total_rows * pieces
     cols = w_down.shape[2]
     count = len(which)
     part = total_rows // count
     blocks = part // CAP
 
-    def body(me, w_ref, near_ref, far_ref, picks_ref, gates_ref, *refs):
+    def body(me, w_ref, picks_ref, gates_ref, *refs):
+        near_refs, far_refs = refs[:pieces], refs[pieces : 2 * pieces]
         outs = refs[-3:]
-        made = [outputs(near_ref, far_ref, w_ref, me[0], s) for s in range(slots)]
+        made = [outputs(near_refs, far_refs, w_ref, me[0], s) for s in range(slots)]
         for n, g in enumerate(which):
             parts = jnp.concatenate(
                 [made[s][n * part : (n + 1) * part] for s in range(slots)], axis=0
@@ -736,17 +748,17 @@
                 if decode is None:
                     continue
                 late = (n * blocks + b) * skip
-                late = jnp.concatenate([refs[0][late : late + skip, :], block[skip:16]], axis=0)
+                late = jnp.concatenate([refs[2 * pieces][late : late + skip, :], block[skip:16]], axis=0)
                 out[low : low + 16, :] = late.astype(BF16)
 
     more = [] if decode is None else [decode]
     shapes = [((blocks * rows, cols), BF16)] + [((blocks // 2 * rows, cols), BF16)] * 2
     return call(body, shapes, smem=(0,), flops=1)(
-        me_kv, w_down, near, far, picks, gates, *more
-    )
-
-
-def split_sum(kept, halves, rows, first=BF16):
+        me_kv, w_down, picks, gates, *near, *far, *more
+    )
+
+
+def split_sum(kept, halves, rows, first=BF16, pad=0):
     cols = kept.shape[1]
     high = halves[0].shape[0]
     count = kept.shape[0] // rows
@@ -756,10 +768,13 @@
             low = n * rows
             more = refs[low // high][low % high : low % high + rows, :]
             total = kept_ref[low : low + rows, :].astype(F32) + more.astype(F32)
-            refs[2 + n][...] = total.astype(refs[2 + n].dtype)
+            out = refs[2 + n]
+            out[0:rows, :] = total.astype(out.dtype)
+            if n and pad:
+                out[rows:, :] = jnp.zeros((pad, cols), out.dtype)
 
     return call(
-        body, [((rows, cols), first)] + [((rows, cols), BF16)] * (count - 1), flops=1
+        body, [((rows, cols), first)] + [((rows + pad, cols), BF16)] * (count - 1), flops=1
     )(kept, *halves)
 
 
@@ -770,7 +785,7 @@
         out = refs[-1]
         total = refs[0][...]
         for ref in refs[1:-1]:
-            total = total + ref[...].astype(F32)
+            total = total + ref[0:rows, :].astype(F32)
         out[...] = total + mid[...]
         put = iota((8, dec.shape[0]), 1) == pg[0] * skip + iota((8, dec.shape[0]), 0)
         put = put & (iota((8, dec.shape[0]), 0) < skip)
@@ -877,7 +892,7 @@
     partial = page_attention(sent, kv_cache, owner, live, own_req, cols)
     got, far = after([swap_kv(send), swap_kv(near)], partial)
     middle, payload = norm_and_pages(base, send, got, far, norm_gain_in, partial)
-    line = [swap_pg(payload, 4 * z, n_pg) for z in range(1, zs)]
+    line = [swap_pg(payload, 4 * z, n_pg) for z in reversed(range(1, zs))][::-1]
     picks, gates, dec_gates = plan(
         after(sent, payload), first, top, experts, me_pg, slots, rows, own_req, zs
     )
@@ -906,30 +921,32 @@
     )
     dec_got, dec_far = swap_kv(dec_send), swap_kv(dec_near)
     near0 = activate(own0, after(got0, dec_send))
-    far0 = swap_kv(near0)
+    far0 = swap_units(near0)
     across = after(across, near0)
     across_core = swap_each(across, 1)
     dec_got, dec_far = after([dec_got, dec_far], across)
     dec_middle, dec_normed = first_norm(dec_base, dec_send, dec_got, dec_far, norm_gain_in)
     dec_own, dec_units = pick_decode(dec_normed, w_units, me_pg, own_req, zs)
     dec_got = swap_kv(dec_units)
-    xs1, *out1 = gathered([1, 3], after([across, across_core], [dec_units, far0]), (slots - 1, 1), dec_normed)
+    xs1, *out1 = gathered([1, 3], after([across, across_core], [dec_units, far0]), (slots,), dec_normed)
     got1 = swap_units(out1)
     own1 = own_products(xs1, w_units, me_kv)
-    decode = decode_experts(dec_own, after(dec_got, out1), w_rows, dec_gates)
+    decode = decode_experts(dec_own, after(dec_got, own1), w_rows, dec_gates)
     keep0, *give0 = down(
         near0, after(far0, decode), w_rows, [0, 2], picks, gates, me_kv, rows, own_req, decode
     )
-    parts0 = split_sum(keep0, swap_each(give0, 1), rows, F32)
-    lines0 = [swap_pg(parts0[z], 4 * z, n_pg) for z in range(1, zs)]
-    near1 = activate(own1, after(got1, parts0))
-    far1 = swap_kv(near1)
+    parts0 = split_sum(keep0, swap_each(give0, 1), rows, F32, 8)
+    lines0 = [swap_pg(parts0[z], 4 * z, n_pg) for z in reversed(range(1, zs))]
+    near1 = activate(own1, after(got1, parts0), 2)
+    far1 = swap_units(near1)
     base = line_base(middle, dec_middle, parts0[0], after(lines0, near1), me_pg, own_req)
     keep1, *give1 = down(
         near1, after(far1, base), w_rows, [1, 3], picks, gates, me_kv, rows, own_req
     )
     parts1 = split_sum(keep1, swap_each(give1, 1), rows)
-    mixed, squares = close(base, [swap_pg(parts1[z], 4 * z + 2, n_pg) for z in range(zs)])
+    mixed, squares = close(
+        base, [swap_pg(parts1[z], 4 * z + 2, n_pg) for z in reversed(range(zs))]
+    )
     return last_norm(mixed, squares, swap_kv(squares), norm_gain_out)
 
 

time: 104 us -> 100 us (0.962)
  waiting for transfers between devices: 41.5 us -> 38.2 us
    ppermute x11, waiting for transfers between devices: 13.7 us -> 8.92 us  [swap_kv(): return lax.ppermute(x, 'kv', [(0, 1), (1, 0)])]
    ppermute x23, waiting for transfers between devices: 23.9 us -> 25.4 us  [swap_pg(): return lax.ppermute(x, 'pg', [(i, i ^ mask) for i in range(n)])]
  transfers between devices with their start and end apart: 35 -> 35, of which waited for: 18 -> 20; matrix products, arithmetic and copies ran while one was open for 1% -> 1% of each run, Pallas kernels for 12% -> 13%
where the time goes in v4:
time: 100 us
  starting transfers between devices  42.3 us (42%)
  waiting for transfers between devices  38.2 us (38%)
  Pallas kernels  16.3 us (16%)
  local copies, waits for them, and re-layouts  2.36 us (2%)
    ppermute x23, waiting for transfers between devices, swap_pg(): return lax.ppermute(x, 'pg', [(i, i ^ mask) for i in range(n)])  25.4 us
    ppermute x23, starting transfers between devices, swap_pg(): return lax.ppermute(x, 'pg', [(i, i ^ mask) for i in range(n)])  20.8 us
    pallas_call x24, Pallas kernels, run(): pl.pallas_call(body, out_shape=[jax.ShapeDtypeStruct(s, d) for s, d in ou...  16.3 us
    ppermute x11, starting transfers between devices, swap_kv(): return lax.ppermute(x, 'kv', [(0, 1), (1, 0)])  14 us
    ppermute x11, waiting for transfers between devices, swap_kv(): return lax.ppermute(x, 'kv', [(0, 1), (1, 0)])  8.92 us
    all_to_all x1, starting transfers between devices, fast_local(): sent = lax.all_to_all(packed, 'pg', split_axis=0, concat_axis=0, tiled=True)  7.53 us
    all_to_all x1, waiting for transfers between devices, fast_local(): sent = lax.all_to_all(packed, 'pg', split_axis=0, concat_axis=0, tiled=True)  3.86 us
  transfers between devices with their start and end apart: 35, of which 20 were waited for; matrix products, arithmetic and copies ran while one was open for 1% of the time, Pallas kernels for 13%

profile of v4, /device:TPU:0, one launch (start us, length us, event | category | flops | bytes accessed | tf_op | source)
XLA Modules:
  0.0 100.2 jit_solution(16307329223813100164)
XLA Ops:
  0.0 1.6 %shard_map.136 = bf16[16,56,128]{2,1,0:T(8,128)(2,1)} custom-call(bf16[4,768]{1,0:T(4,128)(2,1)} %q_hbm.1, bf16[64,768]{1,0:T(8,128)(2,1)} %res.1, s32[8,64]{1,0:T(8,128)} %bitcast.6, f32[8,64]{1,0:T(8,128)} %bitcast.7), custom_call_target="tpu_custom_call" | custom-call | flops 1000000000 | bytes 1 | tf_op jit(solution)/shard_map/pallas_call | solution.py:202
  1.7 7.5 %all-to-all-start = ((bf16[16,56,128]{2,1,0:T(8,128)(2,1)}), bf16[16,56,128]{2,1,0:T(8,128)(2,1)S(1)}, u32[]{:S(2)}, u32[]{:S(2)}) async-start(bf16[16,56,128]{2,1,0:T(8,128)(2,1)} %shard_map.136), calls=%async_computation | async-start | bytes 458752 | tf_op jit(solution)/shard_map/all_to_all | solution.py:866
  9.2 1.7 %copy-done.2 = bf16[768,1536]{1,0:T(8,128)(2,1)S(1)} copy-done((bf16[768,1536]{1,0:T(8,128)(2,1)S(1)}, bf16[768,1536]{1,0:T(8,128)(2,1)}, u32[]{:S(2)}) %copy-start.2) | copy-done | bytes 2359320
  11.5 1.6 %collective-permute-start = (bf16[64,768]{1,0:T(8,128)(2,1)S(1)}, bf16[64,768]{1,0:T(8,128)(2,1)S(1)}, u32[]{:S(2)}, u32[]{:S(2)}) collective-permute-start(bf16[64,768]{1,0:T(8,128)(2,1)S(1)} %get-tuple-element.76.sent_ref), channel_id=1, source_target_pairs={{0,16},{16,0},{1,17},{17,1},{2,18},{18,2},{3,19},{19,3},{4,20},{20... | collective-permute-start | bytes 294920 | tf_op jit(solution)/shard_map/ppermute | solution.py:238
  14.9 3.9 %all-to-all-done.sent_ref = bf16[16,56,128]{2,1,0:T(8,128)(2,1)S(1)} async-done(((bf16[16,56,128]{2,1,0:T(8,128)(2,1)}), bf16[16,56,128]{2,1,0:T(8,128)(2,1)S(1)}, u32[]{:S(2)}, u32[]{:S(2)}) %all-to-all-start) | async-done | bytes 229408 | tf_op jit(solution)/shard_map/all_to_all | solution.py:866
  18.7 1.7 %shard_map.138.pages_ref = bf16[16,1024]{1,0:T(8,128)(2,1)S(1)} custom-call(s32[256,1]{1,0:T(8,128)S(1)} %broadcast_in_dim_reshape.9.owner_col, s32[256,1]{1,0:T(8,128)S(1)} %broadcast_in_dim_reshape.10.live_col, bf16[16,56,128]{2,1,0:T(8,128)(2,1)S(1)} %all-to-all-done.sent_ref, bf16[16,4,128,128]{3,2,1,0:T(8,128)(2,1)S(1)} %copy-done.4), custom_call_target="tpu_custom_call" | custom-call | flops 1000000000 | bytes 1 | tf_op jit(solution)/shard_map/pallas_call | solution.py:202
  20.7 2.3 %collective-permute-start.3 = (bf16[64,1024]{1,0:T(8,128)(2,1)S(1)}, bf16[64,1024]{1,0:T(8,128)(2,1)S(1)}, u32[]{:S(2)}, u32[]{:S(2)}) collective-permute-start(bf16[64,1024]{1,0:T(8,128)(2,1)S(1)} %get-tuple-element.81.refs_0_), channel_id=1, source_target_pairs={{0,8},{1,9},{2,10},{3,11},{4,12},{5,13},{6,14},{7,15},{8,0},{9,1},... | collective-permute-start | bytes 393224 | tf_op jit(solution)/shard_map/ppermute | solution.py:242
  23.0 2.0 %collective-permute-start.4 = (bf16[64,1024]{1,0:T(8,128)(2,1)S(1)}, bf16[64,1024]{1,0:T(8,128)(2,1)S(1)}, u32[]{:S(2)}, u32[]{:S(2)}) collective-permute-start(bf16[64,1024]{1,0:T(8,128)(2,1)S(1)} %get-tuple-element.81.refs_0_), channel_id=1, source_target_pairs={{0,12},{1,13},{2,14},{3,15},{4,8},{5,9},{6,10},{7,11},{8,4},{9,5},... | collective-permute-start | bytes 393224 | tf_op jit(solution)/shard_map/ppermute | solution.py:242
  26.0 2.4 %shard_map.141 = (bf16[3,768,1024]{2,1,0:T(8,128)(2,1)S(1)}, bf16[3,512,768]{2,1,0:T(8,128)(2,1)S(1)}) custom-call(bf16[3,768,1024]{2,1,0:T(8,128)(2,1)} %refs_0_, bf16[3,512,768]{2,1,0:T(8,128)(2,1)S(1)} %copy-done), custom_call_target="tpu_custom_call" | custom-call | flops 1000000000 | bytes 1 | tf_op jit(solution)/shard_map/pallas_call | solution.py:202
  28.5 5.1 %collective-permute-done.3.refs_2_ = bf16[64,1024]{1,0:T(8,128)(2,1)S(1)} collective-permute-done((bf16[64,1024]{1,0:T(8,128)(2,1)S(1)}, bf16[64,1024]{1,0:T(8,128)(2,1)S(1)}, u32[]{:S(2)}, u32[]{:S(2)}) %collective-permute-start.3) | collective-permute-done | bytes 131104 | tf_op jit(solution)/shard_map/ppermute | solution.py:242
  36.1 1.5 %collective-permute-start.14 = (bf16[3,128,512]{2,1,0:T(8,128)(2,1)S(1)}, bf16[3,128,512]{2,1,0:T(8,128)(2,1)S(1)}, u32[]{:S(2)}, u32[]{:S(2)}) collective-permute-start(bf16[3,128,512]{2,1,0:T(8,128)(2,1)S(1)} %get-tuple-element.98), channel_id=1, source_target_pairs={{0,16},{16,0},{1,17},{17,1},{2,18},{18,2},{3,19},{19,3},{4,20},{20... | collective-permute-start | bytes 1179656 | tf_op jit(solution)/shard_map/ppermute | solution.py:238
  43.1 1.5 %collective-permute-start.10 = (bf16[64,768]{1,0:T(8,128)(2,1)S(1)}, bf16[64,768]{1,0:T(8,128)(2,1)S(1)}, u32[]{:S(2)}, u32[]{:S(2)}) collective-permute-start(bf16[64,768]{1,0:T(8,128)(2,1)S(1)} %get-tuple-element.96.sent_ref), channel_id=1, source_target_pairs={{0,16},{16,0},{1,17},{17,1},{2,18},{18,2},{3,19},{19,3},{4,20},{20... | collective-permute-start | bytes 294920 | tf_op jit(solution)/shard_map/ppermute | solution.py:238
  45.2 2.9 %collective-permute-done.14.refs_0_ = bf16[3,128,512]{2,1,0:T(8,128)(2,1)S(1)} collective-permute-done((bf16[3,128,512]{2,1,0:T(8,128)(2,1)S(1)}, bf16[3,128,512]{2,1,0:T(8,128)(2,1)S(1)}, u32[]{:S(2)}, u32[]{:S(2)}) %collective-permute-start.14) | collective-permute-done | bytes 393248 | tf_op jit(solution)/shard_map/ppermute | solution.py:238
  57.1 1.6 %collective-permute-start.24 = (bf16[3,128,512]{2,1,0:T(8,128)(2,1)S(1)}, bf16[3,128,512]{2,1,0:T(8,128)(2,1)S(1)}, u32[]{:S(2)}, u32[]{:S(2)}) collective-permute-start(bf16[3,128,512]{2,1,0:T(8,128)(2,1)S(1)} %get-tuple-element.125), channel_id=1, source_target_pairs={{0,16},{16,0},{1,17},{17,1},{2,18},{18,2},{3,19},{19,3},{4,20},{20... | collective-permute-start | bytes 1179656 | tf_op jit(solution)/shard_map/ppermute | solution.py:238
  59.2 1.8 %collective-permute-done.16.got_ref = bf16[3,32,1024]{2,1,0:T(8,128)(2,1)S(1)} collective-permute-done((bf16[3,32,1024]{2,1,0:T(8,128)(2,1)S(1)}, bf16[3,32,1024]{2,1,0:T(8,128)(2,1)S(1)}, u32[]{:S(2)}, u32[]{:S(2)}) %collective-permute-start.16) | collective-permute-done | bytes 196640 | tf_op jit(solution)/shard_map/ppermute | solution.py:238
  64.3 2.1 %collective-permute-start.21 = (bf16[72,768]{1,0:T(8,128)(2,1)S(1)}, bf16[72,768]{1,0:T(8,128)(2,1)S(1)}, u32[]{:S(2)}, u32[]{:S(2)}) collective-permute-start(bf16[72,768]{1,0:T(8,128)(2,1)S(1)} %get-tuple-element.122), channel_id=1, source_target_pairs={{0,12},{1,13},{2,14},{3,15},{4,8},{5,9},{6,10},{7,11},{8,4},{9,5},... | collective-permute-start | bytes 331784 | tf_op jit(solution)/shard_map/ppermute | solution.py:242
  66.4 2.0 %collective-permute-start.22 = (bf16[72,768]{1,0:T(8,128)(2,1)S(1)}, bf16[72,768]{1,0:T(8,128)(2,1)S(1)}, u32[]{:S(2)}, u32[]{:S(2)}) collective-permute-start(bf16[72,768]{1,0:T(8,128)(2,1)S(1)} %get-tuple-element.123), channel_id=1, source_target_pairs={{0,8},{1,9},{2,10},{3,11},{4,12},{5,13},{6,14},{7,15},{8,0},{9,1},... | collective-permute-start | bytes 331784 | tf_op jit(solution)/shard_map/ppermute | solution.py:242
  72.1 6.3 %collective-permute-done.22.refs_2_ = bf16[72,768]{1,0:T(8,128)(2,1)S(1)} collective-permute-done((bf16[72,768]{1,0:T(8,128)(2,1)S(1)}, bf16[72,768]{1,0:T(8,128)(2,1)S(1)}, u32[]{:S(2)}, u32[]{:S(2)}) %collective-permute-start.22) | collective-permute-done | bytes 110624 | tf_op jit(solution)/shard_map/ppermute | solution.py:242
  81.4 2.4 %collective-permute-start.29 = (bf16[64,768]{1,0:T(8,128)(2,1)S(1)}, bf16[64,768]{1,0:T(8,128)(2,1)S(1)}, u32[]{:S(2)}, u32[]{:S(2)}) collective-permute-start(bf16[64,768]{1,0:T(8,128)(2,1)S(1)} %get-tuple-element.137), channel_id=1, source_target_pairs={{0,14},{1,15},{2,12},{3,13},{4,10},{5,11},{6,8},{7,9},{8,6},{9,7},... | collective-permute-start | bytes 294920 | tf_op jit(solution)/shard_map/ppermute | solution.py:242
  83.8 3.2 %collective-permute-start.31 = (bf16[64,768]{1,0:T(8,128)(2,1)S(1)}, bf16[64,768]{1,0:T(8,128)(2,1)S(1)}, u32[]{:S(2)}, u32[]{:S(2)}) collective-permute-start(bf16[64,768]{1,0:T(8,128)(2,1)S(1)} %get-tuple-element.139), channel_id=1, source_target_pairs={{0,6},{1,7},{2,4},{3,5},{4,2},{5,3},{6,0},{7,1},{8,14},{9,15},{10,... | collective-permute-start | bytes 294920 | tf_op jit(solution)/shard_map/ppermute | solution.py:242
  88.2 1.8 %collective-permute-done.29.refs_0_ = bf16[64,768]{1,0:T(8,128)(2,1)S(1)} collective-permute-done((bf16[64,768]{1,0:T(8,128)(2,1)S(1)}, bf16[64,768]{1,0:T(8,128)(2,1)S(1)}, u32[]{:S(2)}, u32[]{:S(2)}) %collective-permute-start.29) | collective-permute-done | bytes 98336 | tf_op jit(solution)/shard_map/ppermute | solution.py:242
  89.9 3.4 %collective-permute-done.30.refs_1_ = bf16[64,768]{1,0:T(8,128)(2,1)S(1)} collective-permute-done((bf16[64,768]{1,0:T(8,128)(2,1)S(1)}, bf16[64,768]{1,0:T(8,128)(2,1)S(1)}, u32[]{:S(2)}, u32[]{:S(2)}) %collective-permute-start.30) | collective-permute-done | bytes 98336 | tf_op jit(solution)/shard_map/ppermute | solution.py:242
  93.4 2.0 %collective-permute-done.32.refs_3_ = bf16[64,768]{1,0:T(8,128)(2,1)S(1)} collective-permute-done((bf16[64,768]{1,0:T(8,128)(2,1)S(1)}, bf16[64,768]{1,0:T(8,128)(2,1)S(1)}, u32[]{:S(2)}, u32[]{:S(2)}) %collective-permute-start.32) | collective-permute-done | bytes 98336 | tf_op jit(solution)/shard_map/ppermute | solution.py:242
  97.0 2.4 %collective-permute-done.33.far_ref = f32[64,128]{1,0:T(8,128)S(1)} collective-permute-done((f32[64,128]{1,0:T(8,128)S(1)}, f32[64,128]{1,0:T(8,128)S(1)}, u32[]{:S(2)}, u32[]{:S(2)}) %collective-permute-start.33) | collective-permute-done | bytes 32800 | tf_op jit(solution)/shard_map/ppermute | solution.py:238
  (108 shorter events, 34.9 us)
Async XLA Ops:
  1.7 17.1 %all-to-all-start = ((bf16[16,56,128]{2,1,0:T(8,128)(2,1)}), bf16[16,56,128]{2,1,0:T(8,128)(2,1)S(1)}, u32[]{:S(2)}, u32[]{:S(2)}) async-start(bf16[16,56,128]{2,1,0:T(8,128)(2,1)} %shard_map.136), calls=%async_computation | async-start | bytes 458752 | tf_op jit(solution)/shard_map/all_to_all | solution.py:866
  11.5 8.9 %collective-permute-start = (bf16[64,768]{1,0:T(8,128)(2,1)S(1)}, bf16[64,768]{1,0:T(8,128)(2,1)S(1)}, u32[]{:S(2)}, u32[]{:S(2)}) collective-permute-start(bf16[64,768]{1,0:T(8,128)(2,1)S(1)} %get-tuple-element.76.sent_ref), channel_id=1, source_target_pairs={{0,16},{16,0},{1,17},{17,1},{2,18},{18,2},{3,19},{19,3},{4,20},{20... | collective-permute-start | bytes 294920 | tf_op jit(solution)/shard_map/ppermute | solution.py:238
  13.0 7.4 %collective-permute-start.1 = (bf16[64,768]{1,0:T(8,128)(2,1)S(1)}, bf16[64,768]{1,0:T(8,128)(2,1)S(1)}, u32[]{:S(2)}, u32[]{:S(2)}) collective-permute-start(bf16[64,768]{1,0:T(8,128)(2,1)S(1)} %get-tuple-element.77), channel_id=1, source_target_pairs={{0,16},{16,0},{1,17},{17,1},{2,18},{18,2},{3,19},{19,3},{4,20},{20... | collective-permute-start | bytes 294920 | tf_op jit(solution)/shard_map/ppermute | solution.py:238
  20.6 7.9 %collective-permute-start.2 = (bf16[64,1024]{1,0:T(8,128)(2,1)S(1)}, bf16[64,1024]{1,0:T(8,128)(2,1)S(1)}, u32[]{:S(2)}, u32[]{:S(2)}) collective-permute-start(bf16[64,1024]{1,0:T(8,128)(2,1)S(1)} %get-tuple-element.81.refs_0_), channel_id=1, source_target_pairs={{0,4},{1,5},{2,6},{3,7},{4,0},{5,1},{6,2},{7,3},{8,12},{9,13},{10,... | collective-permute-start | bytes 393224 | tf_op jit(solution)/shard_map/ppermute | solution.py:242
  20.7 12.9 %collective-permute-start.3 = (bf16[64,1024]{1,0:T(8,128)(2,1)S(1)}, bf16[64,1024]{1,0:T(8,128)(2,1)S(1)}, u32[]{:S(2)}, u32[]{:S(2)}) collective-permute-start(bf16[64,1024]{1,0:T(8,128)(2,1)S(1)} %get-tuple-element.81.refs_0_), channel_id=1, source_target_pairs={{0,8},{1,9},{2,10},{3,11},{4,12},{5,13},{6,14},{7,15},{8,0},{9,1},... | collective-permute-start | bytes 393224 | tf_op jit(solution)/shard_map/ppermute | solution.py:242
  23.0 10.6 %collective-permute-start.4 = (bf16[64,1024]{1,0:T(8,128)(2,1)S(1)}, bf16[64,1024]{1,0:T(8,128)(2,1)S(1)}, u32[]{:S(2)}, u32[]{:S(2)}) collective-permute-start(bf16[64,1024]{1,0:T(8,128)(2,1)S(1)} %get-tuple-element.81.refs_0_), channel_id=1, source_target_pairs={{0,12},{1,13},{2,14},{3,15},{4,8},{5,9},{6,10},{7,11},{8,4},{9,5},... | collective-permute-start | bytes 393224 | tf_op jit(solution)/shard_map/ppermute | solution.py:242
  34.2 5.5 %collective-permute-start.5 = (bf16[64,1024]{1,0:T(8,128)(2,1)S(1)}, bf16[64,1024]{1,0:T(8,128)(2,1)S(1)}, u32[]{:S(2)}, u32[]{:S(2)}) collective-permute-start(bf16[64,1024]{1,0:T(8,128)(2,1)S(1)} %get-tuple-element.90.refs_0_), channel_id=1, source_target_pairs={{0,2},{1,3},{2,0},{3,1},{4,6},{5,7},{6,4},{7,5},{8,10},{9,11},{10,... | collective-permute-start | bytes 393224 | tf_op jit(solution)/shard_map/ppermute | solution.py:242
  36.1 12.0 %collective-permute-start.14 = (bf16[3,128,512]{2,1,0:T(8,128)(2,1)S(1)}, bf16[3,128,512]{2,1,0:T(8,128)(2,1)S(1)}, u32[]{:S(2)}, u32[]{:S(2)}) collective-permute-start(bf16[3,128,512]{2,1,0:T(8,128)(2,1)S(1)} %get-tuple-element.98), channel_id=1, source_target_pairs={{0,16},{16,0},{1,17},{17,1},{2,18},{18,2},{3,19},{19,3},{4,20},{20... | collective-permute-start | bytes 1179656 | tf_op jit(solution)/shard_map/ppermute | solution.py:238
  39.7 10.1 %collective-permute-start.12 = (bf16[128,768]{1,0:T(8,128)(2,1)S(1)}, bf16[128,768]{1,0:T(8,128)(2,1)S(1)}, u32[]{:S(2)}, u32[]{:S(2)}) collective-permute-start(bf16[128,768]{1,0:T(8,128)(2,1)S(1)} %get-tuple-element.91.refs_0_), channel_id=1, source_target_pairs={{0,2},{1,3},{2,0},{3,1},{4,6},{5,7},{6,4},{7,5},{8,10},{9,11},{10,... | collective-permute-start | bytes 589832 | tf_op jit(solution)/shard_map/ppermute | solution.py:242
  40.5 10.7 %collective-permute-start.13 = (bf16[128,768]{1,0:T(8,128)(2,1)S(1)}, bf16[128,768]{1,0:T(8,128)(2,1)S(1)}, u32[]{:S(2)}, u32[]{:S(2)}) collective-permute-start(bf16[128,768]{1,0:T(8,128)(2,1)S(1)} %get-tuple-element.92.refs_1_), channel_id=1, source_target_pairs={{0,2},{1,3},{2,0},{3,1},{4,6},{5,7},{6,4},{7,5},{8,10},{9,11},{10,... | collective-permute-start | bytes 589832 | tf_op jit(solution)/shard_map/ppermute | solution.py:242
  43.1 8.6 %collective-permute-start.10 = (bf16[64,768]{1,0:T(8,128)(2,1)S(1)}, bf16[64,768]{1,0:T(8,128)(2,1)S(1)}, u32[]{:S(2)}, u32[]{:S(2)}) collective-permute-start(bf16[64,768]{1,0:T(8,128)(2,1)S(1)} %get-tuple-element.96.sent_ref), channel_id=1, source_target_pairs={{0,16},{16,0},{1,17},{17,1},{2,18},{18,2},{3,19},{19,3},{4,20},{20... | collective-permute-start | bytes 294920 | tf_op jit(solution)/shard_map/ppermute | solution.py:238
  44.6 7.7 %collective-permute-start.11 = (bf16[64,768]{1,0:T(8,128)(2,1)S(1)}, bf16[64,768]{1,0:T(8,128)(2,1)S(1)}, u32[]{:S(2)}, u32[]{:S(2)}) collective-permute-start(bf16[64,768]{1,0:T(8,128)(2,1)S(1)} %get-tuple-element.97), channel_id=1, source_target_pairs={{0,16},{16,0},{1,17},{17,1},{2,18},{18,2},{3,19},{19,3},{4,20},{20... | collective-permute-start | bytes 294920 | tf_op jit(solution)/shard_map/ppermute | solution.py:238
  48.3 7.8 %collective-permute-start.15 = (bf16[3,128,256]{2,1,0:T(8,128)(2,1)S(1)}, bf16[3,128,256]{2,1,0:T(8,128)(2,1)S(1)}, u32[]{:S(2)}, u32[]{:S(2)}) collective-permute-start(bf16[3,128,256]{2,1,0:T(8,128)(2,1)S(1)} %shard_map.146.refs_0_), channel_id=1, source_target_pairs={{0,16},{16,0},{1,17},{17,1},{2,18},{18,2},{3,19},{19,3},{4,20},{20... | collective-permute-start | bytes 589832 | tf_op jit(solution)/shard_map/ppermute | solution.py:238
  53.5 7.6 %collective-permute-start.16 = (bf16[3,32,1024]{2,1,0:T(8,128)(2,1)S(1)}, bf16[3,32,1024]{2,1,0:T(8,128)(2,1)S(1)}, u32[]{:S(2)}, u32[]{:S(2)}) collective-permute-start(bf16[3,32,1024]{2,1,0:T(8,128)(2,1)S(1)} %get-tuple-element.109), channel_id=1, source_target_pairs={{0,16},{16,0},{1,17},{17,1},{2,18},{18,2},{3,19},{19,3},{4,20},{20... | collective-permute-start | bytes 589832 | tf_op jit(solution)/shard_map/ppermute | solution.py:238
  57.1 11.6 %collective-permute-start.24 = (bf16[3,128,512]{2,1,0:T(8,128)(2,1)S(1)}, bf16[3,128,512]{2,1,0:T(8,128)(2,1)S(1)}, u32[]{:S(2)}, u32[]{:S(2)}) collective-permute-start(bf16[3,128,512]{2,1,0:T(8,128)(2,1)S(1)} %get-tuple-element.125), channel_id=1, source_target_pairs={{0,16},{16,0},{1,17},{17,1},{2,18},{18,2},{3,19},{19,3},{4,20},{20... | collective-permute-start | bytes 1179656 | tf_op jit(solution)/shard_map/ppermute | solution.py:238
  64.3 7.9 %collective-permute-start.21 = (bf16[72,768]{1,0:T(8,128)(2,1)S(1)}, bf16[72,768]{1,0:T(8,128)(2,1)S(1)}, u32[]{:S(2)}, u32[]{:S(2)}) collective-permute-start(bf16[72,768]{1,0:T(8,128)(2,1)S(1)} %get-tuple-element.122), channel_id=1, source_target_pairs={{0,12},{1,13},{2,14},{3,15},{4,8},{5,9},{6,10},{7,11},{8,4},{9,5},... | collective-permute-start | bytes 331784 | tf_op jit(solution)/shard_map/ppermute | solution.py:242
  66.4 12.0 %collective-permute-start.22 = (bf16[72,768]{1,0:T(8,128)(2,1)S(1)}, bf16[72,768]{1,0:T(8,128)(2,1)S(1)}, u32[]{:S(2)}, u32[]{:S(2)}) collective-permute-start(bf16[72,768]{1,0:T(8,128)(2,1)S(1)} %get-tuple-element.123), channel_id=1, source_target_pairs={{0,8},{1,9},{2,10},{3,11},{4,12},{5,13},{6,14},{7,15},{8,0},{9,1},... | collective-permute-start | bytes 331784 | tf_op jit(solution)/shard_map/ppermute | solution.py:242
  68.4 10.0 %collective-permute-start.23 = (bf16[72,768]{1,0:T(8,128)(2,1)S(1)}, bf16[72,768]{1,0:T(8,128)(2,1)S(1)}, u32[]{:S(2)}, u32[]{:S(2)}) collective-permute-start(bf16[72,768]{1,0:T(8,128)(2,1)S(1)} %get-tuple-element.124), channel_id=1, source_target_pairs={{0,4},{1,5},{2,6},{3,7},{4,0},{5,1},{6,2},{7,3},{8,12},{9,13},{10,... | collective-permute-start | bytes 331784 | tf_op jit(solution)/shard_map/ppermute | solution.py:242
  68.9 9.7 %collective-permute-start.25 = (bf16[3,64,256]{2,1,0:T(8,128)(2,1)S(1)}, bf16[3,64,256]{2,1,0:T(8,128)(2,1)S(1)}, u32[]{:S(2)}, u32[]{:S(2)}) collective-permute-start(bf16[3,64,256]{2,1,0:T(8,128)(2,1)S(1)} %get-tuple-element.127.refs_0_), channel_id=1, source_target_pairs={{0,16},{16,0},{1,17},{17,1},{2,18},{18,2},{3,19},{19,3},{4,20},{20... | collective-permute-start | bytes 294920 | tf_op jit(solution)/shard_map/ppermute | solution.py:238
  70.4 8.2 %collective-permute-start.26 = (bf16[3,64,256]{2,1,0:T(8,128)(2,1)S(1)}, bf16[3,64,256]{2,1,0:T(8,128)(2,1)S(1)}, u32[]{:S(2)}, u32[]{:S(2)}) collective-permute-start(bf16[3,64,256]{2,1,0:T(8,128)(2,1)S(1)} %get-tuple-element.128.refs_1_), channel_id=1, source_target_pairs={{0,16},{16,0},{1,17},{17,1},{2,18},{18,2},{3,19},{19,3},{4,20},{20... | collective-permute-start | bytes 294920 | tf_op jit(solution)/shard_map/ppermute | solution.py:238
  81.4 8.6 %collective-permute-start.29 = (bf16[64,768]{1,0:T(8,128)(2,1)S(1)}, bf16[64,768]{1,0:T(8,128)(2,1)S(1)}, u32[]{:S(2)}, u32[]{:S(2)}) collective-permute-start(bf16[64,768]{1,0:T(8,128)(2,1)S(1)} %get-tuple-element.137), channel_id=1, source_target_pairs={{0,14},{1,15},{2,12},{3,13},{4,10},{5,11},{6,8},{7,9},{8,6},{9,7},... | collective-permute-start | bytes 294920 | tf_op jit(solution)/shard_map/ppermute | solution.py:242
  83.8 9.6 %collective-permute-start.30 = (bf16[64,768]{1,0:T(8,128)(2,1)S(1)}, bf16[64,768]{1,0:T(8,128)(2,1)S(1)}, u32[]{:S(2)}, u32[]{:S(2)}) collective-permute-start(bf16[64,768]{1,0:T(8,128)(2,1)S(1)} %get-tuple-element.138), channel_id=1, source_target_pairs={{0,10},{1,11},{2,8},{3,9},{4,14},{5,15},{6,12},{7,13},{8,2},{9,3},... | collective-permute-start | bytes 294920 | tf_op jit(solution)/shard_map/ppermute | solution.py:242
  83.8 9.6 %collective-permute-start.31 = (bf16[64,768]{1,0:T(8,128)(2,1)S(1)}, bf16[64,768]{1,0:T(8,128)(2,1)S(1)}, u32[]{:S(2)}, u32[]{:S(2)}) collective-permute-start(bf16[64,768]{1,0:T(8,128)(2,1)S(1)} %get-tuple-element.139), channel_id=1, source_target_pairs={{0,6},{1,7},{2,4},{3,5},{4,2},{5,3},{6,0},{7,1},{8,14},{9,15},{10,... | collective-permute-start | bytes 294920 | tf_op jit(solution)/shard_map/ppermute | solution.py:242
  87.0 8.4 %collective-permute-start.32 = (bf16[64,768]{1,0:T(8,128)(2,1)S(1)}, bf16[64,768]{1,0:T(8,128)(2,1)S(1)}, u32[]{:S(2)}, u32[]{:S(2)}) collective-permute-start(bf16[64,768]{1,0:T(8,128)(2,1)S(1)} %get-tuple-element.140), channel_id=1, source_target_pairs={{0,2},{1,3},{2,0},{3,1},{4,6},{5,7},{6,4},{7,5},{8,10},{9,11},{10,... | collective-permute-start | bytes 294920 | tf_op jit(solution)/shard_map/ppermute | solution.py:242
  (22 other events, 134.3 us)

commit v5 on v4

--- a/solution.py
+++ b/solution.py
@@ -935,7 +935,7 @@
     keep0, *give0 = down(
         near0, after(far0, decode), w_rows, [0, 2], picks, gates, me_kv, rows, own_req, decode
     )
-    parts0 = split_sum(keep0, swap_each(give0, 1), rows, F32, 8)
+    parts0 = split_sum(keep0, swap_each(give0, 1), rows, F32, 0)
     lines0 = [swap_pg(parts0[z], 4 * z, n_pg) for z in reversed(range(1, zs))]
     near1 = activate(own1, after(got1, parts0), 2)
     far1 = swap_units(near1)

time: 100 us -> 99.4 us (level)
  waiting for transfers between devices: 38.2 us -> 37.2 us
    ppermute x23, waiting for transfers between devices: 25.4 us -> 24.4 us  [swap_pg(): return lax.ppermute(x, 'pg', [(i, i ^ mask) for i in range(n)])]
where the time goes in v5:
time: 99.4 us; the launch traced here: 99.1 us
  starting transfers between devices  42.3 us (43%)
  waiting for transfers between devices  37.2 us (37%)
  Pallas kernels  16.3 us (16%)
  local copies, waits for them, and re-layouts  2.36 us (2%)
    ppermute x23, waiting for transfers between devices, swap_pg(): return lax.ppermute(x, 'pg', [(i, i ^ mask) for i in range(n)])  24.4 us
    ppermute x23, starting transfers between devices, swap_pg(): return lax.ppermute(x, 'pg', [(i, i ^ mask) for i in range(n)])  20.8 us
    pallas_call x24, Pallas kernels, run(): pl.pallas_call(body, out_shape=[jax.ShapeDtypeStruct(s, d) for s, d in ou...  16.3 us
    ppermute x11, starting transfers between devices, swap_kv(): return lax.ppermute(x, 'kv', [(0, 1), (1, 0)])  14 us
    ppermute x11, waiting for transfers between devices, swap_kv(): return lax.ppermute(x, 'kv', [(0, 1), (1, 0)])  8.92 us
    all_to_all x1, starting transfers between devices, fast_local(): sent = lax.all_to_all(packed, 'pg', split_axis=0, concat_axis=0, tiled=True)  7.53 us
    all_to_all x1, waiting for transfers between devices, fast_local(): sent = lax.all_to_all(packed, 'pg', split_axis=0, concat_axis=0, tiled=True)  3.86 us
  transfers between devices with their start and end apart: 35, of which 20 were waited for; matrix products, arithmetic and copies ran while one was open for 1% of the time, Pallas kernels for 13%

profile of v5, /device:TPU:0, one launch (start us, length us, event | category | flops | bytes accessed | tf_op | source)
XLA Modules:
  0.0 99.1 jit_solution(330620770663167912)
XLA Ops:
  0.0 1.6 %shard_map.136 = bf16[16,56,128]{2,1,0:T(8,128)(2,1)} custom-call(bf16[4,768]{1,0:T(4,128)(2,1)} %q_hbm.1, bf16[64,768]{1,0:T(8,128)(2,1)} %res.1, s32[8,64]{1,0:T(8,128)} %bitcast.6, f32[8,64]{1,0:T(8,128)} %bitcast.7), custom_call_target="tpu_custom_call" | custom-call | flops 1000000000 | bytes 1 | tf_op jit(solution)/shard_map/pallas_call | solution.py:202
  1.7 7.5 %all-to-all-start = ((bf16[16,56,128]{2,1,0:T(8,128)(2,1)}), bf16[16,56,128]{2,1,0:T(8,128)(2,1)S(1)}, u32[]{:S(2)}, u32[]{:S(2)}) async-start(bf16[16,56,128]{2,1,0:T(8,128)(2,1)} %shard_map.136), calls=%async_computation | async-start | bytes 458752 | tf_op jit(solution)/shard_map/all_to_all | solution.py:866
  9.2 1.7 %copy-done.2 = bf16[768,1536]{1,0:T(8,128)(2,1)S(1)} copy-done((bf16[768,1536]{1,0:T(8,128)(2,1)S(1)}, bf16[768,1536]{1,0:T(8,128)(2,1)}, u32[]{:S(2)}) %copy-start.2) | copy-done | bytes 2359320
  11.5 1.6 %collective-permute-start = (bf16[64,768]{1,0:T(8,128)(2,1)S(1)}, bf16[64,768]{1,0:T(8,128)(2,1)S(1)}, u32[]{:S(2)}, u32[]{:S(2)}) collective-permute-start(bf16[64,768]{1,0:T(8,128)(2,1)S(1)} %get-tuple-element.76.sent_ref), channel_id=1, source_target_pairs={{0,16},{16,0},{1,17},{17,1},{2,18},{18,2},{3,19},{19,3},{4,20},{20... | collective-permute-start | bytes 294920 | tf_op jit(solution)/shard_map/ppermute | solution.py:238
  14.9 3.9 %all-to-all-done.sent_ref = bf16[16,56,128]{2,1,0:T(8,128)(2,1)S(1)} async-done(((bf16[16,56,128]{2,1,0:T(8,128)(2,1)}), bf16[16,56,128]{2,1,0:T(8,128)(2,1)S(1)}, u32[]{:S(2)}, u32[]{:S(2)}) %all-to-all-start) | async-done | bytes 229408 | tf_op jit(solution)/shard_map/all_to_all | solution.py:866
  18.7 1.7 %shard_map.138.pages_ref = bf16[16,1024]{1,0:T(8,128)(2,1)S(1)} custom-call(s32[256,1]{1,0:T(8,128)S(1)} %broadcast_in_dim_reshape.9.owner_col, s32[256,1]{1,0:T(8,128)S(1)} %broadcast_in_dim_reshape.10.live_col, bf16[16,56,128]{2,1,0:T(8,128)(2,1)S(1)} %all-to-all-done.sent_ref, bf16[16,4,128,128]{3,2,1,0:T(8,128)(2,1)S(1)} %copy-done.4), custom_call_target="tpu_custom_call" | custom-call | flops 1000000000 | bytes 1 | tf_op jit(solution)/shard_map/pallas_call | solution.py:202
  20.7 2.3 %collective-permute-start.3 = (bf16[64,1024]{1,0:T(8,128)(2,1)S(1)}, bf16[64,1024]{1,0:T(8,128)(2,1)S(1)}, u32[]{:S(2)}, u32[]{:S(2)}) collective-permute-start(bf16[64,1024]{1,0:T(8,128)(2,1)S(1)} %get-tuple-element.81.refs_0_), channel_id=1, source_target_pairs={{0,8},{1,9},{2,10},{3,11},{4,12},{5,13},{6,14},{7,15},{8,0},{9,1},... | collective-permute-start | bytes 393224 | tf_op jit(solution)/shard_map/ppermute | solution.py:242
  23.0 2.0 %collective-permute-start.4 = (bf16[64,1024]{1,0:T(8,128)(2,1)S(1)}, bf16[64,1024]{1,0:T(8,128)(2,1)S(1)}, u32[]{:S(2)}, u32[]{:S(2)}) collective-permute-start(bf16[64,1024]{1,0:T(8,128)(2,1)S(1)} %get-tuple-element.81.refs_0_), channel_id=1, source_target_pairs={{0,12},{1,13},{2,14},{3,15},{4,8},{5,9},{6,10},{7,11},{8,4},{9,5},... | collective-permute-start | bytes 393224 | tf_op jit(solution)/shard_map/ppermute | solution.py:242
  26.0 2.4 %shard_map.141 = (bf16[3,768,1024]{2,1,0:T(8,128)(2,1)S(1)}, bf16[3,512,768]{2,1,0:T(8,128)(2,1)S(1)}) custom-call(bf16[3,768,1024]{2,1,0:T(8,128)(2,1)} %refs_0_, bf16[3,512,768]{2,1,0:T(8,128)(2,1)S(1)} %copy-done), custom_call_target="tpu_custom_call" | custom-call | flops 1000000000 | bytes 1 | tf_op jit(solution)/shard_map/pallas_call | solution.py:202
  28.5 5.1 %collective-permute-done.3.refs_2_ = bf16[64,1024]{1,0:T(8,128)(2,1)S(1)} collective-permute-done((bf16[64,1024]{1,0:T(8,128)(2,1)S(1)}, bf16[64,1024]{1,0:T(8,128)(2,1)S(1)}, u32[]{:S(2)}, u32[]{:S(2)}) %collective-permute-start.3) | collective-permute-done | bytes 131104 | tf_op jit(solution)/shard_map/ppermute | solution.py:242
  36.1 1.5 %collective-permute-start.14 = (bf16[3,128,512]{2,1,0:T(8,128)(2,1)S(1)}, bf16[3,128,512]{2,1,0:T(8,128)(2,1)S(1)}, u32[]{:S(2)}, u32[]{:S(2)}) collective-permute-start(bf16[3,128,512]{2,1,0:T(8,128)(2,1)S(1)} %get-tuple-element.98), channel_id=1, source_target_pairs={{0,16},{16,0},{1,17},{17,1},{2,18},{18,2},{3,19},{19,3},{4,20},{20... | collective-permute-start | bytes 1179656 | tf_op jit(solution)/shard_map/ppermute | solution.py:238
  43.1 1.5 %collective-permute-start.10 = (bf16[64,768]{1,0:T(8,128)(2,1)S(1)}, bf16[64,768]{1,0:T(8,128)(2,1)S(1)}, u32[]{:S(2)}, u32[]{:S(2)}) collective-permute-start(bf16[64,768]{1,0:T(8,128)(2,1)S(1)} %get-tuple-element.96.sent_ref), channel_id=1, source_target_pairs={{0,16},{16,0},{1,17},{17,1},{2,18},{18,2},{3,19},{19,3},{4,20},{20... | collective-permute-start | bytes 294920 | tf_op jit(solution)/shard_map/ppermute | solution.py:238
  45.2 2.9 %collective-permute-done.14.refs_0_ = bf16[3,128,512]{2,1,0:T(8,128)(2,1)S(1)} collective-permute-done((bf16[3,128,512]{2,1,0:T(8,128)(2,1)S(1)}, bf16[3,128,512]{2,1,0:T(8,128)(2,1)S(1)}, u32[]{:S(2)}, u32[]{:S(2)}) %collective-permute-start.14) | collective-permute-done | bytes 393248 | tf_op jit(solution)/shard_map/ppermute | solution.py:238
  57.1 1.6 %collective-permute-start.24 = (bf16[3,128,512]{2,1,0:T(8,128)(2,1)S(1)}, bf16[3,128,512]{2,1,0:T(8,128)(2,1)S(1)}, u32[]{:S(2)}, u32[]{:S(2)}) collective-permute-start(bf16[3,128,512]{2,1,0:T(8,128)(2,1)S(1)} %get-tuple-element.125), channel_id=1, source_target_pairs={{0,16},{16,0},{1,17},{17,1},{2,18},{18,2},{3,19},{19,3},{4,20},{20... | collective-permute-start | bytes 1179656 | tf_op jit(solution)/shard_map/ppermute | solution.py:238
  59.2 1.8 %collective-permute-done.16.got_ref = bf16[3,32,1024]{2,1,0:T(8,128)(2,1)S(1)} collective-permute-done((bf16[3,32,1024]{2,1,0:T(8,128)(2,1)S(1)}, bf16[3,32,1024]{2,1,0:T(8,128)(2,1)S(1)}, u32[]{:S(2)}, u32[]{:S(2)}) %collective-permute-start.16) | collective-permute-done | bytes 196640 | tf_op jit(solution)/shard_map/ppermute | solution.py:238
  64.3 2.1 %collective-permute-start.21 = (bf16[64,768]{1,0:T(8,128)(2,1)S(1)}, bf16[64,768]{1,0:T(8,128)(2,1)S(1)}, u32[]{:S(2)}, u32[]{:S(2)}) collective-permute-start(bf16[64,768]{1,0:T(8,128)(2,1)S(1)} %get-tuple-element.122), channel_id=1, source_target_pairs={{0,12},{1,13},{2,14},{3,15},{4,8},{5,9},{6,10},{7,11},{8,4},{9,5},... | collective-permute-start | bytes 294920 | tf_op jit(solution)/shard_map/ppermute | solution.py:242
  66.4 2.0 %collective-permute-start.22 = (bf16[64,768]{1,0:T(8,128)(2,1)S(1)}, bf16[64,768]{1,0:T(8,128)(2,1)S(1)}, u32[]{:S(2)}, u32[]{:S(2)}) collective-permute-start(bf16[64,768]{1,0:T(8,128)(2,1)S(1)} %get-tuple-element.123), channel_id=1, source_target_pairs={{0,8},{1,9},{2,10},{3,11},{4,12},{5,13},{6,14},{7,15},{8,0},{9,1},... | collective-permute-start | bytes 294920 | tf_op jit(solution)/shard_map/ppermute | solution.py:242
  71.9 5.5 %collective-permute-done.22.refs_2_ = bf16[64,768]{1,0:T(8,128)(2,1)S(1)} collective-permute-done((bf16[64,768]{1,0:T(8,128)(2,1)S(1)}, bf16[64,768]{1,0:T(8,128)(2,1)S(1)}, u32[]{:S(2)}, u32[]{:S(2)}) %collective-permute-start.22) | collective-permute-done | bytes 98336 | tf_op jit(solution)/shard_map/ppermute | solution.py:242
  80.3 2.4 %collective-permute-start.29 = (bf16[64,768]{1,0:T(8,128)(2,1)S(1)}, bf16[64,768]{1,0:T(8,128)(2,1)S(1)}, u32[]{:S(2)}, u32[]{:S(2)}) collective-permute-start(bf16[64,768]{1,0:T(8,128)(2,1)S(1)} %get-tuple-element.137), channel_id=1, source_target_pairs={{0,14},{1,15},{2,12},{3,13},{4,10},{5,11},{6,8},{7,9},{8,6},{9,7},... | collective-permute-start | bytes 294920 | tf_op jit(solution)/shard_map/ppermute | solution.py:242
  82.7 3.2 %collective-permute-start.31 = (bf16[64,768]{1,0:T(8,128)(2,1)S(1)}, bf16[64,768]{1,0:T(8,128)(2,1)S(1)}, u32[]{:S(2)}, u32[]{:S(2)}) collective-permute-start(bf16[64,768]{1,0:T(8,128)(2,1)S(1)} %get-tuple-element.139), channel_id=1, source_target_pairs={{0,6},{1,7},{2,4},{3,5},{4,2},{5,3},{6,0},{7,1},{8,14},{9,15},{10,... | collective-permute-start | bytes 294920 | tf_op jit(solution)/shard_map/ppermute | solution.py:242
  87.1 1.8 %collective-permute-done.29.refs_0_ = bf16[64,768]{1,0:T(8,128)(2,1)S(1)} collective-permute-done((bf16[64,768]{1,0:T(8,128)(2,1)S(1)}, bf16[64,768]{1,0:T(8,128)(2,1)S(1)}, u32[]{:S(2)}, u32[]{:S(2)}) %collective-permute-start.29) | collective-permute-done | bytes 98336 | tf_op jit(solution)/shard_map/ppermute | solution.py:242
  88.9 3.4 %collective-permute-done.30.refs_1_ = bf16[64,768]{1,0:T(8,128)(2,1)S(1)} collective-permute-done((bf16[64,768]{1,0:T(8,128)(2,1)S(1)}, bf16[64,768]{1,0:T(8,128)(2,1)S(1)}, u32[]{:S(2)}, u32[]{:S(2)}) %collective-permute-start.30) | collective-permute-done | bytes 98336 | tf_op jit(solution)/shard_map/ppermute | solution.py:242
  92.3 2.0 %collective-permute-done.32.refs_3_ = bf16[64,768]{1,0:T(8,128)(2,1)S(1)} collective-permute-done((bf16[64,768]{1,0:T(8,128)(2,1)S(1)}, bf16[64,768]{1,0:T(8,128)(2,1)S(1)}, u32[]{:S(2)}, u32[]{:S(2)}) %collective-permute-start.32) | collective-permute-done | bytes 98336 | tf_op jit(solution)/shard_map/ppermute | solution.py:242
  95.9 2.4 %collective-permute-done.33.far_ref = f32[64,128]{1,0:T(8,128)S(1)} collective-permute-done((f32[64,128]{1,0:T(8,128)S(1)}, f32[64,128]{1,0:T(8,128)S(1)}, u32[]{:S(2)}, u32[]{:S(2)}) %collective-permute-start.33) | collective-permute-done | bytes 32800 | tf_op jit(solution)/shard_map/ppermute | solution.py:238
  (108 shorter events, 34.7 us)
Async XLA Ops:
  1.7 17.1 %all-to-all-start = ((bf16[16,56,128]{2,1,0:T(8,128)(2,1)}), bf16[16,56,128]{2,1,0:T(8,128)(2,1)S(1)}, u32[]{:S(2)}, u32[]{:S(2)}) async-start(bf16[16,56,128]{2,1,0:T(8,128)(2,1)} %shard_map.136), calls=%async_computation | async-start | bytes 458752 | tf_op jit(solution)/shard_map/all_to_all | solution.py:866
  11.5 8.9 %collective-permute-start = (bf16[64,768]{1,0:T(8,128)(2,1)S(1)}, bf16[64,768]{1,0:T(8,128)(2,1)S(1)}, u32[]{:S(2)}, u32[]{:S(2)}) collective-permute-start(bf16[64,768]{1,0:T(8,128)(2,1)S(1)} %get-tuple-element.76.sent_ref), channel_id=1, source_target_pairs={{0,16},{16,0},{1,17},{17,1},{2,18},{18,2},{3,19},{19,3},{4,20},{20... | collective-permute-start | bytes 294920 | tf_op jit(solution)/shard_map/ppermute | solution.py:238
  13.0 7.4 %collective-permute-start.1 = (bf16[64,768]{1,0:T(8,128)(2,1)S(1)}, bf16[64,768]{1,0:T(8,128)(2,1)S(1)}, u32[]{:S(2)}, u32[]{:S(2)}) collective-permute-start(bf16[64,768]{1,0:T(8,128)(2,1)S(1)} %get-tuple-element.77), channel_id=1, source_target_pairs={{0,16},{16,0},{1,17},{17,1},{2,18},{18,2},{3,19},{19,3},{4,20},{20... | collective-permute-start | bytes 294920 | tf_op jit(solution)/shard_map/ppermute | solution.py:238
  20.6 7.9 %collective-permute-start.2 = (bf16[64,1024]{1,0:T(8,128)(2,1)S(1)}, bf16[64,1024]{1,0:T(8,128)(2,1)S(1)}, u32[]{:S(2)}, u32[]{:S(2)}) collective-permute-start(bf16[64,1024]{1,0:T(8,128)(2,1)S(1)} %get-tuple-element.81.refs_0_), channel_id=1, source_target_pairs={{0,4},{1,5},{2,6},{3,7},{4,0},{5,1},{6,2},{7,3},{8,12},{9,13},{10,... | collective-permute-start | bytes 393224 | tf_op jit(solution)/shard_map/ppermute | solution.py:242
  20.7 12.9 %collective-permute-start.3 = (bf16[64,1024]{1,0:T(8,128)(2,1)S(1)}, bf16[64,1024]{1,0:T(8,128)(2,1)S(1)}, u32[]{:S(2)}, u32[]{:S(2)}) collective-permute-start(bf16[64,1024]{1,0:T(8,128)(2,1)S(1)} %get-tuple-element.81.refs_0_), channel_id=1, source_target_pairs={{0,8},{1,9},{2,10},{3,11},{4,12},{5,13},{6,14},{7,15},{8,0},{9,1},... | collective-permute-start | bytes 393224 | tf_op jit(solution)/shard_map/ppermute | solution.py:242
  23.0 10.6 %collective-permute-start.4 = (bf16[64,1024]{1,0:T(8,128)(2,1)S(1)}, bf16[64,1024]{1,0:T(8,128)(2,1)S(1)}, u32[]{:S(2)}, u32[]{:S(2)}) collective-permute-start(bf16[64,1024]{1,0:T(8,128)(2,1)S(1)} %get-tuple-element.81.refs_0_), channel_id=1, source_target_pairs={{0,12},{1,13},{2,14},{3,15},{4,8},{5,9},{6,10},{7,11},{8,4},{9,5},... | collective-permute-start | bytes 393224 | tf_op jit(solution)/shard_map/ppermute | solution.py:242
  34.2 5.5 %collective-permute-start.5 = (bf16[64,1024]{1,0:T(8,128)(2,1)S(1)}, bf16[64,1024]{1,0:T(8,128)(2,1)S(1)}, u32[]{:S(2)}, u32[]{:S(2)}) collective-permute-start(bf16[64,1024]{1,0:T(8,128)(2,1)S(1)} %get-tuple-element.90.refs_0_), channel_id=1, source_target_pairs={{0,2},{1,3},{2,0},{3,1},{4,6},{5,7},{6,4},{7,5},{8,10},{9,11},{10,... | collective-permute-start | bytes 393224 | tf_op jit(solution)/shard_map/ppermute | solution.py:242
  36.1 12.0 %collective-permute-start.14 = (bf16[3,128,512]{2,1,0:T(8,128)(2,1)S(1)}, bf16[3,128,512]{2,1,0:T(8,128)(2,1)S(1)}, u32[]{:S(2)}, u32[]{:S(2)}) collective-permute-start(bf16[3,128,512]{2,1,0:T(8,128)(2,1)S(1)} %get-tuple-element.98), channel_id=1, source_target_pairs={{0,16},{16,0},{1,17},{17,1},{2,18},{18,2},{3,19},{19,3},{4,20},{20... | collective-permute-start | bytes 1179656 | tf_op jit(solution)/shard_map/ppermute | solution.py:238
  39.7 10.1 %collective-permute-start.12 = (bf16[128,768]{1,0:T(8,128)(2,1)S(1)}, bf16[128,768]{1,0:T(8,128)(2,1)S(1)}, u32[]{:S(2)}, u32[]{:S(2)}) collective-permute-start(bf16[128,768]{1,0:T(8,128)(2,1)S(1)} %get-tuple-element.91.refs_0_), channel_id=1, source_target_pairs={{0,2},{1,3},{2,0},{3,1},{4,6},{5,7},{6,4},{7,5},{8,10},{9,11},{10,... | collective-permute-start | bytes 589832 | tf_op jit(solution)/shard_map/ppermute | solution.py:242
  40.5 10.7 %collective-permute-start.13 = (bf16[128,768]{1,0:T(8,128)(2,1)S(1)}, bf16[128,768]{1,0:T(8,128)(2,1)S(1)}, u32[]{:S(2)}, u32[]{:S(2)}) collective-permute-start(bf16[128,768]{1,0:T(8,128)(2,1)S(1)} %get-tuple-element.92.refs_1_), channel_id=1, source_target_pairs={{0,2},{1,3},{2,0},{3,1},{4,6},{5,7},{6,4},{7,5},{8,10},{9,11},{10,... | collective-permute-start | bytes 589832 | tf_op jit(solution)/shard_map/ppermute | solution.py:242
  43.1 8.6 %collective-permute-start.10 = (bf16[64,768]{1,0:T(8,128)(2,1)S(1)}, bf16[64,768]{1,0:T(8,128)(2,1)S(1)}, u32[]{:S(2)}, u32[]{:S(2)}) collective-permute-start(bf16[64,768]{1,0:T(8,128)(2,1)S(1)} %get-tuple-element.96.sent_ref), channel_id=1, source_target_pairs={{0,16},{16,0},{1,17},{17,1},{2,18},{18,2},{3,19},{19,3},{4,20},{20... | collective-permute-start | bytes 294920 | tf_op jit(solution)/shard_map/ppermute | solution.py:238
  44.6 7.7 %collective-permute-start.11 = (bf16[64,768]{1,0:T(8,128)(2,1)S(1)}, bf16[64,768]{1,0:T(8,128)(2,1)S(1)}, u32[]{:S(2)}, u32[]{:S(2)}) collective-permute-start(bf16[64,768]{1,0:T(8,128)(2,1)S(1)} %get-tuple-element.97), channel_id=1, source_target_pairs={{0,16},{16,0},{1,17},{17,1},{2,18},{18,2},{3,19},{19,3},{4,20},{20... | collective-permute-start | bytes 294920 | tf_op jit(solution)/shard_map/ppermute | solution.py:238
  48.3 7.8 %collective-permute-start.15 = (bf16[3,128,256]{2,1,0:T(8,128)(2,1)S(1)}, bf16[3,128,256]{2,1,0:T(8,128)(2,1)S(1)}, u32[]{:S(2)}, u32[]{:S(2)}) collective-permute-start(bf16[3,128,256]{2,1,0:T(8,128)(2,1)S(1)} %shard_map.146.refs_0_), channel_id=1, source_target_pairs={{0,16},{16,0},{1,17},{17,1},{2,18},{18,2},{3,19},{19,3},{4,20},{20... | collective-permute-start | bytes 589832 | tf_op jit(solution)/shard_map/ppermute | solution.py:238
  53.5 7.6 %collective-permute-start.16 = (bf16[3,32,1024]{2,1,0:T(8,128)(2,1)S(1)}, bf16[3,32,1024]{2,1,0:T(8,128)(2,1)S(1)}, u32[]{:S(2)}, u32[]{:S(2)}) collective-permute-start(bf16[3,32,1024]{2,1,0:T(8,128)(2,1)S(1)} %get-tuple-element.109), channel_id=1, source_target_pairs={{0,16},{16,0},{1,17},{17,1},{2,18},{18,2},{3,19},{19,3},{4,20},{20... | collective-permute-start | bytes 589832 | tf_op jit(solution)/shard_map/ppermute | solution.py:238
  57.1 11.6 %collective-permute-start.24 = (bf16[3,128,512]{2,1,0:T(8,128)(2,1)S(1)}, bf16[3,128,512]{2,1,0:T(8,128)(2,1)S(1)}, u32[]{:S(2)}, u32[]{:S(2)}) collective-permute-start(bf16[3,128,512]{2,1,0:T(8,128)(2,1)S(1)} %get-tuple-element.125), channel_id=1, source_target_pairs={{0,16},{16,0},{1,17},{17,1},{2,18},{18,2},{3,19},{19,3},{4,20},{20... | collective-permute-start | bytes 1179656 | tf_op jit(solution)/shard_map/ppermute | solution.py:238
  64.3 7.6 %collective-permute-start.21 = (bf16[64,768]{1,0:T(8,128)(2,1)S(1)}, bf16[64,768]{1,0:T(8,128)(2,1)S(1)}, u32[]{:S(2)}, u32[]{:S(2)}) collective-permute-start(bf16[64,768]{1,0:T(8,128)(2,1)S(1)} %get-tuple-element.122), channel_id=1, source_target_pairs={{0,12},{1,13},{2,14},{3,15},{4,8},{5,9},{6,10},{7,11},{8,4},{9,5},... | collective-permute-start | bytes 294920 | tf_op jit(solution)/shard_map/ppermute | solution.py:242
  66.4 11.0 %collective-permute-start.22 = (bf16[64,768]{1,0:T(8,128)(2,1)S(1)}, bf16[64,768]{1,0:T(8,128)(2,1)S(1)}, u32[]{:S(2)}, u32[]{:S(2)}) collective-permute-start(bf16[64,768]{1,0:T(8,128)(2,1)S(1)} %get-tuple-element.123), channel_id=1, source_target_pairs={{0,8},{1,9},{2,10},{3,11},{4,12},{5,13},{6,14},{7,15},{8,0},{9,1},... | collective-permute-start | bytes 294920 | tf_op jit(solution)/shard_map/ppermute | solution.py:242
  68.4 9.0 %collective-permute-start.23 = (bf16[64,768]{1,0:T(8,128)(2,1)S(1)}, bf16[64,768]{1,0:T(8,128)(2,1)S(1)}, u32[]{:S(2)}, u32[]{:S(2)}) collective-permute-start(bf16[64,768]{1,0:T(8,128)(2,1)S(1)} %get-tuple-element.124), channel_id=1, source_target_pairs={{0,4},{1,5},{2,6},{3,7},{4,0},{5,1},{6,2},{7,3},{8,12},{9,13},{10,... | collective-permute-start | bytes 294920 | tf_op jit(solution)/shard_map/ppermute | solution.py:242
  68.9 8.7 %collective-permute-start.25 = (bf16[3,64,256]{2,1,0:T(8,128)(2,1)S(1)}, bf16[3,64,256]{2,1,0:T(8,128)(2,1)S(1)}, u32[]{:S(2)}, u32[]{:S(2)}) collective-permute-start(bf16[3,64,256]{2,1,0:T(8,128)(2,1)S(1)} %get-tuple-element.127.refs_0_), channel_id=1, source_target_pairs={{0,16},{16,0},{1,17},{17,1},{2,18},{18,2},{3,19},{19,3},{4,20},{20... | collective-permute-start | bytes 294920 | tf_op jit(solution)/shard_map/ppermute | solution.py:238
  70.4 7.2 %collective-permute-start.26 = (bf16[3,64,256]{2,1,0:T(8,128)(2,1)S(1)}, bf16[3,64,256]{2,1,0:T(8,128)(2,1)S(1)}, u32[]{:S(2)}, u32[]{:S(2)}) collective-permute-start(bf16[3,64,256]{2,1,0:T(8,128)(2,1)S(1)} %get-tuple-element.128.refs_1_), channel_id=1, source_target_pairs={{0,16},{16,0},{1,17},{17,1},{2,18},{18,2},{3,19},{19,3},{4,20},{20... | collective-permute-start | bytes 294920 | tf_op jit(solution)/shard_map/ppermute | solution.py:238
  80.3 8.6 %collective-permute-start.29 = (bf16[64,768]{1,0:T(8,128)(2,1)S(1)}, bf16[64,768]{1,0:T(8,128)(2,1)S(1)}, u32[]{:S(2)}, u32[]{:S(2)}) collective-permute-start(bf16[64,768]{1,0:T(8,128)(2,1)S(1)} %get-tuple-element.137), channel_id=1, source_target_pairs={{0,14},{1,15},{2,12},{3,13},{4,10},{5,11},{6,8},{7,9},{8,6},{9,7},... | collective-permute-start | bytes 294920 | tf_op jit(solution)/shard_map/ppermute | solution.py:242
  82.7 9.6 %collective-permute-start.30 = (bf16[64,768]{1,0:T(8,128)(2,1)S(1)}, bf16[64,768]{1,0:T(8,128)(2,1)S(1)}, u32[]{:S(2)}, u32[]{:S(2)}) collective-permute-start(bf16[64,768]{1,0:T(8,128)(2,1)S(1)} %get-tuple-element.138), channel_id=1, source_target_pairs={{0,10},{1,11},{2,8},{3,9},{4,14},{5,15},{6,12},{7,13},{8,2},{9,3},... | collective-permute-start | bytes 294920 | tf_op jit(solution)/shard_map/ppermute | solution.py:242
  82.7 9.6 %collective-permute-start.31 = (bf16[64,768]{1,0:T(8,128)(2,1)S(1)}, bf16[64,768]{1,0:T(8,128)(2,1)S(1)}, u32[]{:S(2)}, u32[]{:S(2)}) collective-permute-start(bf16[64,768]{1,0:T(8,128)(2,1)S(1)} %get-tuple-element.139), channel_id=1, source_target_pairs={{0,6},{1,7},{2,4},{3,5},{4,2},{5,3},{6,0},{7,1},{8,14},{9,15},{10,... | collective-permute-start | bytes 294920 | tf_op jit(solution)/shard_map/ppermute | solution.py:242
  85.9 8.4 %collective-permute-start.32 = (bf16[64,768]{1,0:T(8,128)(2,1)S(1)}, bf16[64,768]{1,0:T(8,128)(2,1)S(1)}, u32[]{:S(2)}, u32[]{:S(2)}) collective-permute-start(bf16[64,768]{1,0:T(8,128)(2,1)S(1)} %get-tuple-element.140), channel_id=1, source_target_pairs={{0,2},{1,3},{2,0},{3,1},{4,6},{5,7},{6,4},{7,5},{8,10},{9,11},{10,... | collective-permute-start | bytes 294920 | tf_op jit(solution)/shard_map/ppermute | solution.py:242
  (22 other events, 134.3 us)

commit v6 on v5

--- a/solution.py
+++ b/solution.py
@@ -945,7 +945,7 @@
     )
     parts1 = split_sum(keep1, swap_each(give1, 1), rows)
     mixed, squares = close(
-        base, [swap_pg(parts1[z], 4 * z + 2, n_pg) for z in reversed(range(zs))]
+        base, [swap_pg(parts1[z], 4 * z + 2, n_pg) for z in (0, 3, 2, 1)]
     )
     return last_norm(mixed, squares, swap_kv(squares), norm_gain_out)
 

time: 99.4 us -> 97.9 us (0.985)
  waiting for transfers between devices: 37.2 us -> 35.6 us
    ppermute x23, waiting for transfers between devices: 24.4 us -> 22.9 us  [swap_pg(): return lax.ppermute(x, 'pg', [(i, i ^ mask) for i in range(n)])]
  transfers between devices with their start and end apart: 35 -> 35, of which waited for: 20 -> 19; matrix products, arithmetic and copies ran while one was open for 1% -> 1% of each run, Pallas kernels for 13% -> 13%
where the time goes in v6:
time: 97.9 us; the launch traced here: 97.6 us
  starting transfers between devices  42.4 us (43%)
  waiting for transfers between devices  35.6 us (36%)
  Pallas kernels  16.3 us (17%)
  local copies, waits for them, and re-layouts  2.36 us (2%)
    ppermute x23, waiting for transfers between devices, swap_pg(): return lax.ppermute(x, 'pg', [(i, i ^ mask) for i in range(n)])  22.9 us
    ppermute x23, starting transfers between devices, swap_pg(): return lax.ppermute(x, 'pg', [(i, i ^ mask) for i in range(n)])  20.8 us
    pallas_call x24, Pallas kernels, run(): pl.pallas_call(body, out_shape=[jax.ShapeDtypeStruct(s, d) for s, d in ou...  16.3 us
    ppermute x11, starting transfers between devices, swap_kv(): return lax.ppermute(x, 'kv', [(0, 1), (1, 0)])  14 us
    ppermute x11, waiting for transfers between devices, swap_kv(): return lax.ppermute(x, 'kv', [(0, 1), (1, 0)])  8.86 us
    all_to_all x1, starting transfers between devices, fast_local(): sent = lax.all_to_all(packed, 'pg', split_axis=0, concat_axis=0, tiled=True)  7.53 us
    all_to_all x1, waiting for transfers between devices, fast_local(): sent = lax.all_to_all(packed, 'pg', split_axis=0, concat_axis=0, tiled=True)  3.86 us
  transfers between devices with their start and end apart: 35, of which 19 were waited for; matrix products, arithmetic and copies ran while one was open for 1% of the time, Pallas kernels for 13%

profile of v6, /device:TPU:0, one launch (start us, length us, event | category | flops | bytes accessed | tf_op | source)
XLA Modules:
  0.0 97.6 jit_solution(4926007334120483139)
XLA Ops:
  0.0 1.6 %shard_map.136 = bf16[16,56,128]{2,1,0:T(8,128)(2,1)} custom-call(bf16[4,768]{1,0:T(4,128)(2,1)} %q_hbm.1, bf16[64,768]{1,0:T(8,128)(2,1)} %res.1, s32[8,64]{1,0:T(8,128)} %bitcast.6, f32[8,64]{1,0:T(8,128)} %bitcast.7), custom_call_target="tpu_custom_call" | custom-call | flops 1000000000 | bytes 1 | tf_op jit(solution)/shard_map/pallas_call | solution.py:202
  1.7 7.5 %all-to-all-start = ((bf16[16,56,128]{2,1,0:T(8,128)(2,1)}), bf16[16,56,128]{2,1,0:T(8,128)(2,1)S(1)}, u32[]{:S(2)}, u32[]{:S(2)}) async-start(bf16[16,56,128]{2,1,0:T(8,128)(2,1)} %shard_map.136), calls=%async_computation | async-start | bytes 458752 | tf_op jit(solution)/shard_map/all_to_all | solution.py:866
  9.2 1.7 %copy-done.2 = bf16[768,1536]{1,0:T(8,128)(2,1)S(1)} copy-done((bf16[768,1536]{1,0:T(8,128)(2,1)S(1)}, bf16[768,1536]{1,0:T(8,128)(2,1)}, u32[]{:S(2)}) %copy-start.2) | copy-done | bytes 2359320
  11.5 1.6 %collective-permute-start = (bf16[64,768]{1,0:T(8,128)(2,1)S(1)}, bf16[64,768]{1,0:T(8,128)(2,1)S(1)}, u32[]{:S(2)}, u32[]{:S(2)}) collective-permute-start(bf16[64,768]{1,0:T(8,128)(2,1)S(1)} %get-tuple-element.76.sent_ref), channel_id=1, source_target_pairs={{0,16},{16,0},{1,17},{17,1},{2,18},{18,2},{3,19},{19,3},{4,20},{20... | collective-permute-start | bytes 294920 | tf_op jit(solution)/shard_map/ppermute | solution.py:238
  14.9 3.9 %all-to-all-done.sent_ref = bf16[16,56,128]{2,1,0:T(8,128)(2,1)S(1)} async-done(((bf16[16,56,128]{2,1,0:T(8,128)(2,1)}), bf16[16,56,128]{2,1,0:T(8,128)(2,1)S(1)}, u32[]{:S(2)}, u32[]{:S(2)}) %all-to-all-start) | async-done | bytes 229408 | tf_op jit(solution)/shard_map/all_to_all | solution.py:866
  18.7 1.7 %shard_map.138.pages_ref = bf16[16,1024]{1,0:T(8,128)(2,1)S(1)} custom-call(s32[256,1]{1,0:T(8,128)S(1)} %broadcast_in_dim_reshape.9.owner_col, s32[256,1]{1,0:T(8,128)S(1)} %broadcast_in_dim_reshape.10.live_col, bf16[16,56,128]{2,1,0:T(8,128)(2,1)S(1)} %all-to-all-done.sent_ref, bf16[16,4,128,128]{3,2,1,0:T(8,128)(2,1)S(1)} %copy-done.4), custom_call_target="tpu_custom_call" | custom-call | flops 1000000000 | bytes 1 | tf_op jit(solution)/shard_map/pallas_call | solution.py:202
  20.7 2.3 %collective-permute-start.3 = (bf16[64,1024]{1,0:T(8,128)(2,1)S(1)}, bf16[64,1024]{1,0:T(8,128)(2,1)S(1)}, u32[]{:S(2)}, u32[]{:S(2)}) collective-permute-start(bf16[64,1024]{1,0:T(8,128)(2,1)S(1)} %get-tuple-element.81.refs_0_), channel_id=1, source_target_pairs={{0,8},{1,9},{2,10},{3,11},{4,12},{5,13},{6,14},{7,15},{8,0},{9,1},... | collective-permute-start | bytes 393224 | tf_op jit(solution)/shard_map/ppermute | solution.py:242
  23.0 2.0 %collective-permute-start.4 = (bf16[64,1024]{1,0:T(8,128)(2,1)S(1)}, bf16[64,1024]{1,0:T(8,128)(2,1)S(1)}, u32[]{:S(2)}, u32[]{:S(2)}) collective-permute-start(bf16[64,1024]{1,0:T(8,128)(2,1)S(1)} %get-tuple-element.81.refs_0_), channel_id=1, source_target_pairs={{0,12},{1,13},{2,14},{3,15},{4,8},{5,9},{6,10},{7,11},{8,4},{9,5},... | collective-permute-start | bytes 393224 | tf_op jit(solution)/shard_map/ppermute | solution.py:242
  26.0 2.4 %shard_map.141 = (bf16[3,768,1024]{2,1,0:T(8,128)(2,1)S(1)}, bf16[3,512,768]{2,1,0:T(8,128)(2,1)S(1)}) custom-call(bf16[3,768,1024]{2,1,0:T(8,128)(2,1)} %refs_0_, bf16[3,512,768]{2,1,0:T(8,128)(2,1)S(1)} %copy-done), custom_call_target="tpu_custom_call" | custom-call | flops 1000000000 | bytes 1 | tf_op jit(solution)/shard_map/pallas_call | solution.py:202
  28.5 5.1 %collective-permute-done.3.refs_2_ = bf16[64,1024]{1,0:T(8,128)(2,1)S(1)} collective-permute-done((bf16[64,1024]{1,0:T(8,128)(2,1)S(1)}, bf16[64,1024]{1,0:T(8,128)(2,1)S(1)}, u32[]{:S(2)}, u32[]{:S(2)}) %collective-permute-start.3) | collective-permute-done | bytes 131104 | tf_op jit(solution)/shard_map/ppermute | solution.py:242
  36.1 1.5 %collective-permute-start.14 = (bf16[3,128,512]{2,1,0:T(8,128)(2,1)S(1)}, bf16[3,128,512]{2,1,0:T(8,128)(2,1)S(1)}, u32[]{:S(2)}, u32[]{:S(2)}) collective-permute-start(bf16[3,128,512]{2,1,0:T(8,128)(2,1)S(1)} %get-tuple-element.98), channel_id=1, source_target_pairs={{0,16},{16,0},{1,17},{17,1},{2,18},{18,2},{3,19},{19,3},{4,20},{20... | collective-permute-start | bytes 1179656 | tf_op jit(solution)/shard_map/ppermute | solution.py:238
  43.1 1.5 %collective-permute-start.10 = (bf16[64,768]{1,0:T(8,128)(2,1)S(1)}, bf16[64,768]{1,0:T(8,128)(2,1)S(1)}, u32[]{:S(2)}, u32[]{:S(2)}) collective-permute-start(bf16[64,768]{1,0:T(8,128)(2,1)S(1)} %get-tuple-element.96.sent_ref), channel_id=1, source_target_pairs={{0,16},{16,0},{1,17},{17,1},{2,18},{18,2},{3,19},{19,3},{4,20},{20... | collective-permute-start | bytes 294920 | tf_op jit(solution)/shard_map/ppermute | solution.py:238
  45.2 2.9 %collective-permute-done.14.refs_0_ = bf16[3,128,512]{2,1,0:T(8,128)(2,1)S(1)} collective-permute-done((bf16[3,128,512]{2,1,0:T(8,128)(2,1)S(1)}, bf16[3,128,512]{2,1,0:T(8,128)(2,1)S(1)}, u32[]{:S(2)}, u32[]{:S(2)}) %collective-permute-start.14) | collective-permute-done | bytes 393248 | tf_op jit(solution)/shard_map/ppermute | solution.py:238
  57.1 1.6 %collective-permute-start.24 = (bf16[3,128,512]{2,1,0:T(8,128)(2,1)S(1)}, bf16[3,128,512]{2,1,0:T(8,128)(2,1)S(1)}, u32[]{:S(2)}, u32[]{:S(2)}) collective-permute-start(bf16[3,128,512]{2,1,0:T(8,128)(2,1)S(1)} %get-tuple-element.125), channel_id=1, source_target_pairs={{0,16},{16,0},{1,17},{17,1},{2,18},{18,2},{3,19},{19,3},{4,20},{20... | collective-permute-start | bytes 1179656 | tf_op jit(solution)/shard_map/ppermute | solution.py:238
  59.2 1.8 %collective-permute-done.16.got_ref = bf16[3,32,1024]{2,1,0:T(8,128)(2,1)S(1)} collective-permute-done((bf16[3,32,1024]{2,1,0:T(8,128)(2,1)S(1)}, bf16[3,32,1024]{2,1,0:T(8,128)(2,1)S(1)}, u32[]{:S(2)}, u32[]{:S(2)}) %collective-permute-start.16) | collective-permute-done | bytes 196640 | tf_op jit(solution)/shard_map/ppermute | solution.py:238
  64.3 2.1 %collective-permute-start.21 = (bf16[64,768]{1,0:T(8,128)(2,1)S(1)}, bf16[64,768]{1,0:T(8,128)(2,1)S(1)}, u32[]{:S(2)}, u32[]{:S(2)}) collective-permute-start(bf16[64,768]{1,0:T(8,128)(2,1)S(1)} %get-tuple-element.122), channel_id=1, source_target_pairs={{0,12},{1,13},{2,14},{3,15},{4,8},{5,9},{6,10},{7,11},{8,4},{9,5},... | collective-permute-start | bytes 294920 | tf_op jit(solution)/shard_map/ppermute | solution.py:242
  66.4 2.0 %collective-permute-start.22 = (bf16[64,768]{1,0:T(8,128)(2,1)S(1)}, bf16[64,768]{1,0:T(8,128)(2,1)S(1)}, u32[]{:S(2)}, u32[]{:S(2)}) collective-permute-start(bf16[64,768]{1,0:T(8,128)(2,1)S(1)} %get-tuple-element.123), channel_id=1, source_target_pairs={{0,8},{1,9},{2,10},{3,11},{4,12},{5,13},{6,14},{7,15},{8,0},{9,1},... | collective-permute-start | bytes 294920 | tf_op jit(solution)/shard_map/ppermute | solution.py:242
  71.9 5.5 %collective-permute-done.22.refs_2_ = bf16[64,768]{1,0:T(8,128)(2,1)S(1)} collective-permute-done((bf16[64,768]{1,0:T(8,128)(2,1)S(1)}, bf16[64,768]{1,0:T(8,128)(2,1)S(1)}, u32[]{:S(2)}, u32[]{:S(2)}) %collective-permute-start.22) | collective-permute-done | bytes 98336 | tf_op jit(solution)/shard_map/ppermute | solution.py:242
  81.2 2.3 %collective-permute-start.30 = (bf16[64,768]{1,0:T(8,128)(2,1)S(1)}, bf16[64,768]{1,0:T(8,128)(2,1)S(1)}, u32[]{:S(2)}, u32[]{:S(2)}) collective-permute-start(bf16[64,768]{1,0:T(8,128)(2,1)S(1)} %get-tuple-element.138), channel_id=1, source_target_pairs={{0,14},{1,15},{2,12},{3,13},{4,10},{5,11},{6,8},{7,9},{8,6},{9,7},... | collective-permute-start | bytes 294920 | tf_op jit(solution)/shard_map/ppermute | solution.py:242
  83.6 3.5 %collective-permute-start.32 = (bf16[64,768]{1,0:T(8,128)(2,1)S(1)}, bf16[64,768]{1,0:T(8,128)(2,1)S(1)}, u32[]{:S(2)}, u32[]{:S(2)}) collective-permute-start(bf16[64,768]{1,0:T(8,128)(2,1)S(1)} %get-tuple-element.140), channel_id=1, source_target_pairs={{0,6},{1,7},{2,4},{3,5},{4,2},{5,3},{6,0},{7,1},{8,14},{9,15},{10,... | collective-permute-start | bytes 294920 | tf_op jit(solution)/shard_map/ppermute | solution.py:242
  87.1 2.6 %collective-permute-done.30.refs_1_ = bf16[64,768]{1,0:T(8,128)(2,1)S(1)} collective-permute-done((bf16[64,768]{1,0:T(8,128)(2,1)S(1)}, bf16[64,768]{1,0:T(8,128)(2,1)S(1)}, u32[]{:S(2)}, u32[]{:S(2)}) %collective-permute-start.30) | collective-permute-done | bytes 98336 | tf_op jit(solution)/shard_map/ppermute | solution.py:242
  89.7 3.1 %collective-permute-done.31.refs_2_ = bf16[64,768]{1,0:T(8,128)(2,1)S(1)} collective-permute-done((bf16[64,768]{1,0:T(8,128)(2,1)S(1)}, bf16[64,768]{1,0:T(8,128)(2,1)S(1)}, u32[]{:S(2)}, u32[]{:S(2)}) %collective-permute-start.31) | collective-permute-done | bytes 98336 | tf_op jit(solution)/shard_map/ppermute | solution.py:242
  92.9 1.6 %collective-permute-start.33 = (f32[64,128]{1,0:T(8,128)S(1)}, f32[64,128]{1,0:T(8,128)S(1)}, u32[]{:S(2)}, u32[]{:S(2)}) collective-permute-start(f32[64,128]{1,0:T(8,128)S(1)} %get-tuple-element.142.near_ref), channel_id=1, source_target_pairs={{0,16},{16,0},{1,17},{17,1},{2,18},{18,2},{3,19},{19,3},{4,20},{20... | collective-permute-start | bytes 98312 | tf_op jit(solution)/shard_map/ppermute | solution.py:238
  94.5 2.4 %collective-permute-done.33.far_ref = f32[64,128]{1,0:T(8,128)S(1)} collective-permute-done((f32[64,128]{1,0:T(8,128)S(1)}, f32[64,128]{1,0:T(8,128)S(1)}, u32[]{:S(2)}, u32[]{:S(2)}) %collective-permute-start.33) | collective-permute-done | bytes 32800 | tf_op jit(solution)/shard_map/ppermute | solution.py:238
  (108 shorter events, 32.9 us)
Async XLA Ops:
  1.7 17.1 %all-to-all-start = ((bf16[16,56,128]{2,1,0:T(8,128)(2,1)}), bf16[16,56,128]{2,1,0:T(8,128)(2,1)S(1)}, u32[]{:S(2)}, u32[]{:S(2)}) async-start(bf16[16,56,128]{2,1,0:T(8,128)(2,1)} %shard_map.136), calls=%async_computation | async-start | bytes 458752 | tf_op jit(solution)/shard_map/all_to_all | solution.py:866
  11.5 8.9 %collective-permute-start = (bf16[64,768]{1,0:T(8,128)(2,1)S(1)}, bf16[64,768]{1,0:T(8,128)(2,1)S(1)}, u32[]{:S(2)}, u32[]{:S(2)}) collective-permute-start(bf16[64,768]{1,0:T(8,128)(2,1)S(1)} %get-tuple-element.76.sent_ref), channel_id=1, source_target_pairs={{0,16},{16,0},{1,17},{17,1},{2,18},{18,2},{3,19},{19,3},{4,20},{20... | collective-permute-start | bytes 294920 | tf_op jit(solution)/shard_map/ppermute | solution.py:238
  13.0 7.4 %collective-permute-start.1 = (bf16[64,768]{1,0:T(8,128)(2,1)S(1)}, bf16[64,768]{1,0:T(8,128)(2,1)S(1)}, u32[]{:S(2)}, u32[]{:S(2)}) collective-permute-start(bf16[64,768]{1,0:T(8,128)(2,1)S(1)} %get-tuple-element.77), channel_id=1, source_target_pairs={{0,16},{16,0},{1,17},{17,1},{2,18},{18,2},{3,19},{19,3},{4,20},{20... | collective-permute-start | bytes 294920 | tf_op jit(solution)/shard_map/ppermute | solution.py:238
  20.6 7.9 %collective-permute-start.2 = (bf16[64,1024]{1,0:T(8,128)(2,1)S(1)}, bf16[64,1024]{1,0:T(8,128)(2,1)S(1)}, u32[]{:S(2)}, u32[]{:S(2)}) collective-permute-start(bf16[64,1024]{1,0:T(8,128)(2,1)S(1)} %get-tuple-element.81.refs_0_), channel_id=1, source_target_pairs={{0,4},{1,5},{2,6},{3,7},{4,0},{5,1},{6,2},{7,3},{8,12},{9,13},{10,... | collective-permute-start | bytes 393224 | tf_op jit(solution)/shard_map/ppermute | solution.py:242
  20.7 12.9 %collective-permute-start.3 = (bf16[64,1024]{1,0:T(8,128)(2,1)S(1)}, bf16[64,1024]{1,0:T(8,128)(2,1)S(1)}, u32[]{:S(2)}, u32[]{:S(2)}) collective-permute-start(bf16[64,1024]{1,0:T(8,128)(2,1)S(1)} %get-tuple-element.81.refs_0_), channel_id=1, source_target_pairs={{0,8},{1,9},{2,10},{3,11},{4,12},{5,13},{6,14},{7,15},{8,0},{9,1},... | collective-permute-start | bytes 393224 | tf_op jit(solution)/shard_map/ppermute | solution.py:242
  23.0 10.6 %collective-permute-start.4 = (bf16[64,1024]{1,0:T(8,128)(2,1)S(1)}, bf16[64,1024]{1,0:T(8,128)(2,1)S(1)}, u32[]{:S(2)}, u32[]{:S(2)}) collective-permute-start(bf16[64,1024]{1,0:T(8,128)(2,1)S(1)} %get-tuple-element.81.refs_0_), channel_id=1, source_target_pairs={{0,12},{1,13},{2,14},{3,15},{4,8},{5,9},{6,10},{7,11},{8,4},{9,5},... | collective-permute-start | bytes 393224 | tf_op jit(solution)/shard_map/ppermute | solution.py:242
  34.2 5.5 %collective-permute-start.5 = (bf16[64,1024]{1,0:T(8,128)(2,1)S(1)}, bf16[64,1024]{1,0:T(8,128)(2,1)S(1)}, u32[]{:S(2)}, u32[]{:S(2)}) collective-permute-start(bf16[64,1024]{1,0:T(8,128)(2,1)S(1)} %get-tuple-element.90.refs_0_), channel_id=1, source_target_pairs={{0,2},{1,3},{2,0},{3,1},{4,6},{5,7},{6,4},{7,5},{8,10},{9,11},{10,... | collective-permute-start | bytes 393224 | tf_op jit(solution)/shard_map/ppermute | solution.py:242
  36.1 12.0 %collective-permute-start.14 = (bf16[3,128,512]{2,1,0:T(8,128)(2,1)S(1)}, bf16[3,128,512]{2,1,0:T(8,128)(2,1)S(1)}, u32[]{:S(2)}, u32[]{:S(2)}) collective-permute-start(bf16[3,128,512]{2,1,0:T(8,128)(2,1)S(1)} %get-tuple-element.98), channel_id=1, source_target_pairs={{0,16},{16,0},{1,17},{17,1},{2,18},{18,2},{3,19},{19,3},{4,20},{20... | collective-permute-start | bytes 1179656 | tf_op jit(solution)/shard_map/ppermute | solution.py:238
  39.7 10.1 %collective-permute-start.12 = (bf16[128,768]{1,0:T(8,128)(2,1)S(1)}, bf16[128,768]{1,0:T(8,128)(2,1)S(1)}, u32[]{:S(2)}, u32[]{:S(2)}) collective-permute-start(bf16[128,768]{1,0:T(8,128)(2,1)S(1)} %get-tuple-element.91.refs_0_), channel_id=1, source_target_pairs={{0,2},{1,3},{2,0},{3,1},{4,6},{5,7},{6,4},{7,5},{8,10},{9,11},{10,... | collective-permute-start | bytes 589832 | tf_op jit(solution)/shard_map/ppermute | solution.py:242
  40.5 10.7 %collective-permute-start.13 = (bf16[128,768]{1,0:T(8,128)(2,1)S(1)}, bf16[128,768]{1,0:T(8,128)(2,1)S(1)}, u32[]{:S(2)}, u32[]{:S(2)}) collective-permute-start(bf16[128,768]{1,0:T(8,128)(2,1)S(1)} %get-tuple-element.92.refs_1_), channel_id=1, source_target_pairs={{0,2},{1,3},{2,0},{3,1},{4,6},{5,7},{6,4},{7,5},{8,10},{9,11},{10,... | collective-permute-start | bytes 589832 | tf_op jit(solution)/shard_map/ppermute | solution.py:242
  43.1 8.6 %collective-permute-start.10 = (bf16[64,768]{1,0:T(8,128)(2,1)S(1)}, bf16[64,768]{1,0:T(8,128)(2,1)S(1)}, u32[]{:S(2)}, u32[]{:S(2)}) collective-permute-start(bf16[64,768]{1,0:T(8,128)(2,1)S(1)} %get-tuple-element.96.sent_ref), channel_id=1, source_target_pairs={{0,16},{16,0},{1,17},{17,1},{2,18},{18,2},{3,19},{19,3},{4,20},{20... | collective-permute-start | bytes 294920 | tf_op jit(solution)/shard_map/ppermute | solution.py:238
  44.6 7.7 %collective-permute-start.11 = (bf16[64,768]{1,0:T(8,128)(2,1)S(1)}, bf16[64,768]{1,0:T(8,128)(2,1)S(1)}, u32[]{:S(2)}, u32[]{:S(2)}) collective-permute-start(bf16[64,768]{1,0:T(8,128)(2,1)S(1)} %get-tuple-element.97), channel_id=1, source_target_pairs={{0,16},{16,0},{1,17},{17,1},{2,18},{18,2},{3,19},{19,3},{4,20},{20... | collective-permute-start | bytes 294920 | tf_op jit(solution)/shard_map/ppermute | solution.py:238
  48.3 7.8 %collective-permute-start.15 = (bf16[3,128,256]{2,1,0:T(8,128)(2,1)S(1)}, bf16[3,128,256]{2,1,0:T(8,128)(2,1)S(1)}, u32[]{:S(2)}, u32[]{:S(2)}) collective-permute-start(bf16[3,128,256]{2,1,0:T(8,128)(2,1)S(1)} %shard_map.146.refs_0_), channel_id=1, source_target_pairs={{0,16},{16,0},{1,17},{17,1},{2,18},{18,2},{3,19},{19,3},{4,20},{20... | collective-permute-start | bytes 589832 | tf_op jit(solution)/shard_map/ppermute | solution.py:238
  53.5 7.6 %collective-permute-start.16 = (bf16[3,32,1024]{2,1,0:T(8,128)(2,1)S(1)}, bf16[3,32,1024]{2,1,0:T(8,128)(2,1)S(1)}, u32[]{:S(2)}, u32[]{:S(2)}) collective-permute-start(bf16[3,32,1024]{2,1,0:T(8,128)(2,1)S(1)} %get-tuple-element.109), channel_id=1, source_target_pairs={{0,16},{16,0},{1,17},{17,1},{2,18},{18,2},{3,19},{19,3},{4,20},{20... | collective-permute-start | bytes 589832 | tf_op jit(solution)/shard_map/ppermute | solution.py:238
  57.1 11.6 %collective-permute-start.24 = (bf16[3,128,512]{2,1,0:T(8,128)(2,1)S(1)}, bf16[3,128,512]{2,1,0:T(8,128)(2,1)S(1)}, u32[]{:S(2)}, u32[]{:S(2)}) collective-permute-start(bf16[3,128,512]{2,1,0:T(8,128)(2,1)S(1)} %get-tuple-element.125), channel_id=1, source_target_pairs={{0,16},{16,0},{1,17},{17,1},{2,18},{18,2},{3,19},{19,3},{4,20},{20... | collective-permute-start | bytes 1179656 | tf_op jit(solution)/shard_map/ppermute | solution.py:238
  64.3 7.6 %collective-permute-start.21 = (bf16[64,768]{1,0:T(8,128)(2,1)S(1)}, bf16[64,768]{1,0:T(8,128)(2,1)S(1)}, u32[]{:S(2)}, u32[]{:S(2)}) collective-permute-start(bf16[64,768]{1,0:T(8,128)(2,1)S(1)} %get-tuple-element.122), channel_id=1, source_target_pairs={{0,12},{1,13},{2,14},{3,15},{4,8},{5,9},{6,10},{7,11},{8,4},{9,5},... | collective-permute-start | bytes 294920 | tf_op jit(solution)/shard_map/ppermute | solution.py:242
  66.4 11.0 %collective-permute-start.22 = (bf16[64,768]{1,0:T(8,128)(2,1)S(1)}, bf16[64,768]{1,0:T(8,128)(2,1)S(1)}, u32[]{:S(2)}, u32[]{:S(2)}) collective-permute-start(bf16[64,768]{1,0:T(8,128)(2,1)S(1)} %get-tuple-element.123), channel_id=1, source_target_pairs={{0,8},{1,9},{2,10},{3,11},{4,12},{5,13},{6,14},{7,15},{8,0},{9,1},... | collective-permute-start | bytes 294920 | tf_op jit(solution)/shard_map/ppermute | solution.py:242
  68.4 9.0 %collective-permute-start.23 = (bf16[64,768]{1,0:T(8,128)(2,1)S(1)}, bf16[64,768]{1,0:T(8,128)(2,1)S(1)}, u32[]{:S(2)}, u32[]{:S(2)}) collective-permute-start(bf16[64,768]{1,0:T(8,128)(2,1)S(1)} %get-tuple-element.124), channel_id=1, source_target_pairs={{0,4},{1,5},{2,6},{3,7},{4,0},{5,1},{6,2},{7,3},{8,12},{9,13},{10,... | collective-permute-start | bytes 294920 | tf_op jit(solution)/shard_map/ppermute | solution.py:242
  68.9 8.7 %collective-permute-start.25 = (bf16[3,64,256]{2,1,0:T(8,128)(2,1)S(1)}, bf16[3,64,256]{2,1,0:T(8,128)(2,1)S(1)}, u32[]{:S(2)}, u32[]{:S(2)}) collective-permute-start(bf16[3,64,256]{2,1,0:T(8,128)(2,1)S(1)} %get-tuple-element.127.refs_0_), channel_id=1, source_target_pairs={{0,16},{16,0},{1,17},{17,1},{2,18},{18,2},{3,19},{19,3},{4,20},{20... | collective-permute-start | bytes 294920 | tf_op jit(solution)/shard_map/ppermute | solution.py:238
  70.4 7.2 %collective-permute-start.26 = (bf16[3,64,256]{2,1,0:T(8,128)(2,1)S(1)}, bf16[3,64,256]{2,1,0:T(8,128)(2,1)S(1)}, u32[]{:S(2)}, u32[]{:S(2)}) collective-permute-start(bf16[3,64,256]{2,1,0:T(8,128)(2,1)S(1)} %get-tuple-element.128.refs_1_), channel_id=1, source_target_pairs={{0,16},{16,0},{1,17},{17,1},{2,18},{18,2},{3,19},{19,3},{4,20},{20... | collective-permute-start | bytes 294920 | tf_op jit(solution)/shard_map/ppermute | solution.py:238
  80.3 6.8 %collective-permute-start.29 = (bf16[64,768]{1,0:T(8,128)(2,1)S(1)}, bf16[64,768]{1,0:T(8,128)(2,1)S(1)}, u32[]{:S(2)}, u32[]{:S(2)}) collective-permute-start(bf16[64,768]{1,0:T(8,128)(2,1)S(1)} %get-tuple-element.137), channel_id=1, source_target_pairs={{0,2},{1,3},{2,0},{3,1},{4,6},{5,7},{6,4},{7,5},{8,10},{9,11},{10,... | collective-permute-start | bytes 294920 | tf_op jit(solution)/shard_map/ppermute | solution.py:242
  81.2 8.5 %collective-permute-start.30 = (bf16[64,768]{1,0:T(8,128)(2,1)S(1)}, bf16[64,768]{1,0:T(8,128)(2,1)S(1)}, u32[]{:S(2)}, u32[]{:S(2)}) collective-permute-start(bf16[64,768]{1,0:T(8,128)(2,1)S(1)} %get-tuple-element.138), channel_id=1, source_target_pairs={{0,14},{1,15},{2,12},{3,13},{4,10},{5,11},{6,8},{7,9},{8,6},{9,7},... | collective-permute-start | bytes 294920 | tf_op jit(solution)/shard_map/ppermute | solution.py:242
  83.5 9.3 %collective-permute-start.31 = (bf16[64,768]{1,0:T(8,128)(2,1)S(1)}, bf16[64,768]{1,0:T(8,128)(2,1)S(1)}, u32[]{:S(2)}, u32[]{:S(2)}) collective-permute-start(bf16[64,768]{1,0:T(8,128)(2,1)S(1)} %get-tuple-element.139), channel_id=1, source_target_pairs={{0,10},{1,11},{2,8},{3,9},{4,14},{5,15},{6,12},{7,13},{8,2},{9,3},... | collective-permute-start | bytes 294920 | tf_op jit(solution)/shard_map/ppermute | solution.py:242
  83.6 9.2 %collective-permute-start.32 = (bf16[64,768]{1,0:T(8,128)(2,1)S(1)}, bf16[64,768]{1,0:T(8,128)(2,1)S(1)}, u32[]{:S(2)}, u32[]{:S(2)}) collective-permute-start(bf16[64,768]{1,0:T(8,128)(2,1)S(1)} %get-tuple-element.140), channel_id=1, source_target_pairs={{0,6},{1,7},{2,4},{3,5},{4,2},{5,3},{6,0},{7,1},{8,14},{9,15},{10,... | collective-permute-start | bytes 294920 | tf_op jit(solution)/shard_map/ppermute | solution.py:242
  (22 other events, 132.8 us)

commit v7 on v6

--- a/solution.py
+++ b/solution.py
@@ -811,16 +811,24 @@
         folded = total[:, 0:128]
         for n in range(1, cols // 128):
             folded = folded + total[:, n * 128 : (n + 1) * 128]
-        squares[...] = folded
-
-    return call(body, [((rows, cols), F32), ((rows, 128), F32)])(base, *parts)
+        squares[...] = lax.dot_general(
+            jnp.ones((8, 128), F32),
+            folded,
+            (((1,), (1,)), ((), ())),
+            precision=HIGH,
+            preferred_element_type=F32,
+        )
+
+    return call(body, [((rows, cols), F32), ((8, rows), F32)])(base, *parts)
 
 
 def last_norm(mixed, near, far, gain):
     rows, cols = mixed.shape
 
     def body(mixed_ref, near_ref, far_ref, gain_ref, out):
-        squares = jnp.sum(near_ref[...] + far_ref[...], axis=1, keepdims=True)
+        both = near_ref[0:1, :] + far_ref[0:1, :]
+        eye = iota((rows, rows), 0) == iota((rows, rows), 1)
+        squares = jnp.sum(jnp.where(eye, both, 0.0), axis=1, keepdims=True)
         out[...] = (
             mixed_ref[...] * lax.rsqrt(squares / (2 * cols) + EPSILON) * gain_ref[...]
         ).astype(BF16)
@@ -931,7 +939,7 @@
     xs1, *out1 = gathered([1, 3], after([across, across_core], [dec_units, far0]), (slots,), dec_normed)
     got1 = swap_units(out1)
     own1 = own_products(xs1, w_units, me_kv)
-    decode = decode_experts(dec_own, after(dec_got, own1), w_rows, dec_gates)
+    decode = decode_experts(dec_own, after(dec_got, out1), w_rows, dec_gates)
     keep0, *give0 = down(
         near0, after(far0, decode), w_rows, [0, 2], picks, gates, me_kv, rows, own_req, decode
     )

time: 97.9 us -> 97.7 us (level)
  no operation moved by 1% of the time
where the time goes in v7:
time: 97.7 us; the launch traced here: 97.4 us
  starting transfers between devices  42.3 us (43%)
  waiting for transfers between devices  35.3 us (36%)
  Pallas kernels  16.4 us (17%)
  local copies, waits for them, and re-layouts  2.36 us (2%)
    ppermute x23, waiting for transfers between devices, swap_pg(): return lax.ppermute(x, 'pg', [(i, i ^ mask) for i in range(n)])  22.3 us
    ppermute x23, starting transfers between devices, swap_pg(): return lax.ppermute(x, 'pg', [(i, i ^ mask) for i in range(n)])  20.8 us
    pallas_call x24, Pallas kernels, run(): pl.pallas_call(body, out_shape=[jax.ShapeDtypeStruct(s, d) for s, d in ou...  16.4 us
    ppermute x11, starting transfers between devices, swap_kv(): return lax.ppermute(x, 'kv', [(0, 1), (1, 0)])  14 us
    ppermute x11, waiting for transfers between devices, swap_kv(): return lax.ppermute(x, 'kv', [(0, 1), (1, 0)])  9.11 us
    all_to_all x1, starting transfers between devices, fast_local(): sent = lax.all_to_all(packed, 'pg', split_axis=0, concat_axis=0, tiled=True)  7.53 us
    all_to_all x1, waiting for transfers between devices, fast_local(): sent = lax.all_to_all(packed, 'pg', split_axis=0, concat_axis=0, tiled=True)  3.86 us
  transfers between devices with their start and end apart: 35, of which 19 were waited for; matrix products, arithmetic and copies ran while one was open for 1% of the time, Pallas kernels for 13%

profile of v7, /device:TPU:0, one launch (start us, length us, event | category | flops | bytes accessed | tf_op | source)
XLA Modules:
  0.0 97.4 jit_solution(9062871230082057312)
XLA Ops:
  0.0 1.6 %shard_map.136 = bf16[16,56,128]{2,1,0:T(8,128)(2,1)} custom-call(bf16[4,768]{1,0:T(4,128)(2,1)} %q_hbm.1, bf16[64,768]{1,0:T(8,128)(2,1)} %res.1, s32[8,64]{1,0:T(8,128)} %bitcast.6, f32[8,64]{1,0:T(8,128)} %bitcast.7), custom_call_target="tpu_custom_call" | custom-call | flops 1000000000 | bytes 1 | tf_op jit(solution)/shard_map/pallas_call | solution.py:202
  1.7 7.5 %all-to-all-start = ((bf16[16,56,128]{2,1,0:T(8,128)(2,1)}), bf16[16,56,128]{2,1,0:T(8,128)(2,1)S(1)}, u32[]{:S(2)}, u32[]{:S(2)}) async-start(bf16[16,56,128]{2,1,0:T(8,128)(2,1)} %shard_map.136), calls=%async_computation | async-start | bytes 458752 | tf_op jit(solution)/shard_map/all_to_all | solution.py:874
  9.2 1.7 %copy-done.2 = bf16[768,1536]{1,0:T(8,128)(2,1)S(1)} copy-done((bf16[768,1536]{1,0:T(8,128)(2,1)S(1)}, bf16[768,1536]{1,0:T(8,128)(2,1)}, u32[]{:S(2)}) %copy-start.2) | copy-done | bytes 2359320
  11.5 1.6 %collective-permute-start = (bf16[64,768]{1,0:T(8,128)(2,1)S(1)}, bf16[64,768]{1,0:T(8,128)(2,1)S(1)}, u32[]{:S(2)}, u32[]{:S(2)}) collective-permute-start(bf16[64,768]{1,0:T(8,128)(2,1)S(1)} %get-tuple-element.76.sent_ref), channel_id=1, source_target_pairs={{0,16},{16,0},{1,17},{17,1},{2,18},{18,2},{3,19},{19,3},{4,20},{20... | collective-permute-start | bytes 294920 | tf_op jit(solution)/shard_map/ppermute | solution.py:238
  14.9 3.9 %all-to-all-done.sent_ref = bf16[16,56,128]{2,1,0:T(8,128)(2,1)S(1)} async-done(((bf16[16,56,128]{2,1,0:T(8,128)(2,1)}), bf16[16,56,128]{2,1,0:T(8,128)(2,1)S(1)}, u32[]{:S(2)}, u32[]{:S(2)}) %all-to-all-start) | async-done | bytes 229408 | tf_op jit(solution)/shard_map/all_to_all | solution.py:874
  18.7 1.7 %shard_map.138.pages_ref = bf16[16,1024]{1,0:T(8,128)(2,1)S(1)} custom-call(s32[256,1]{1,0:T(8,128)S(1)} %broadcast_in_dim_reshape.9.owner_col, s32[256,1]{1,0:T(8,128)S(1)} %broadcast_in_dim_reshape.10.live_col, bf16[16,56,128]{2,1,0:T(8,128)(2,1)S(1)} %all-to-all-done.sent_ref, bf16[16,4,128,128]{3,2,1,0:T(8,128)(2,1)S(1)} %copy-done.4), custom_call_target="tpu_custom_call" | custom-call | flops 1000000000 | bytes 1 | tf_op jit(solution)/shard_map/pallas_call | solution.py:202
  20.7 2.3 %collective-permute-start.3 = (bf16[64,1024]{1,0:T(8,128)(2,1)S(1)}, bf16[64,1024]{1,0:T(8,128)(2,1)S(1)}, u32[]{:S(2)}, u32[]{:S(2)}) collective-permute-start(bf16[64,1024]{1,0:T(8,128)(2,1)S(1)} %get-tuple-element.81.refs_0_), channel_id=1, source_target_pairs={{0,8},{1,9},{2,10},{3,11},{4,12},{5,13},{6,14},{7,15},{8,0},{9,1},... | collective-permute-start | bytes 393224 | tf_op jit(solution)/shard_map/ppermute | solution.py:242
  23.0 2.0 %collective-permute-start.4 = (bf16[64,1024]{1,0:T(8,128)(2,1)S(1)}, bf16[64,1024]{1,0:T(8,128)(2,1)S(1)}, u32[]{:S(2)}, u32[]{:S(2)}) collective-permute-start(bf16[64,1024]{1,0:T(8,128)(2,1)S(1)} %get-tuple-element.81.refs_0_), channel_id=1, source_target_pairs={{0,12},{1,13},{2,14},{3,15},{4,8},{5,9},{6,10},{7,11},{8,4},{9,5},... | collective-permute-start | bytes 393224 | tf_op jit(solution)/shard_map/ppermute | solution.py:242
  26.0 2.4 %shard_map.141 = (bf16[3,768,1024]{2,1,0:T(8,128)(2,1)S(1)}, bf16[3,512,768]{2,1,0:T(8,128)(2,1)S(1)}) custom-call(bf16[3,768,1024]{2,1,0:T(8,128)(2,1)} %refs_0_, bf16[3,512,768]{2,1,0:T(8,128)(2,1)S(1)} %copy-done), custom_call_target="tpu_custom_call" | custom-call | flops 1000000000 | bytes 1 | tf_op jit(solution)/shard_map/pallas_call | solution.py:202
  28.5 5.1 %collective-permute-done.3.refs_2_ = bf16[64,1024]{1,0:T(8,128)(2,1)S(1)} collective-permute-done((bf16[64,1024]{1,0:T(8,128)(2,1)S(1)}, bf16[64,1024]{1,0:T(8,128)(2,1)S(1)}, u32[]{:S(2)}, u32[]{:S(2)}) %collective-permute-start.3) | collective-permute-done | bytes 131104 | tf_op jit(solution)/shard_map/ppermute | solution.py:242
  36.1 1.6 %collective-permute-start.14 = (bf16[3,128,512]{2,1,0:T(8,128)(2,1)S(1)}, bf16[3,128,512]{2,1,0:T(8,128)(2,1)S(1)}, u32[]{:S(2)}, u32[]{:S(2)}) collective-permute-start(bf16[3,128,512]{2,1,0:T(8,128)(2,1)S(1)} %get-tuple-element.98), channel_id=1, source_target_pairs={{0,16},{16,0},{1,17},{17,1},{2,18},{18,2},{3,19},{19,3},{4,20},{20... | collective-permute-start | bytes 1179656 | tf_op jit(solution)/shard_map/ppermute | solution.py:238
  43.1 1.5 %collective-permute-start.10 = (bf16[64,768]{1,0:T(8,128)(2,1)S(1)}, bf16[64,768]{1,0:T(8,128)(2,1)S(1)}, u32[]{:S(2)}, u32[]{:S(2)}) collective-permute-start(bf16[64,768]{1,0:T(8,128)(2,1)S(1)} %get-tuple-element.96.sent_ref), channel_id=1, source_target_pairs={{0,16},{16,0},{1,17},{17,1},{2,18},{18,2},{3,19},{19,3},{4,20},{20... | collective-permute-start | bytes 294920 | tf_op jit(solution)/shard_map/ppermute | solution.py:238
  45.2 2.9 %collective-permute-done.14.refs_0_ = bf16[3,128,512]{2,1,0:T(8,128)(2,1)S(1)} collective-permute-done((bf16[3,128,512]{2,1,0:T(8,128)(2,1)S(1)}, bf16[3,128,512]{2,1,0:T(8,128)(2,1)S(1)}, u32[]{:S(2)}, u32[]{:S(2)}) %collective-permute-start.14) | collective-permute-done | bytes 393248 | tf_op jit(solution)/shard_map/ppermute | solution.py:238
  48.3 1.6 %collective-permute-start.15 = (bf16[3,128,256]{2,1,0:T(8,128)(2,1)S(1)}, bf16[3,128,256]{2,1,0:T(8,128)(2,1)S(1)}, u32[]{:S(2)}, u32[]{:S(2)}) collective-permute-start(bf16[3,128,256]{2,1,0:T(8,128)(2,1)S(1)} %shard_map.146.refs_0_), channel_id=1, source_target_pairs={{0,16},{16,0},{1,17},{17,1},{2,18},{18,2},{3,19},{19,3},{4,20},{20... | collective-permute-start | bytes 589832 | tf_op jit(solution)/shard_map/ppermute | solution.py:238
  58.7 2.4 %collective-permute-done.16.got_ref = bf16[3,32,1024]{2,1,0:T(8,128)(2,1)S(1)} collective-permute-done((bf16[3,32,1024]{2,1,0:T(8,128)(2,1)S(1)}, bf16[3,32,1024]{2,1,0:T(8,128)(2,1)S(1)}, u32[]{:S(2)}, u32[]{:S(2)}) %collective-permute-start.16) | collective-permute-done | bytes 196640 | tf_op jit(solution)/shard_map/ppermute | solution.py:238
  64.3 2.1 %collective-permute-start.21 = (bf16[64,768]{1,0:T(8,128)(2,1)S(1)}, bf16[64,768]{1,0:T(8,128)(2,1)S(1)}, u32[]{:S(2)}, u32[]{:S(2)}) collective-permute-start(bf16[64,768]{1,0:T(8,128)(2,1)S(1)} %get-tuple-element.122), channel_id=1, source_target_pairs={{0,12},{1,13},{2,14},{3,15},{4,8},{5,9},{6,10},{7,11},{8,4},{9,5},... | collective-permute-start | bytes 294920 | tf_op jit(solution)/shard_map/ppermute | solution.py:242
  66.4 2.0 %collective-permute-start.22 = (bf16[64,768]{1,0:T(8,128)(2,1)S(1)}, bf16[64,768]{1,0:T(8,128)(2,1)S(1)}, u32[]{:S(2)}, u32[]{:S(2)}) collective-permute-start(bf16[64,768]{1,0:T(8,128)(2,1)S(1)} %get-tuple-element.123), channel_id=1, source_target_pairs={{0,8},{1,9},{2,10},{3,11},{4,12},{5,13},{6,14},{7,15},{8,0},{9,1},... | collective-permute-start | bytes 294920 | tf_op jit(solution)/shard_map/ppermute | solution.py:242
  69.4 1.6 %collective-permute-start.25 = (bf16[3,64,256]{2,1,0:T(8,128)(2,1)S(1)}, bf16[3,64,256]{2,1,0:T(8,128)(2,1)S(1)}, u32[]{:S(2)}, u32[]{:S(2)}) collective-permute-start(bf16[3,64,256]{2,1,0:T(8,128)(2,1)S(1)} %get-tuple-element.127.refs_0_), channel_id=1, source_target_pairs={{0,16},{16,0},{1,17},{17,1},{2,18},{18,2},{3,19},{19,3},{4,20},{20... | collective-permute-start | bytes 294920 | tf_op jit(solution)/shard_map/ppermute | solution.py:238
  71.9 5.5 %collective-permute-done.22.refs_2_ = bf16[64,768]{1,0:T(8,128)(2,1)S(1)} collective-permute-done((bf16[64,768]{1,0:T(8,128)(2,1)S(1)}, bf16[64,768]{1,0:T(8,128)(2,1)S(1)}, u32[]{:S(2)}, u32[]{:S(2)}) %collective-permute-start.22) | collective-permute-done | bytes 98336 | tf_op jit(solution)/shard_map/ppermute | solution.py:242
  81.2 2.3 %collective-permute-start.30 = (bf16[64,768]{1,0:T(8,128)(2,1)S(1)}, bf16[64,768]{1,0:T(8,128)(2,1)S(1)}, u32[]{:S(2)}, u32[]{:S(2)}) collective-permute-start(bf16[64,768]{1,0:T(8,128)(2,1)S(1)} %get-tuple-element.138), channel_id=1, source_target_pairs={{0,14},{1,15},{2,12},{3,13},{4,10},{5,11},{6,8},{7,9},{8,6},{9,7},... | collective-permute-start | bytes 294920 | tf_op jit(solution)/shard_map/ppermute | solution.py:242
  83.8 3.4 %collective-permute-start.32 = (bf16[64,768]{1,0:T(8,128)(2,1)S(1)}, bf16[64,768]{1,0:T(8,128)(2,1)S(1)}, u32[]{:S(2)}, u32[]{:S(2)}) collective-permute-start(bf16[64,768]{1,0:T(8,128)(2,1)S(1)} %get-tuple-element.140), channel_id=1, source_target_pairs={{0,6},{1,7},{2,4},{3,5},{4,2},{5,3},{6,0},{7,1},{8,14},{9,15},{10,... | collective-permute-start | bytes 294920 | tf_op jit(solution)/shard_map/ppermute | solution.py:242
  87.1 2.6 %collective-permute-done.30.refs_1_ = bf16[64,768]{1,0:T(8,128)(2,1)S(1)} collective-permute-done((bf16[64,768]{1,0:T(8,128)(2,1)S(1)}, bf16[64,768]{1,0:T(8,128)(2,1)S(1)}, u32[]{:S(2)}, u32[]{:S(2)}) %collective-permute-start.30) | collective-permute-done | bytes 98336 | tf_op jit(solution)/shard_map/ppermute | solution.py:242
  89.7 3.1 %collective-permute-done.31.refs_2_ = bf16[64,768]{1,0:T(8,128)(2,1)S(1)} collective-permute-done((bf16[64,768]{1,0:T(8,128)(2,1)S(1)}, bf16[64,768]{1,0:T(8,128)(2,1)S(1)}, u32[]{:S(2)}, u32[]{:S(2)}) %collective-permute-start.31) | collective-permute-done | bytes 98336 | tf_op jit(solution)/shard_map/ppermute | solution.py:242
  94.5 2.1 %collective-permute-done.33.far_ref = f32[8,64]{1,0:T(8,128)S(1)} collective-permute-done((f32[8,64]{1,0:T(8,128)S(1)}, f32[8,64]{1,0:T(8,128)S(1)}, u32[]{:S(2)}, u32[]{:S(2)}) %collective-permute-start.33) | collective-permute-done | bytes 2080 | tf_op jit(solution)/shard_map/ppermute | solution.py:238
  (108 shorter events, 32.7 us)
Async XLA Ops:
  1.7 17.1 %all-to-all-start = ((bf16[16,56,128]{2,1,0:T(8,128)(2,1)}), bf16[16,56,128]{2,1,0:T(8,128)(2,1)S(1)}, u32[]{:S(2)}, u32[]{:S(2)}) async-start(bf16[16,56,128]{2,1,0:T(8,128)(2,1)} %shard_map.136), calls=%async_computation | async-start | bytes 458752 | tf_op jit(solution)/shard_map/all_to_all | solution.py:874
  11.5 8.9 %collective-permute-start = (bf16[64,768]{1,0:T(8,128)(2,1)S(1)}, bf16[64,768]{1,0:T(8,128)(2,1)S(1)}, u32[]{:S(2)}, u32[]{:S(2)}) collective-permute-start(bf16[64,768]{1,0:T(8,128)(2,1)S(1)} %get-tuple-element.76.sent_ref), channel_id=1, source_target_pairs={{0,16},{16,0},{1,17},{17,1},{2,18},{18,2},{3,19},{19,3},{4,20},{20... | collective-permute-start | bytes 294920 | tf_op jit(solution)/shard_map/ppermute | solution.py:238
  13.0 7.4 %collective-permute-start.1 = (bf16[64,768]{1,0:T(8,128)(2,1)S(1)}, bf16[64,768]{1,0:T(8,128)(2,1)S(1)}, u32[]{:S(2)}, u32[]{:S(2)}) collective-permute-start(bf16[64,768]{1,0:T(8,128)(2,1)S(1)} %get-tuple-element.77), channel_id=1, source_target_pairs={{0,16},{16,0},{1,17},{17,1},{2,18},{18,2},{3,19},{19,3},{4,20},{20... | collective-permute-start | bytes 294920 | tf_op jit(solution)/shard_map/ppermute | solution.py:238
  20.6 7.9 %collective-permute-start.2 = (bf16[64,1024]{1,0:T(8,128)(2,1)S(1)}, bf16[64,1024]{1,0:T(8,128)(2,1)S(1)}, u32[]{:S(2)}, u32[]{:S(2)}) collective-permute-start(bf16[64,1024]{1,0:T(8,128)(2,1)S(1)} %get-tuple-element.81.refs_0_), channel_id=1, source_target_pairs={{0,4},{1,5},{2,6},{3,7},{4,0},{5,1},{6,2},{7,3},{8,12},{9,13},{10,... | collective-permute-start | bytes 393224 | tf_op jit(solution)/shard_map/ppermute | solution.py:242
  20.7 12.9 %collective-permute-start.3 = (bf16[64,1024]{1,0:T(8,128)(2,1)S(1)}, bf16[64,1024]{1,0:T(8,128)(2,1)S(1)}, u32[]{:S(2)}, u32[]{:S(2)}) collective-permute-start(bf16[64,1024]{1,0:T(8,128)(2,1)S(1)} %get-tuple-element.81.refs_0_), channel_id=1, source_target_pairs={{0,8},{1,9},{2,10},{3,11},{4,12},{5,13},{6,14},{7,15},{8,0},{9,1},... | collective-permute-start | bytes 393224 | tf_op jit(solution)/shard_map/ppermute | solution.py:242
  23.0 10.6 %collective-permute-start.4 = (bf16[64,1024]{1,0:T(8,128)(2,1)S(1)}, bf16[64,1024]{1,0:T(8,128)(2,1)S(1)}, u32[]{:S(2)}, u32[]{:S(2)}) collective-permute-start(bf16[64,1024]{1,0:T(8,128)(2,1)S(1)} %get-tuple-element.81.refs_0_), channel_id=1, source_target_pairs={{0,12},{1,13},{2,14},{3,15},{4,8},{5,9},{6,10},{7,11},{8,4},{9,5},... | collective-permute-start | bytes 393224 | tf_op jit(solution)/shard_map/ppermute | solution.py:242
  34.2 5.5 %collective-permute-start.5 = (bf16[64,1024]{1,0:T(8,128)(2,1)S(1)}, bf16[64,1024]{1,0:T(8,128)(2,1)S(1)}, u32[]{:S(2)}, u32[]{:S(2)}) collective-permute-start(bf16[64,1024]{1,0:T(8,128)(2,1)S(1)} %get-tuple-element.90.refs_0_), channel_id=1, source_target_pairs={{0,2},{1,3},{2,0},{3,1},{4,6},{5,7},{6,4},{7,5},{8,10},{9,11},{10,... | collective-permute-start | bytes 393224 | tf_op jit(solution)/shard_map/ppermute | solution.py:242
  36.1 12.0 %collective-permute-start.14 = (bf16[3,128,512]{2,1,0:T(8,128)(2,1)S(1)}, bf16[3,128,512]{2,1,0:T(8,128)(2,1)S(1)}, u32[]{:S(2)}, u32[]{:S(2)}) collective-permute-start(bf16[3,128,512]{2,1,0:T(8,128)(2,1)S(1)} %get-tuple-element.98), channel_id=1, source_target_pairs={{0,16},{16,0},{1,17},{17,1},{2,18},{18,2},{3,19},{19,3},{4,20},{20... | collective-permute-start | bytes 1179656 | tf_op jit(solution)/shard_map/ppermute | solution.py:238
  39.7 10.1 %collective-permute-start.12 = (bf16[128,768]{1,0:T(8,128)(2,1)S(1)}, bf16[128,768]{1,0:T(8,128)(2,1)S(1)}, u32[]{:S(2)}, u32[]{:S(2)}) collective-permute-start(bf16[128,768]{1,0:T(8,128)(2,1)S(1)} %get-tuple-element.91.refs_0_), channel_id=1, source_target_pairs={{0,2},{1,3},{2,0},{3,1},{4,6},{5,7},{6,4},{7,5},{8,10},{9,11},{10,... | collective-permute-start | bytes 589832 | tf_op jit(solution)/shard_map/ppermute | solution.py:242
  40.5 10.7 %collective-permute-start.13 = (bf16[128,768]{1,0:T(8,128)(2,1)S(1)}, bf16[128,768]{1,0:T(8,128)(2,1)S(1)}, u32[]{:S(2)}, u32[]{:S(2)}) collective-permute-start(bf16[128,768]{1,0:T(8,128)(2,1)S(1)} %get-tuple-element.92.refs_1_), channel_id=1, source_target_pairs={{0,2},{1,3},{2,0},{3,1},{4,6},{5,7},{6,4},{7,5},{8,10},{9,11},{10,... | collective-permute-start | bytes 589832 | tf_op jit(solution)/shard_map/ppermute | solution.py:242
  43.1 8.6 %collective-permute-start.10 = (bf16[64,768]{1,0:T(8,128)(2,1)S(1)}, bf16[64,768]{1,0:T(8,128)(2,1)S(1)}, u32[]{:S(2)}, u32[]{:S(2)}) collective-permute-start(bf16[64,768]{1,0:T(8,128)(2,1)S(1)} %get-tuple-element.96.sent_ref), channel_id=1, source_target_pairs={{0,16},{16,0},{1,17},{17,1},{2,18},{18,2},{3,19},{19,3},{4,20},{20... | collective-permute-start | bytes 294920 | tf_op jit(solution)/shard_map/ppermute | solution.py:238
  44.6 7.7 %collective-permute-start.11 = (bf16[64,768]{1,0:T(8,128)(2,1)S(1)}, bf16[64,768]{1,0:T(8,128)(2,1)S(1)}, u32[]{:S(2)}, u32[]{:S(2)}) collective-permute-start(bf16[64,768]{1,0:T(8,128)(2,1)S(1)} %get-tuple-element.97), channel_id=1, source_target_pairs={{0,16},{16,0},{1,17},{17,1},{2,18},{18,2},{3,19},{19,3},{4,20},{20... | collective-permute-start | bytes 294920 | tf_op jit(solution)/shard_map/ppermute | solution.py:238
  48.3 7.8 %collective-permute-start.15 = (bf16[3,128,256]{2,1,0:T(8,128)(2,1)S(1)}, bf16[3,128,256]{2,1,0:T(8,128)(2,1)S(1)}, u32[]{:S(2)}, u32[]{:S(2)}) collective-permute-start(bf16[3,128,256]{2,1,0:T(8,128)(2,1)S(1)} %shard_map.146.refs_0_), channel_id=1, source_target_pairs={{0,16},{16,0},{1,17},{17,1},{2,18},{18,2},{3,19},{19,3},{4,20},{20... | collective-permute-start | bytes 589832 | tf_op jit(solution)/shard_map/ppermute | solution.py:238
  53.5 7.6 %collective-permute-start.16 = (bf16[3,32,1024]{2,1,0:T(8,128)(2,1)S(1)}, bf16[3,32,1024]{2,1,0:T(8,128)(2,1)S(1)}, u32[]{:S(2)}, u32[]{:S(2)}) collective-permute-start(bf16[3,32,1024]{2,1,0:T(8,128)(2,1)S(1)} %get-tuple-element.109), channel_id=1, source_target_pairs={{0,16},{16,0},{1,17},{17,1},{2,18},{18,2},{3,19},{19,3},{4,20},{20... | collective-permute-start | bytes 589832 | tf_op jit(solution)/shard_map/ppermute | solution.py:238
  57.1 12.1 %collective-permute-start.24 = (bf16[3,128,512]{2,1,0:T(8,128)(2,1)S(1)}, bf16[3,128,512]{2,1,0:T(8,128)(2,1)S(1)}, u32[]{:S(2)}, u32[]{:S(2)}) collective-permute-start(bf16[3,128,512]{2,1,0:T(8,128)(2,1)S(1)} %get-tuple-element.114), channel_id=1, source_target_pairs={{0,16},{16,0},{1,17},{17,1},{2,18},{18,2},{3,19},{19,3},{4,20},{20... | collective-permute-start | bytes 1179656 | tf_op jit(solution)/shard_map/ppermute | solution.py:238
  64.3 7.6 %collective-permute-start.21 = (bf16[64,768]{1,0:T(8,128)(2,1)S(1)}, bf16[64,768]{1,0:T(8,128)(2,1)S(1)}, u32[]{:S(2)}, u32[]{:S(2)}) collective-permute-start(bf16[64,768]{1,0:T(8,128)(2,1)S(1)} %get-tuple-element.122), channel_id=1, source_target_pairs={{0,12},{1,13},{2,14},{3,15},{4,8},{5,9},{6,10},{7,11},{8,4},{9,5},... | collective-permute-start | bytes 294920 | tf_op jit(solution)/shard_map/ppermute | solution.py:242
  66.4 11.0 %collective-permute-start.22 = (bf16[64,768]{1,0:T(8,128)(2,1)S(1)}, bf16[64,768]{1,0:T(8,128)(2,1)S(1)}, u32[]{:S(2)}, u32[]{:S(2)}) collective-permute-start(bf16[64,768]{1,0:T(8,128)(2,1)S(1)} %get-tuple-element.123), channel_id=1, source_target_pairs={{0,8},{1,9},{2,10},{3,11},{4,12},{5,13},{6,14},{7,15},{8,0},{9,1},... | collective-permute-start | bytes 294920 | tf_op jit(solution)/shard_map/ppermute | solution.py:242
  68.4 8.9 %collective-permute-start.23 = (bf16[64,768]{1,0:T(8,128)(2,1)S(1)}, bf16[64,768]{1,0:T(8,128)(2,1)S(1)}, u32[]{:S(2)}, u32[]{:S(2)}) collective-permute-start(bf16[64,768]{1,0:T(8,128)(2,1)S(1)} %get-tuple-element.124), channel_id=1, source_target_pairs={{0,4},{1,5},{2,6},{3,7},{4,0},{5,1},{6,2},{7,3},{8,12},{9,13},{10,... | collective-permute-start | bytes 294920 | tf_op jit(solution)/shard_map/ppermute | solution.py:242
  69.4 8.2 %collective-permute-start.25 = (bf16[3,64,256]{2,1,0:T(8,128)(2,1)S(1)}, bf16[3,64,256]{2,1,0:T(8,128)(2,1)S(1)}, u32[]{:S(2)}, u32[]{:S(2)}) collective-permute-start(bf16[3,64,256]{2,1,0:T(8,128)(2,1)S(1)} %get-tuple-element.127.refs_0_), channel_id=1, source_target_pairs={{0,16},{16,0},{1,17},{17,1},{2,18},{18,2},{3,19},{19,3},{4,20},{20... | collective-permute-start | bytes 294920 | tf_op jit(solution)/shard_map/ppermute | solution.py:238
  71.0 6.6 %collective-permute-start.26 = (bf16[3,64,256]{2,1,0:T(8,128)(2,1)S(1)}, bf16[3,64,256]{2,1,0:T(8,128)(2,1)S(1)}, u32[]{:S(2)}, u32[]{:S(2)}) collective-permute-start(bf16[3,64,256]{2,1,0:T(8,128)(2,1)S(1)} %get-tuple-element.128.refs_1_), channel_id=1, source_target_pairs={{0,16},{16,0},{1,17},{17,1},{2,18},{18,2},{3,19},{19,3},{4,20},{20... | collective-permute-start | bytes 294920 | tf_op jit(solution)/shard_map/ppermute | solution.py:238
  80.3 6.8 %collective-permute-start.29 = (bf16[64,768]{1,0:T(8,128)(2,1)S(1)}, bf16[64,768]{1,0:T(8,128)(2,1)S(1)}, u32[]{:S(2)}, u32[]{:S(2)}) collective-permute-start(bf16[64,768]{1,0:T(8,128)(2,1)S(1)} %get-tuple-element.137), channel_id=1, source_target_pairs={{0,2},{1,3},{2,0},{3,1},{4,6},{5,7},{6,4},{7,5},{8,10},{9,11},{10,... | collective-permute-start | bytes 294920 | tf_op jit(solution)/shard_map/ppermute | solution.py:242
  81.2 8.5 %collective-permute-start.30 = (bf16[64,768]{1,0:T(8,128)(2,1)S(1)}, bf16[64,768]{1,0:T(8,128)(2,1)S(1)}, u32[]{:S(2)}, u32[]{:S(2)}) collective-permute-start(bf16[64,768]{1,0:T(8,128)(2,1)S(1)} %get-tuple-element.138), channel_id=1, source_target_pairs={{0,14},{1,15},{2,12},{3,13},{4,10},{5,11},{6,8},{7,9},{8,6},{9,7},... | collective-permute-start | bytes 294920 | tf_op jit(solution)/shard_map/ppermute | solution.py:242
  83.5 9.3 %collective-permute-start.31 = (bf16[64,768]{1,0:T(8,128)(2,1)S(1)}, bf16[64,768]{1,0:T(8,128)(2,1)S(1)}, u32[]{:S(2)}, u32[]{:S(2)}) collective-permute-start(bf16[64,768]{1,0:T(8,128)(2,1)S(1)} %get-tuple-element.139), channel_id=1, source_target_pairs={{0,10},{1,11},{2,8},{3,9},{4,14},{5,15},{6,12},{7,13},{8,2},{9,3},... | collective-permute-start | bytes 294920 | tf_op jit(solution)/shard_map/ppermute | solution.py:242
  83.8 9.0 %collective-permute-start.32 = (bf16[64,768]{1,0:T(8,128)(2,1)S(1)}, bf16[64,768]{1,0:T(8,128)(2,1)S(1)}, u32[]{:S(2)}, u32[]{:S(2)}) collective-permute-start(bf16[64,768]{1,0:T(8,128)(2,1)S(1)} %get-tuple-element.140), channel_id=1, source_target_pairs={{0,6},{1,7},{2,4},{3,5},{4,2},{5,3},{6,0},{7,1},{8,14},{9,15},{10,... | collective-permute-start | bytes 294920 | tf_op jit(solution)/shard_map/ppermute | solution.py:242
  (22 other events, 132.5 us)
